TPU v7x, 512 devices: a whole 4x4x16 slice. The times are simulated.
512 devices in a mesh: dp: 32 (over z, core), expert: 16 (over y, x).
Axes of the slice: x: 4, y: 4, z: 16, core: 2. Of those that a mesh axis runs over, the one named last changes fastest.
Arguments:
- attn_input: bfloat16 [65536, 3072], P(('dp', 'expert')), may hold values from -24 to 24
- key_cot: bfloat16 [65536, 512], P(('dp', 'expert')), may hold values from -6 to 6
- routing: int32 [65536, 4], P(('dp', 'expert')), may hold values from 0 to 15, all different within a row; in each aligned block of 128 rows (0 to 127, 128 to 255, ...) at most 34 rows name the same one
- router_base: float32 [65536, 16], P(('dp', 'expert')), may hold values from -1.5 to 1.5
- router_weight: bfloat16 [3072, 16], replicated, may hold values from -1.5 to 1.5
- expert_rows: bfloat16 [8192, 34, 3072], P(('dp', 'expert')), may hold values from -6 to 6
- expert_dots: bfloat16 [8192, 34], P(('dp', 'expert')), may hold values from -16 to 16
- key_weight: float32 [3072, 512], P(('dp', 'expert')), may hold values from -0.25 to 0.25
- first_moment: float32 [3072, 512], P(('dp', 'expert')), may hold values from -1536 to 1536
- second_moment: float32 [3072, 512], P(('dp', 'expert')), may hold values from 13107.2 to 327680
Outputs:
- input_grad: bfloat16 [65536, 3072], P(('dp', 'expert'))
- new_key_weight: float32 [3072, 512], P(('dp', 'expert'))
- new_first_moment: float32 [3072, 512], P(('dp', 'expert'))
- new_second_moment: float32 [3072, 512], P(('dp', 'expert'))
Inputs may be any that keep to these rules, and one draw needn't show every extreme that they name: `routing`: each token names 4 different experts. The 128 tokens of one device name any one expert at most 34 times, and that bound is reached.
All inputs are finite; a program needn't handle non-finite values.
Results may differ from a plain program's by a relative error of at most 0.0043.
Values may be sent and summed in bfloat16 or wider, within the bound.
No kernel may reach another device: no remote copies, remote signals or barrier semaphores. Data moves between devices by JAX's collectives and lax.ppermute only.
A program may use at most 64 MiB of HBM per device.

v0:
```python
import jax
import jax.numpy as jnp
from jax import lax
from jax.sharding import PartitionSpec as P

ADAM_STEP = 10


beta_one = 0.9
beta_two = 0.95
epsilon = 1e-08
learn_rate = 0.005
decay_rate = 0.1
routed_offset = 3.5


def route_slots(routing, experts, capacity):
    choose = (routing[:, :, None] == jnp.arange(experts, dtype=jnp.int32)[None, None, :]).astype(
        jnp.int32
    )
    per_expert = jnp.sum(choose, axis=1)
    before = jnp.cumsum(per_expert, axis=0) - per_expert
    slots = jnp.sum(choose * before[:, None, :], axis=2)
    return (choose, routing * capacity + slots)


def combine(routing, router_base, returned, returned_dots, router_weight):
    experts, capacity, features = returned.shape
    choose, flat_index = route_slots(routing, experts, capacity)
    routed_mask = jnp.sum(choose, axis=1).astype(jnp.float32)
    router_probs = jax.nn.softmax(router_base + routed_offset * routed_mask, axis=-1)
    picked = jnp.take(returned.reshape(experts * capacity, features), flat_index, axis=0)
    inner = jnp.take(returned_dots.reshape(experts * capacity), flat_index, axis=0).astype(
        jnp.float32
    )
    chosen = jnp.take_along_axis(router_probs, routing, axis=1)
    chosen_sum = jnp.sum(chosen, axis=1, keepdims=True)
    gate_share = chosen / chosen_sum
    mixed = gate_share[:, 0:1] * picked[:, 0].astype(jnp.float32)
    for position in range(1, routing.shape[1]):
        mixed = mixed + gate_share[:, position : position + 1] * picked[:, position].astype(
            jnp.float32
        )
    mean_inner = jnp.sum(gate_share * inner, axis=1, keepdims=True)
    d_chosen = (inner - mean_inner) / chosen_sum
    d_probs = jnp.sum(choose.astype(jnp.float32) * d_chosen[:, :, None], axis=1)
    d_logits = router_probs * (d_probs - jnp.sum(router_probs * d_probs, axis=1, keepdims=True))
    router_term = jnp.dot(
        d_logits, router_weight.astype(jnp.float32).T, precision=lax.Precision.HIGHEST
    )
    return mixed + router_term


def adamw(weight, first, second, grad):
    new_first = beta_one * first + (1.0 - beta_one) * grad
    new_second = beta_two * second + (1.0 - beta_two) * grad * grad
    first_hat = new_first / (1.0 - beta_one**ADAM_STEP)
    second_hat = new_second / (1.0 - beta_two**ADAM_STEP)
    new_weight = weight - learn_rate * (
        first_hat / (jnp.sqrt(second_hat) + epsilon) + decay_rate * weight
    )
    return (new_weight, new_first, new_second)


def local(
    attn_input,
    key_cot,
    routing,
    router_base,
    router_weight,
    expert_rows,
    expert_dots,
    key_weight,
    first_moment,
    second_moment,
):
    returned, returned_dots = (
        lax.all_to_all(expert_rows, "expert", split_axis=0, concat_axis=0, tiled=True),
        lax.all_to_all(expert_dots, "expert", split_axis=0, concat_axis=0, tiled=True),
    )
    moe_term = combine(routing, router_base, returned, returned_dots, router_weight)
    key_term = lax.dot_general(
        key_cot,
        lax.all_gather(key_weight.astype(jnp.bfloat16), ("dp", "expert"), axis=0, tiled=True),
        (((1,), (1,)), ((), ())),
        preferred_element_type=jnp.float32,
    )
    input_grad = (moe_term + key_term).astype(jnp.bfloat16)
    partial_grad = lax.dot_general(
        attn_input, key_cot, (((0,), (0,)), ((), ())), preferred_element_type=jnp.float32
    )
    cycle_size = lax.axis_size("dp")
    group_size = lax.axis_size("expert")
    shard_rows = key_weight.shape[0]
    stacked = partial_grad.reshape(cycle_size, group_size * shard_rows, partial_grad.shape[1])
    halfway = lax.psum_scatter(stacked.astype(jnp.bfloat16), "dp", scatter_dimension=0, tiled=True)
    summed = lax.psum_scatter(halfway, "expert", scatter_dimension=1, tiled=True).astype(
        jnp.float32
    )
    key_grad = summed.reshape(shard_rows, partial_grad.shape[1])
    new_key_weight, new_first_moment, new_second_moment = adamw(
        key_weight, first_moment, second_moment, key_grad
    )
    return (input_grad, new_key_weight, new_first_moment, new_second_moment)


def solution(mesh):
    in_specs = (
        P(("dp", "expert"), None),
        P(("dp", "expert"), None),
        P(("dp", "expert"), None),
        P(("dp", "expert"), None),
        P(),
        P(("dp", "expert"), None, None),
        P(("dp", "expert"), None),
        P(("dp", "expert"), None),
        P(("dp", "expert"), None),
        P(("dp", "expert"), None),
    )
    out_specs = (
        P(("dp", "expert"), None),
        P(("dp", "expert"), None),
        P(("dp", "expert"), None),
        P(("dp", "expert"), None),
    )
    return jax.shard_map(local, mesh=mesh, in_specs=in_specs, out_specs=out_specs, check_vma=False)
```

profile of v0, /device:TPU:24, one launch (start us, length us, event | category | flops | bytes accessed | tf_op | source)
XLA Modules:
  0.0 478.5 jit_solution(3654150529224520053)
XLA Ops:
  7.2 0.0 copy-start
  7.2 0.0 copy-start.4
  7.2 0.0 copy-start.5
  7.2 0.0 copy-start.6
  7.2 0.0 copy-start.7
  7.2 0.0 reduce-scatter.3.cloned.1.call-start
  7.3 1.0 copy-done
  8.3 3.6 convolution_convert_fusion
  11.9 0.0 reduce-scatter.3.cloned.1.call-update
  11.9 0.0 all-reduce.3.cloned.1.call-start
  12.0 115.8 %reduce-scatter.3.cloned.1.call-done = bf16[1,96,512]{2,1,0:T(8,128)(2,1)} async-done(((bf16[32,96,512]{2,1,0:T(8,128)(2,1)}), bf16[1,96,512]{2,1,0:T(8,128)(2,1)}) %reduce-scatter.3.cloned.1.call-update) | async-done | bytes 98320 | tf_op jit(solution)/shard_map/reduce_scatter | solution.py:96
  127.8 0.0 all-reduce.3.cloned.1.call-update
  127.8 0.0 all-gather.3.cloned.1.call-start
  127.9 1.3 dynamic-slice
  129.8 110.7 %all-reduce.3.cloned.1.call-done = bf16[1,96,512]{2,1,0:T(8,128)(2,1)} async-done(((bf16[1,96,512]{2,1,0:T(8,128)(2,1)}), bf16[1,96,512]{2,1,0:T(8,128)(2,1)}) %all-reduce.3.cloned.1.call-update) | async-done | bytes 98320
  240.5 0.0 copy-done.4
  240.5 0.0 copy-done.5
  240.5 1.4 multiply_subtract_fusion
  241.9 0.0 all-gather.3.cloned.1.call-update
  241.9 0.6 copy.122
  242.5 6.3 %all-to-all-start.1 = ((bf16[16,1,34]{2,1,0:T(2,128)(2,1)}), bf16[16,1,34]{2,1,0:T(2,128)(2,1)S(1)}, u32[]{:S(2)}, u32[]{:S(2)}) async-start(bf16[16,1,34]{2,1,0:T(2,128)(2,1)} %copy.122), calls=%async_computation.1 | async-start | bytes 16384 | tf_op jit(solution)/shard_map/all_to_all | solution.py:79
  248.9 5.8 %copy.119 = bf16[16,34,3072]{2,1,0:T(8,128)(2,1)} copy(bf16[16,34,3072]{2,0,1:T(8,128)(2,1)} %param.15) | data formatting | bytes 6684672 | tf_op args[5]
  254.7 0.0 all-to-all-done.1
  254.7 7.4 %all-to-all-start = ((bf16[16,34,3072]{2,1,0:T(8,128)(2,1)}), bf16[16,34,3072]{2,1,0:T(8,128)(2,1)}, u32[]{:S(2)}, u32[]{:S(2)}) async-start(bf16[16,34,3072]{2,1,0:T(8,128)(2,1)} %copy.119), calls=%async_computation | async-start | bytes 7864320 | tf_op jit(solution)/shard_map/all_to_all | solution.py:78
  262.1 0.1 copy.116
  262.2 0.2 reduce_window_sum.11
  262.3 0.1 copy.118
  262.5 0.1 copy.120
  262.6 0.1 reshape.92
  262.7 0.1 copy.114
  262.8 0.1 reshape.106
  262.9 0.0 copy-done.3
  263.0 3.7 gather_fusion.2
  266.7 0.1 reshape.109
  266.9 0.1 copy.115
  267.0 0.1 reshape.81
  267.1 3.5 gather_fusion.1
  270.6 0.1 reshape.99
  270.7 0.1 copy.123
  270.9 42.6 %all-to-all-done = bf16[16,34,3072]{2,1,0:T(8,128)(2,1)} async-done(((bf16[16,34,3072]{2,1,0:T(8,128)(2,1)}), bf16[16,34,3072]{2,1,0:T(8,128)(2,1)}, u32[]{:S(2)}, u32[]{:S(2)}) %all-to-all-start) | async-done | bytes 3342368 | tf_op jit(solution)/shard_map/all_to_all | solution.py:78
  313.5 4.8 %reshape.80 = bf16[544,3072]{1,0:T(8,128)(2,1)} reshape(bf16[16,34,3072]{2,1,0:T(8,128)(2,1)} %all-to-all-done) | data formatting | bytes 6684672 | tf_op jit(solution)/shard_map/reshape | solution.py:32
  318.3 9.5 %gather_fusion = bf16[512,3072]{1,0:T(8,128)(2,1)} fusion(bf16[544,3072]{1,0:T(8,128)(2,1)} %reshape.80, s32[1024]{0:T(1024)S(1)} %pad_clamp_fusion), kind=kCustom, calls=%fused_computation | custom fusion | bytes 6293504 | tf_op jit(solution)/shard_map/jit(_take)/gather | solution.py:32
  327.8 6.1 %reshape.91 = bf16[128,4,3072]{2,1,0:T(4,128)(2,1)} reshape(bf16[512,3072]{1,0:T(8,128)(2,1)} %gather_fusion) | data formatting | bytes 6291456 | tf_op jit(solution)/shard_map/jit(_take)/gather | solution.py:32
  333.9 5.6 %copy_select_fusion = bf16[128,4,3072]{2,0,1:T(8,128)(2,1)} fusion(bf16[128,4,3072]{2,1,0:T(4,128)(2,1)} %reshape.91, pred[128,4]{0,1:T(4,128)(4,1)S(1)} %get-tuple-element.9), kind=kLoop, calls=%fused_computation.7 | loop fusion | flops 1572864 | bytes 6291968 | tf_op jit(solution)/shard_map/jit(_take)/select_n | solution.py:32
  339.5 118.8 %all-gather.3.cloned.1.call-done = bf16[512,6,512]{2,1,0:T(8,128)(2,1)} async-done(((bf16[1,6,512]{2,1,0:T(8,128)(2,1)}), bf16[512,6,512]{2,1,0:T(8,128)(2,1)}) %all-gather.3.cloned.1.call-update) | async-done | bytes 3145744 | tf_op jit(solution)/shard_map/all_gather | solution.py:84
  458.3 6.4 %reshape.122 = bf16[3072,512]{1,0:T(8,128)(2,1)} reshape(bf16[512,6,512]{2,1,0:T(8,128)(2,1)} %all-gather.3.cloned.1.call-done) | data formatting | bytes 6291456
  464.7 3.1 fusion.20
  467.8 4.2 fusion.1
  (25 shorter events, 0.3 us)
Async XLA Ops:
  7.2 1.1 copy-start
  7.2 233.3 %copy-start.4 = (f32[6,512]{1,0:T(8,128)S(1)}, f32[6,512]{1,0:T(8,128)}, u32[]{:S(2)}) copy-start(f32[6,512]{1,0:T(8,128)} %param.17) | copy-start | bytes 36868
  7.2 233.3 %copy-start.5 = (f32[6,512]{1,0:T(8,128)S(1)}, f32[6,512]{1,0:T(8,128)}, u32[]{:S(2)}) copy-start(f32[6,512]{1,0:T(8,128)} %param.18) | copy-start | bytes 36868
  7.2 233.3 %copy-start.6 = (f32[6,512]{1,0:T(8,128)S(1)}, f32[6,512]{1,0:T(8,128)}, u32[]{:S(2)}) copy-start(f32[6,512]{1,0:T(8,128)} %param.19) | copy-start | bytes 36868
  7.2 234.7 %copy-start.7 = (bf16[16,34]{1,0:T(8,128)(2,1)S(1)}, bf16[16,34]{1,0:T(8,128)(2,1)}, u32[]{:S(2)}) copy-start(bf16[16,34]{1,0:T(8,128)(2,1)} %param.16) | copy-start | bytes 3268
  7.2 120.6 %reduce-scatter.3.cloned.1.call-start = ((), (), s32[]{:S(2)}) async-start(), calls=%async_computation.3 | async-start | bytes 3244032 | tf_op jit(solution)/shard_map/reduce_scatter | solution.py:96
  11.9 228.6 %all-reduce.3.cloned.1.call-start = ((), (), s32[]{:S(2)}) async-start(), calls=%async_computation.5 | async-start | bytes 196608
  127.8 330.5 %all-gather.3.cloned.1.call-start = ((), (), s32[]{:S(2)}) async-start(), calls=%async_computation.4 | async-start | bytes 4202496 | tf_op jit(solution)/shard_map/all_gather | solution.py:84
  242.5 12.2 %all-to-all-start.1 = ((bf16[16,1,34]{2,1,0:T(2,128)(2,1)}), bf16[16,1,34]{2,1,0:T(2,128)(2,1)S(1)}, u32[]{:S(2)}, u32[]{:S(2)}) async-start(bf16[16,1,34]{2,1,0:T(2,128)(2,1)} %copy.122), calls=%async_computation.1 | async-start | bytes 16384 | tf_op jit(solution)/shard_map/all_to_all | solution.py:79
  254.7 7.4 %copy-start.2 = (s32[128,4]{0,1:T(4,128)S(1)}, s32[128,4]{0,1:T(4,128)}, u32[]{:S(2)}) copy-start(s32[128,4]{0,1:T(4,128)} %param.12) | copy-start | bytes 6148
  254.7 8.2 %copy-start.3 = (f32[128,16]{0,1:T(8,128)S(1)}, f32[128,16]{0,1:T(8,128)}, u32[]{:S(2)}) copy-start(f32[128,16]{0,1:T(8,128)} %param.13) | copy-start | bytes 24580
  254.7 58.8 %all-to-all-start = ((bf16[16,34,3072]{2,1,0:T(8,128)(2,1)}), bf16[16,34,3072]{2,1,0:T(8,128)(2,1)}, u32[]{:S(2)}, u32[]{:S(2)}) async-start(bf16[16,34,3072]{2,1,0:T(8,128)(2,1)} %copy.119), calls=%async_computation | async-start | bytes 7864320 | tf_op jit(solution)/shard_map/all_to_all | solution.py:78
  339.5 125.2 %copy-start.1 = (bf16[128,512]{1,0:T(8,128)(2,1)S(1)}, bf16[128,512]{1,0:T(8,128)(2,1)}, u32[]{:S(2)}) copy-start(bf16[128,512]{1,0:T(8,128)(2,1)} %param.11) | copy-start | bytes 393220
  464.7 3.1 copy-start.8
Sparse Core Ops, SparseCore 0:
  12.0 115.7 reduce-scatter.2
  131.3 109.1 all-reduce.2
  245.5 212.7 all-gather.2
where the time goes:
time: 481 us; the launch traced here: 479 us
  waiting for transfers between devices  388 us (81%)
  local copies, waits for them, and re-layouts  43.9 us (9%)
  between operations  14.6 us (3%)
  starting transfers between devices  13.8 us (3%)
  matrix products  10.8 us (2%)
  other arithmetic  7.42 us (2%)
    all_gather x1, waiting for transfers between devices, local(): lax.all_gather(key_weight.astype(jnp.bfloat16), ('dp', 'expert'), axis=0,...  119 us
    reduce_scatter x1, waiting for transfers between devices, local(): lax.psum_scatter(stacked.astype(jnp.bfloat16), 'dp', scatter_dimension=0,...  116 us
    unnamed x4, waiting for transfers between devices  111 us
    all_to_all x1, waiting for transfers between devices, local(): lax.all_to_all(expert_rows, 'expert', split_axis=0, concat_axis=0, tiled=...  42.6 us
    gather x2, local copies, waits for them, and re-layouts, combine(): jnp.take(returned.reshape(experts * capacity, features), flat_index, axis=0)  15.6 us
    unnamed x21, local copies, waits for them, and re-layouts  14.5 us
  transfers between devices with their start and end apart: 5, of which 4 were waited for; matrix products, arithmetic and copies ran while one was open for 9% of the time, Pallas kernels for 0%

commit v1 on v0

v1 whole, which is shorter than its diff:
```python
import jax
import jax.numpy as jnp
from jax import lax
from jax.experimental import pallas as pl
from jax.experimental.pallas import tpu as pltpu
from jax.sharding import PartitionSpec as P

ADAM_STEP = 10

beta_one = 0.9
beta_two = 0.95
epsilon = 1e-08
learn_rate = 0.005
decay_rate = 0.1
routed_offset = 3.5

BF = jnp.bfloat16
F32 = jnp.float32

TOK, D, KC = 128, 3072, 512
EXP, CAP = 16, 34
HEAD = 32
REST = CAP - HEAD
PARTS = 8
COLS = D // PARTS
CHUNK = PARTS * CAP
ZN, CORES, SUB = 16, 2, 6
DPROWS = EXP * SUB

VM = pltpu.VMEM
HB = pl.ANY


def iota(shape, dim):
    return lax.broadcasted_iota(jnp.int32, shape, dim)


def dot(a, b, ca=1, cb=0):
    return lax.dot_general(a, b, (((ca,), (cb,)), ((), ())), preferred_element_type=F32)


def params(mib):
    return pltpu.CompilerParams(vmem_limit_bytes=mib * 1024 * 1024)


def cost(flops, moved):
    return pl.CostEstimate(flops=flops, bytes_accessed=moved, transcendentals=0)


def full(*shape):
    return pl.BlockSpec(shape, lambda *_: (0,) * len(shape))


def pack_kernel(rows_ref, out_ref, rows_in, head_out, rest_out, in_sem, out_sem):
    def fetch(q):
        return pltpu.make_async_copy(
            rows_ref.at[:, :, pl.ds(q * COLS, COLS)], rows_in.at[q], in_sem.at[q]
        )

    def put(q):
        return pltpu.make_async_copy(
            head_out.at[q], out_ref.at[:, pl.ds(q * HEAD, HEAD), :], out_sem.at[q]
        )

    for q in range(PARTS):
        fetch(q).start()
    heads, rests = EXP * HEAD, EXP * REST * PARTS
    to, fr = iota((heads, heads), 0), iota((heads, heads), 1)
    move = jnp.where((to % HEAD) * EXP + to // HEAD == fr, 1.0, 0.0).astype(BF)
    to, fr = iota((rests, rests), 0), iota((rests, rests), 1)
    per = REST * PARTS
    place = (to % per) * EXP + to // per
    move_rest = jnp.where(place == fr, 1.0, 0.0).astype(BF)
    rest = []
    for q in range(PARTS):
        fetch(q).wait()
        block = rows_in[q].reshape(CAP * EXP, COLS)
        head = dot(move, block[: HEAD * EXP])
        head_out[q] = head.astype(BF).reshape(EXP, HEAD, COLS)
        put(q).start()
        rest.append(block[HEAD * EXP :])
    rest = dot(move_rest, jnp.concatenate(rest, axis=0))
    rest_out[...] = rest.astype(BF).reshape(EXP, per, COLS)
    last = pltpu.make_async_copy(
        rest_out, out_ref.at[:, pl.ds(PARTS * HEAD, per), :], out_sem.at[PARTS]
    )
    last.start()
    for q in range(PARTS):
        put(q).wait()
    last.wait()


def pack(rows):
    return pl.pallas_call(
        pack_kernel,
        out_shape=jax.ShapeDtypeStruct((EXP, CHUNK, COLS), BF),
        in_specs=[pl.BlockSpec(memory_space=HB)],
        out_specs=pl.BlockSpec(memory_space=HB),
        scratch_shapes=[
            VM((PARTS, CAP, EXP, COLS), BF),
            VM((PARTS, EXP, HEAD, COLS), BF),
            VM((EXP, REST * PARTS, COLS), BF),
            pltpu.SemaphoreType.DMA((PARTS,)),
            pltpu.SemaphoreType.DMA((PARTS + 1,)),
        ],
        compiler_params=params(32),
        cost_estimate=cost(2 * 512 * 512 * D, 2 * EXP * CAP * D * 2),
        name="pack_rows",
    )(rows)


def split2(x):
    hi = x.astype(BF)
    return hi, (x - hi.astype(F32)).astype(BF)


def gate_kernel(routing_ref, base_ref, dots_ref, pick_ref, rest_ref, logit_ref):
    experts = iota((EXP, TOK), 0)
    mask = jnp.zeros((EXP, TOK), F32)
    for k in range(4):
        mask = mask + jnp.where(routing_ref[k : k + 1, :] == experts, 1.0, 0.0)
    logits = base_ref[...] + routed_offset * mask
    raised = jnp.exp(logits - jnp.max(logits, axis=0, keepdims=True))
    probs = raised / jnp.sum(raised, axis=0, keepdims=True)
    chosen = probs * mask
    chosen_sum = jnp.sum(chosen, axis=0, keepdims=True)
    gate = chosen / chosen_sum
    earlier = jnp.where(iota((TOK, TOK), 0) < iota((TOK, TOK), 1), 1.0, 0.0).astype(BF)
    before = dot(mask.astype(BF), earlier)
    slot = jnp.where(mask > 0, before, -1.0)

    def spread(rows, per):
        grown = jnp.where(iota((rows, EXP), 0) // per == iota((rows, EXP), 1), 1.0, 0.0)
        return grown.astype(BF)

    heads, per = EXP * HEAD, REST * PARTS
    rests = EXP * per
    slot_b = slot.astype(BF)
    grow, grow_rest = spread(heads, HEAD), spread(rests, per)
    hit = dot(grow, slot_b) == (iota((heads, TOK), 0) % HEAD).astype(F32)
    hit_rest = dot(grow_rest, slot_b) == (iota((rests, TOK), 0) % REST + HEAD).astype(F32)
    hi, lo = split2(gate)

    def weighted(grown, hits):
        pair = [jnp.where(hits, dot(grown, part), 0.0).T for part in (hi, lo)]
        return jnp.concatenate(pair, axis=0).astype(BF)

    pick_ref[...] = weighted(grow, hit)
    rest_ref[...] = weighted(grow_rest, hit_rest)
    inner = jnp.zeros((EXP, TOK), F32)
    for r in range(CAP):
        inner = inner + jnp.where(slot == float(r), dots_ref[:, r : r + 1].astype(F32), 0.0)
    mean = jnp.sum(gate * inner, axis=0, keepdims=True)
    d_probs = mask * ((inner - mean) / chosen_sum)
    d_logits = probs * (d_probs - jnp.sum(probs * d_probs, axis=0, keepdims=True))
    one, rem = split2(d_logits)[0], d_logits
    rem = rem - one.astype(F32)
    two, three = split2(rem)
    logit_ref[...] = jnp.concatenate([one, two, three], axis=0)


def gates(routing, base, dots):
    heads, rests = EXP * HEAD, EXP * REST * PARTS
    return pl.pallas_call(
        gate_kernel,
        out_shape=(
            jax.ShapeDtypeStruct((2 * TOK, heads), BF),
            jax.ShapeDtypeStruct((2 * TOK, rests), BF),
            jax.ShapeDtypeStruct((3 * EXP, TOK), BF),
        ),
        compiler_params=params(16),
        cost_estimate=cost(10**8, 10**6),
        name="gates",
    )(routing, base, dots)


def combine_kernel(pick_ref, rest_ref, logit_ref, cot_ref, head_ref, tail_ref, w_ref, router_ref, out_ref):
    q = pl.program_id(0)
    rests = EXP * REST * PARTS
    piece = (iota((2 * TOK, rests), 1) % (REST * PARTS)) // REST
    rest = jnp.where(piece == q, rest_ref[...].astype(F32), 0.0).astype(BF)
    mixed = dot(pick_ref[...], head_ref[...].reshape(EXP * HEAD, COLS))
    mixed = mixed + dot(rest, tail_ref[...].reshape(rests, COLS))
    total = mixed[:TOK] + mixed[TOK:]
    router = router_ref[...]
    total = total + dot(logit_ref[...], jnp.concatenate([router] * 3, axis=0), 0, 0)
    total = total + dot(cot_ref[...], w_ref[...], 1, 1)
    out_ref[...] = total.astype(BF)


def combine(pick, rest, logit, cot, rows, w, router):
    heads, rests, per = EXP * HEAD, EXP * REST * PARTS, REST * PARTS
    return pl.pallas_call(
        combine_kernel,
        grid=(PARTS,),
        out_shape=jax.ShapeDtypeStruct((TOK, D), BF),
        in_specs=[
            full(2 * TOK, heads),
            full(2 * TOK, rests),
            full(3 * EXP, TOK),
            full(TOK, KC),
            pl.BlockSpec((EXP, HEAD, COLS), lambda q: (0, q, 0)),
            pl.BlockSpec((EXP, per, COLS), lambda q: (0, PARTS * HEAD // per, 0)),
            pl.BlockSpec((COLS, KC), lambda q: (q, 0)),
            pl.BlockSpec((EXP, COLS), lambda q: (0, q)),
        ],
        out_specs=pl.BlockSpec((TOK, COLS), lambda q: (0, q)),
        compiler_params=params(32),
        cost_estimate=cost(2 * 10**9, 8 * 10**6),
        name="combine",
    )(pick, rest, logit, cot, rows, rows, w, router)


def partial_kernel(core_ref, attn_ref, cot_ref, keep_ref, send_ref):
    first = core_ref[0] == 0
    grad = dot(attn_ref[...], cot_ref[...], 0, 0)
    for i in range(2):
        zero = grad[(2 * i) * DPROWS : (2 * i + 1) * DPROWS]
        one = grad[(2 * i + 1) * DPROWS : (2 * i + 2) * DPROWS]
        keep_ref[i] = jnp.where(first, zero, one).astype(BF)
        send_ref[i] = jnp.where(first, one, zero).astype(BF)


def partials(core, attn, cot):
    wide = 2 * CORES * DPROWS
    shape = jax.ShapeDtypeStruct((ZN, DPROWS, KC), BF)
    return pl.pallas_call(
        partial_kernel,
        grid_spec=pltpu.PrefetchScalarGridSpec(
            num_scalar_prefetch=1,
            grid=(ZN // 2,),
            in_specs=[
                pl.BlockSpec((TOK, wide), lambda i, c: (0, i)),
                pl.BlockSpec((TOK, KC), lambda i, c: (0, 0)),
            ],
            out_specs=[pl.BlockSpec((2, DPROWS, KC), lambda i, c: (i, 0, 0))] * 2,
        ),
        out_shape=(shape, shape),
        compiler_params=params(16),
        cost_estimate=cost(2 * TOK * D * KC, 5 * 10**6),
        name="key_partials",
    )(core, attn, cot)


HALF = DPROWS // 2


def near_kernel(place_ref, keep_ref, got_ref, own_ref, up_ref, down_ref, up2_ref, down2_ref):
    place = place_ref[0]
    for a in range(4):

        def total(rel):
            at = 4 * a + lax.rem(place + rel, 4)
            return keep_ref[at].astype(F32) + got_ref[at].astype(F32)

        own_ref[a] = total(0).astype(BF)
        up_ref[a] = total(1).astype(BF)
        down_ref[a] = total(3).astype(BF)
        far = total(2).astype(BF)
        up2_ref[a] = far[:HALF]
        down2_ref[a] = far[HALF:]


def smem():
    return pl.BlockSpec(memory_space=pltpu.SMEM)


def vmem():
    return pl.BlockSpec(memory_space=VM)


def near(place, keep, got):
    whole = jax.ShapeDtypeStruct((4, DPROWS, KC), BF)
    half = jax.ShapeDtypeStruct((4, HALF, KC), BF)
    return pl.pallas_call(
        near_kernel,
        in_specs=[smem(), vmem(), vmem()],
        out_specs=[vmem()] * 5,
        out_shape=(whole, whole, whole, half, half),
        compiler_params=params(24),
        cost_estimate=cost(10**6, 5 * 10**6),
        name="near_sums",
    )(place, keep, got)


def far_kernel(place_ref, own_ref, up_ref, down_ref, up2_ref, down2_ref, *outs):
    place = place_ref[0]
    for rel in range(4):
        at = lax.rem(place + rel, 4)
        total = own_ref[at].astype(F32) + up_ref[at].astype(F32) + down_ref[at].astype(F32)
        outs[rel][:HALF] = (total[:HALF] + up2_ref[at].astype(F32)).astype(BF)
        outs[rel][HALF:] = (total[HALF:] + down2_ref[at].astype(F32)).astype(BF)


def far(place, *given):
    return pl.pallas_call(
        far_kernel,
        in_specs=[smem()] + [vmem()] * 5,
        out_specs=[vmem()] * 4,
        out_shape=(jax.ShapeDtypeStruct((DPROWS, KC), BF),) * 4,
        compiler_params=params(16),
        cost_estimate=cost(10**6, 2 * 10**6),
        name="far_sums",
    )(place, *given)


def along_z(step):
    return [(i, ((i // CORES + step) % ZN) * CORES + i % CORES) for i in range(ZN * CORES)]


def shift(x, step):
    return lax.ppermute(x, "dp", along_z(step))


def adamw(weight, first, second, grad):
    new_first = beta_one * first + (1.0 - beta_one) * grad
    new_second = beta_two * second + (1.0 - beta_two) * grad * grad
    first_hat = new_first / (1.0 - beta_one**ADAM_STEP)
    second_hat = new_second / (1.0 - beta_two**ADAM_STEP)
    new_weight = weight - learn_rate * (
        first_hat / (jnp.sqrt(second_hat) + epsilon) + decay_rate * weight
    )
    return (new_weight, new_first, new_second)


def exchange(x):
    return lax.all_to_all(x, "expert", split_axis=0, concat_axis=0, tiled=True)


def local(
    attn_input,
    key_cot,
    routing,
    router_base,
    router_weight,
    expert_rows,
    expert_dots,
    key_weight,
    first_moment,
    second_moment,
):
    dp = lax.axis_index("dp")
    core, z = lax.rem(dp, CORES), dp // CORES
    near_place, far_place = lax.rem(z, 4)[None], (z // 4)[None]
    w = jnp.broadcast_to(key_weight.astype(BF)[None], (EXP, SUB, KC))
    inner = jnp.pad(expert_dots, ((0, 0), (0, KC - CAP)))[:, None, :]
    small = jnp.concatenate([w, inner, jnp.zeros_like(inner)], axis=1)
    small = exchange(small)
    w = small[:, :SUB].reshape(DPROWS, KC)
    dots = small[:, SUB, :CAP]
    w = lax.all_gather(w, "dp", axis=0, tiled=True)
    rows = exchange(pack(jnp.swapaxes(expert_rows, 0, 1)))
    pick, rest, logit = gates(routing.T, router_base.T, dots)
    keep, send = partials(core[None], attn_input, key_cot)
    got = lax.ppermute(send, "dp", [(i, i ^ 1) for i in range(ZN * CORES)])
    own, up, down, up2, down2 = near(near_place, keep, got)
    own, up, across, down = far(
        far_place, own, shift(up, 1), shift(down, -1), shift(up2, 2), shift(down2, -2)
    )
    up, across, down = shift(up, 4), shift(across, 8), shift(down, -4)
    summed = (
        own.astype(F32) + up.astype(F32) + across.astype(F32) + down.astype(F32)
    ).astype(BF)
    summed = exchange(summed.reshape(EXP, SUB, KC))
    key_grad = jnp.sum(summed.astype(F32), axis=0)
    updated = adamw(key_weight, first_moment, second_moment, key_grad)
    input_grad = combine(pick, rest, logit, key_cot, rows, w, router_weight.T)
    return (input_grad, *updated)


def solution(mesh):
    split = P(("dp", "expert"))
    in_specs = (split,) * 4 + (P(),) + (split,) * 5
    return jax.shard_map(
        local, mesh=mesh, in_specs=in_specs, out_specs=(split,) * 4, check_vma=False
    )
```

time: 481 us -> 205 us (0.43)
  waiting for transfers between devices: 388 us -> 83.7 us
  starting transfers between devices: 13.8 us -> 56.2 us
  local copies, waits for them, and re-layouts: 43.9 us -> 19.6 us
  Pallas kernels: 0 us -> 15.9 us
  blocking collectives: 0 us -> 11.1 us
  matrix products: 10.8 us -> 0 us
  other arithmetic: 7.42 us -> 1.55 us
    reduce_scatter x1 -> x0, waiting for transfers between devices: 116 us -> none  [local(): lax.psum_scatter(stacked.astype(jnp.bfloat16), 'dp', scatter_dimension=0,...]
    unnamed x4 -> x1, waiting for transfers between devices: 111 us -> 0.02 us
    all_gather x1, waiting for transfers between devices: 119 us -> 22.1 us  [local(): w = lax.all_gather(w, 'dp', axis=0, tiled=True)]
    ppermute x0 -> x8, starting transfers between devices: none -> 42.9 us  [the longest x7 40.9 us: shift(): return lax.ppermute(x, 'dp', along_z(step))]
    gather x10 -> x0, local copies, waits for them, and re-layouts: 23.4 us -> none  [the longest x2 15.6 us: combine(): jnp.take(returned.reshape(experts * capacity, features), flat_index, axis=0)]
    ppermute x0 -> x8, waiting for transfers between devices: none -> 17.8 us  [the longest x7 14.4 us: shift(): return lax.ppermute(x, 'dp', along_z(step))]
    pallas_call x0 -> x6, Pallas kernels: none -> 15.9 us  [the longest x1 5.44 us: combine(): pl.pallas_call(combine_kernel, grid=(PARTS,), out_shape=jax.ShapeDtypeStr...]
    all_to_all x0 -> x1, blocking collectives: none -> 11.1 us  [exchange(): return lax.all_to_all(x, 'expert', split_axis=0, concat_axis=0, tiled=True)]
  transfers between devices with their start and end apart: 5 -> 11, of which waited for: 4 -> 8; matrix products, arithmetic and copies ran while one was open for 9% -> 1% of each run, Pallas kernels for 0% -> 3%
where the time goes in v1:
time: 205 us; the launch traced here: 202 us
  waiting for transfers between devices  83.7 us (41%)
  starting transfers between devices  56.2 us (27%)
  local copies, waits for them, and re-layouts  19.6 us (10%)
  Pallas kernels  15.9 us (8%)
  between operations  14.3 us (7%)
  blocking collectives  11.1 us (5%)
    all_to_all x2, waiting for transfers between devices, exchange(): return lax.all_to_all(x, 'expert', split_axis=0, concat_axis=0, tiled=True)  43.8 us
    ppermute x7, starting transfers between devices, shift(): return lax.ppermute(x, 'dp', along_z(step))  40.9 us
    all_gather x1, waiting for transfers between devices, local(): w = lax.all_gather(w, 'dp', axis=0, tiled=True)  22.1 us
    unnamed x43, local copies, waits for them, and re-layouts  16.6 us
    ppermute x7, waiting for transfers between devices, shift(): return lax.ppermute(x, 'dp', along_z(step))  14.4 us
    all_to_all x2, starting transfers between devices, exchange(): return lax.all_to_all(x, 'expert', split_axis=0, concat_axis=0, tiled=True)  13.3 us
    all_to_all x1, blocking collectives, exchange(): return lax.all_to_all(x, 'expert', split_axis=0, concat_axis=0, tiled=True)  11.1 us
    pallas_call x1, Pallas kernels, combine(): pl.pallas_call(combine_kernel, grid=(PARTS,), out_shape=jax.ShapeDtypeStr...  5.44 us
  transfers between devices with their start and end apart: 11, of which 8 were waited for; matrix products, arithmetic and copies ran while one was open for 1% of the time, Pallas kernels for 3%

profile of v1, /device:TPU:24, one launch (start us, length us, event | category | flops | bytes accessed | tf_op | source)
XLA Modules:
  0.0 202.3 jit_solution(13893873302822936946)
XLA Ops:
  7.2 0.9 copy-done.11
  8.1 1.1 copy-done.16
  9.2 2.4 %key_partials.1 = (bf16[16,96,512]{2,1,0:T(8,128)(2,1)S(1)}, bf16[16,96,512]{2,1,0:T(8,128)(2,1)S(1)}) custom-call(s32[1]{0:T(128)} %bitcast.8.core_ref, bf16[128,3072]{1,0:T(8,128)(2,1)S(1)} %copy-done.16, bf16[128,512]{1,0:T(8,128)(2,1)S(1)} %copy-done.11), custom_call_target="tpu_custom_call" | custom-call | flops 402653184 | bytes 5000000 | tf_op jit(solution)/shard_map/key_partials/pallas_call | solution.py:227
  11.7 1.2 copy-done.3
  12.9 2.0 %collective-permute-start = (bf16[16,96,512]{2,1,0:T(8,128)(2,1)S(1)}, bf16[16,96,512]{2,1,0:T(8,128)(2,1)S(1)}, u32[]{:S(2)}, u32[]{:S(2)}) collective-permute-start(bf16[16,96,512]{2,1,0:T(8,128)(2,1)S(1)} %get-tuple-element.22), channel_id=1, source_target_pairs={{0,16},{16,0},{32,48},{48,32},{64,80},{80,64},{96,112},{112,96},{1... | collective-permute-start | bytes 4718600 | tf_op jit(solution)/shard_map/ppermute | solution.py:355
  14.9 3.4 %collective-permute-done.got_ref = bf16[16,96,512]{2,1,0:T(8,128)(2,1)S(1)} collective-permute-done((bf16[16,96,512]{2,1,0:T(8,128)(2,1)S(1)}, bf16[16,96,512]{2,1,0:T(8,128)(2,1)S(1)}, u32[]{:S(2)}, u32[]{:S(2)}) %collective-permute-start) | collective-permute-done | bytes 1572896 | tf_op jit(solution)/shard_map/ppermute | solution.py:355
  18.3 1.1 copy-done.5
  19.4 1.4 copy-done.4
  20.9 1.4 copy-done.6
  22.3 1.2 near_sums.1
  23.5 0.7 copy-done.7
  24.2 3.8 %collective-permute-start.1 = (bf16[4,96,512]{2,1,0:T(8,128)(2,1)}, bf16[4,96,512]{2,1,0:T(8,128)(2,1)}, u32[]{:S(2)}, u32[]{:S(2)}) collective-permute-start(bf16[4,96,512]{2,1,0:T(8,128)(2,1)} %get-tuple-element.24), channel_id=1, source_target_pairs={{0,32},{16,48},{32,64},{48,80},{64,96},{80,112},{96,128},{112,144}... | collective-permute-start | bytes 1179656 | tf_op jit(solution)/shard_map/ppermute | solution.py:312
  28.0 9.5 %collective-permute-start.2 = (bf16[4,96,512]{2,1,0:T(8,128)(2,1)}, bf16[4,96,512]{2,1,0:T(8,128)(2,1)}, u32[]{:S(2)}, u32[]{:S(2)}) collective-permute-start(bf16[4,96,512]{2,1,0:T(8,128)(2,1)} %get-tuple-element.25), channel_id=1, source_target_pairs={{0,480},{16,496},{32,0},{48,16},{64,32},{80,48},{96,64},{112,80},{... | collective-permute-start | bytes 1179656 | tf_op jit(solution)/shard_map/ppermute | solution.py:312
  37.6 1.9 collective-permute-start.3
  39.5 6.0 %collective-permute-start.4 = (bf16[4,48,512]{2,1,0:T(8,128)(2,1)}, bf16[4,48,512]{2,1,0:T(8,128)(2,1)}, u32[]{:S(2)}, u32[]{:S(2)}) collective-permute-start(bf16[4,48,512]{2,1,0:T(8,128)(2,1)} %get-tuple-element.27), channel_id=1, source_target_pairs={{0,448},{16,464},{32,480},{48,496},{64,0},{80,16},{96,32},{112,48}... | collective-permute-start | bytes 589832 | tf_op jit(solution)/shard_map/ppermute | solution.py:312
  45.6 6.6 %collective-permute-done.3.up2_ref = bf16[4,48,512]{2,1,0:T(8,128)(2,1)S(1)} collective-permute-done((bf16[4,48,512]{2,1,0:T(8,128)(2,1)}, bf16[4,48,512]{2,1,0:T(8,128)(2,1)S(1)}, u32[]{:S(2)}, u32[]{:S(2)}) %collective-permute-start.3) | collective-permute-done | bytes 196640 | tf_op jit(solution)/shard_map/ppermute | solution.py:312
  52.2 2.8 %collective-permute-done.4.down2_ref = bf16[4,48,512]{2,1,0:T(8,128)(2,1)} collective-permute-done((bf16[4,48,512]{2,1,0:T(8,128)(2,1)}, bf16[4,48,512]{2,1,0:T(8,128)(2,1)}, u32[]{:S(2)}, u32[]{:S(2)}) %collective-permute-start.4) | collective-permute-done | bytes 196640 | tf_op jit(solution)/shard_map/ppermute | solution.py:312
  55.0 1.0 copy-done.8
  56.0 1.4 far_sums.1
  57.3 6.9 %collective-permute-start.7 = (bf16[96,512]{1,0:T(8,128)(2,1)S(1)}, bf16[96,512]{1,0:T(8,128)(2,1)S(1)}, u32[]{:S(2)}, u32[]{:S(2)}) collective-permute-start(bf16[96,512]{1,0:T(8,128)(2,1)S(1)} %get-tuple-element.31), channel_id=1, source_target_pairs={{0,384},{16,400},{32,416},{48,432},{64,448},{80,464},{96,480},{112... | collective-permute-start | bytes 294920 | tf_op jit(solution)/shard_map/ppermute | solution.py:312
  64.2 6.3 %collective-permute-start.6 = (bf16[96,512]{1,0:T(8,128)(2,1)S(1)}, bf16[96,512]{1,0:T(8,128)(2,1)S(1)}, u32[]{:S(2)}, u32[]{:S(2)}) collective-permute-start(bf16[96,512]{1,0:T(8,128)(2,1)S(1)} %get-tuple-element.30), channel_id=1, source_target_pairs={{0,256},{16,272},{32,288},{48,304},{64,320},{80,336},{96,352},{112... | collective-permute-start | bytes 294920 | tf_op jit(solution)/shard_map/ppermute | solution.py:312
  70.5 6.4 %collective-permute-start.5 = (bf16[96,512]{1,0:T(8,128)(2,1)S(1)}, bf16[96,512]{1,0:T(8,128)(2,1)S(1)}, u32[]{:S(2)}, u32[]{:S(2)}) collective-permute-start(bf16[96,512]{1,0:T(8,128)(2,1)S(1)} %get-tuple-element.29), channel_id=1, source_target_pairs={{0,128},{16,144},{32,160},{48,176},{64,192},{80,208},{96,224},{112... | collective-permute-start | bytes 294920 | tf_op jit(solution)/shard_map/ppermute | solution.py:312
  77.0 4.1 %collective-permute-done.6 = bf16[96,512]{1,0:T(8,128)(2,1)S(1)} collective-permute-done((bf16[96,512]{1,0:T(8,128)(2,1)S(1)}, bf16[96,512]{1,0:T(8,128)(2,1)S(1)}, u32[]{:S(2)}, u32[]{:S(2)}) %collective-permute-start.6) | collective-permute-done | bytes 98336 | tf_op jit(solution)/shard_map/ppermute | solution.py:312
  81.1 0.9 collective-permute-done.5
  82.0 0.1 add_convert_fusion
  82.1 0.7 reshape.16
  82.8 7.2 %all-to-all-start.2 = ((bf16[16,6,512]{2,1,0:T(8,128)(2,1)}), bf16[16,6,512]{2,1,0:T(8,128)(2,1)S(1)}, u32[]{:S(2)}, u32[]{:S(2)}) async-start(bf16[16,6,512]{2,1,0:T(8,128)(2,1)} %reshape.16), calls=%async_computation.2 | async-start | bytes 262144 | tf_op jit(solution)/shard_map/all_to_all | solution.py:327
  90.0 0.7 pad_bitcast_fusion
  90.7 0.1 pad.7.clone
  90.8 4.9 %all-to-all-done.2 = bf16[16,6,512]{2,1,0:T(8,128)(2,1)S(1)} async-done(((bf16[16,6,512]{2,1,0:T(8,128)(2,1)}), bf16[16,6,512]{2,1,0:T(8,128)(2,1)S(1)}, u32[]{:S(2)}, u32[]{:S(2)}) %all-to-all-start.2) | async-done | bytes 98336 | tf_op jit(solution)/shard_map/all_to_all | solution.py:327
  95.7 1.4 multiply_subtract_fusion
  97.1 0.1 maximum_maximum_fusion
  97.2 11.1 %all_to_all.15 = bf16[16,8,512]{2,1,0:T(8,128)(2,1)S(1)} all-to-all(bf16[16,8,512]{2,1,0:T(8,128)(2,1)S(1)} %maximum_maximum_fusion), channel_id=1, replica_groups=mesh['dp'=32,'expert'=16] {'expert'}, dimensions={0} | all-to-all | bytes 262144 | tf_op jit(solution)/shard_map/all_to_all | solution.py:327
  108.3 0.7 reshape.15
  109.0 4.8 %pack_rows.1 = bf16[16,272,384]{2,1,0:T(8,128)(2,1)S(1)} custom-call(bf16[34,16,3072]{2,1,0:T(8,128)(2,1)S(1)} %bitcast.14), custom_call_target="tpu_custom_call" | custom-call | flops 1610612736 | bytes 6684672 | tf_op jit(solution)/shard_map/pack_rows/pallas_call | solution.py:94
  113.9 1.7 copy-done
  115.5 6.1 %all-to-all-start.1 = ((bf16[16,272,384]{2,1,0:T(8,128)(2,1)}), bf16[16,272,384]{2,1,0:T(8,128)(2,1)S(1)}, u32[]{:S(2)}, u32[]{:S(2)}) async-start(bf16[16,272,384]{2,1,0:T(8,128)(2,1)} %copy-done), calls=%async_computation.1 | async-start | bytes 6684672 | tf_op jit(solution)/shard_map/all_to_all | solution.py:327
  121.6 0.8 slice.8
  122.4 0.6 gates.1
  123.0 0.7 copy-done.9
  123.7 0.6 copy-done.13
  124.4 38.9 %all-to-all-done.1.head_ref.tail_ref = bf16[16,272,384]{2,1,0:T(8,128)(2,1)S(1)} async-done(((bf16[16,272,384]{2,1,0:T(8,128)(2,1)}), bf16[16,272,384]{2,1,0:T(8,128)(2,1)S(1)}, u32[]{:S(2)}, u32[]{:S(2)}) %all-to-all-start.1) | async-done | bytes 3342368 | tf_op jit(solution)/shard_map/all_to_all | solution.py:327
  163.2 22.1 %all-gather.2.cloned.1.call-done.w_ref = bf16[3072,512]{1,0:T(8,128)(2,1)} async-done(((bf16[96,512]{1,0:T(8,128)(2,1)}), bf16[3072,512]{1,0:T(8,128)(2,1)}) %all-gather.2.cloned.1.call-update) | async-done | bytes 3145744 | tf_op jit(solution)/shard_map/all_gather | solution.py:351
  185.4 1.9 copy-done.2
  187.3 0.9 copy-done.10
  188.2 0.9 copy-done.14
  189.1 0.9 copy-done.15
  190.0 5.4 %combine.1 = bf16[128,3072]{1,0:T(8,128)(2,1)} custom-call(bf16[256,512]{1,0:T(8,128)(2,1)S(1)} %copy-done.10, bf16[256,256]{1,0:T(8,128)(2,1)S(1)} %copy-done.14, bf16[48,128]{1,0:T(8,128)(2,1)S(1)} %get-tuple-element.20.logit_ref, bf16[128,512]{1,0:T(8,128)(2,1)S(1)} %copy-done.12, bf16[16,272,384]{2,1,0:T(8,128)(2,1)S(1)} %all-to-all-done.1.head_ref.tail_ref, ...), custom_call_target="tpu_custom_call" | custom-call | flops 2000000000 | bytes 8000000 | tf_op jit(solution)/shard_map/combine/pallas_call | solution.py:193
  (36 shorter events, 0.2 us)
Async XLA Ops:
  7.2 0.9 copy-start.11
  8.1 1.1 copy-start.16
  11.7 1.2 copy-start.3
  12.9 82.9 %copy-start.20 = (f32[6,512]{1,0:T(8,128)S(1)}, f32[6,512]{1,0:T(8,128)}, u32[]{:S(2)}) copy-start(f32[6,512]{1,0:T(8,128)} %param.17) | copy-start | bytes 36868
  12.9 5.4 %collective-permute-start = (bf16[16,96,512]{2,1,0:T(8,128)(2,1)S(1)}, bf16[16,96,512]{2,1,0:T(8,128)(2,1)S(1)}, u32[]{:S(2)}, u32[]{:S(2)}) collective-permute-start(bf16[16,96,512]{2,1,0:T(8,128)(2,1)S(1)} %get-tuple-element.22), channel_id=1, source_target_pairs={{0,16},{16,0},{32,48},{48,32},{64,80},{80,64},{96,112},{112,96},{1... | collective-permute-start | bytes 4718600 | tf_op jit(solution)/shard_map/ppermute | solution.py:355
  18.3 1.2 copy-start.5
  19.4 1.4 copy-start.4
  20.8 1.4 copy-start.6
  22.3 86.7 %copy-start.1 = (bf16[16,34,3072]{2,0,1:T(8,128)(2,1)S(1)}, bf16[16,34,3072]{2,0,1:T(8,128)(2,1)}, u32[]{:S(2)}) copy-start(bf16[16,34,3072]{2,0,1:T(8,128)(2,1)} %param.15) | copy-start | bytes 10027012
  23.5 0.8 copy-start.7
  24.2 30.8 %collective-permute-start.1 = (bf16[4,96,512]{2,1,0:T(8,128)(2,1)}, bf16[4,96,512]{2,1,0:T(8,128)(2,1)}, u32[]{:S(2)}, u32[]{:S(2)}) collective-permute-start(bf16[4,96,512]{2,1,0:T(8,128)(2,1)} %get-tuple-element.24), channel_id=1, source_target_pairs={{0,32},{16,48},{32,64},{48,80},{64,96},{80,112},{96,128},{112,144}... | collective-permute-start | bytes 1179656 | tf_op jit(solution)/shard_map/ppermute | solution.py:312
  28.0 26.9 %collective-permute-start.2 = (bf16[4,96,512]{2,1,0:T(8,128)(2,1)}, bf16[4,96,512]{2,1,0:T(8,128)(2,1)}, u32[]{:S(2)}, u32[]{:S(2)}) collective-permute-start(bf16[4,96,512]{2,1,0:T(8,128)(2,1)} %get-tuple-element.25), channel_id=1, source_target_pairs={{0,480},{16,496},{32,0},{48,16},{64,32},{80,48},{96,64},{112,80},{... | collective-permute-start | bytes 1179656 | tf_op jit(solution)/shard_map/ppermute | solution.py:312
  37.6 14.6 %collective-permute-start.3 = (bf16[4,48,512]{2,1,0:T(8,128)(2,1)}, bf16[4,48,512]{2,1,0:T(8,128)(2,1)S(1)}, u32[]{:S(2)}, u32[]{:S(2)}) collective-permute-start(bf16[4,48,512]{2,1,0:T(8,128)(2,1)} %get-tuple-element.26), channel_id=1, source_target_pairs={{0,64},{16,80},{32,96},{48,112},{64,128},{80,144},{96,160},{112,17... | collective-permute-start | bytes 589832 | tf_op jit(solution)/shard_map/ppermute | solution.py:312
  39.5 15.5 %collective-permute-start.4 = (bf16[4,48,512]{2,1,0:T(8,128)(2,1)}, bf16[4,48,512]{2,1,0:T(8,128)(2,1)}, u32[]{:S(2)}, u32[]{:S(2)}) collective-permute-start(bf16[4,48,512]{2,1,0:T(8,128)(2,1)} %get-tuple-element.27), channel_id=1, source_target_pairs={{0,448},{16,464},{32,480},{48,496},{64,0},{80,16},{96,32},{112,48}... | collective-permute-start | bytes 589832 | tf_op jit(solution)/shard_map/ppermute | solution.py:312
  55.0 1.0 copy-start.8
  57.3 19.6 %collective-permute-start.7 = (bf16[96,512]{1,0:T(8,128)(2,1)S(1)}, bf16[96,512]{1,0:T(8,128)(2,1)S(1)}, u32[]{:S(2)}, u32[]{:S(2)}) collective-permute-start(bf16[96,512]{1,0:T(8,128)(2,1)S(1)} %get-tuple-element.31), channel_id=1, source_target_pairs={{0,384},{16,400},{32,416},{48,432},{64,448},{80,464},{96,480},{112... | collective-permute-start | bytes 294920 | tf_op jit(solution)/shard_map/ppermute | solution.py:312
  64.2 16.9 %collective-permute-start.6 = (bf16[96,512]{1,0:T(8,128)(2,1)S(1)}, bf16[96,512]{1,0:T(8,128)(2,1)S(1)}, u32[]{:S(2)}, u32[]{:S(2)}) collective-permute-start(bf16[96,512]{1,0:T(8,128)(2,1)S(1)} %get-tuple-element.30), channel_id=1, source_target_pairs={{0,256},{16,272},{32,288},{48,304},{64,320},{80,336},{96,352},{112... | collective-permute-start | bytes 294920 | tf_op jit(solution)/shard_map/ppermute | solution.py:312
  70.5 11.5 %collective-permute-start.5 = (bf16[96,512]{1,0:T(8,128)(2,1)S(1)}, bf16[96,512]{1,0:T(8,128)(2,1)S(1)}, u32[]{:S(2)}, u32[]{:S(2)}) collective-permute-start(bf16[96,512]{1,0:T(8,128)(2,1)S(1)} %get-tuple-element.29), channel_id=1, source_target_pairs={{0,128},{16,144},{32,160},{48,176},{64,192},{80,208},{96,224},{112... | collective-permute-start | bytes 294920 | tf_op jit(solution)/shard_map/ppermute | solution.py:312
  82.8 12.9 %all-to-all-start.2 = ((bf16[16,6,512]{2,1,0:T(8,128)(2,1)}), bf16[16,6,512]{2,1,0:T(8,128)(2,1)S(1)}, u32[]{:S(2)}, u32[]{:S(2)}) async-start(bf16[16,6,512]{2,1,0:T(8,128)(2,1)} %reshape.16), calls=%async_computation.2 | async-start | bytes 262144 | tf_op jit(solution)/shard_map/all_to_all | solution.py:327
  89.9 95.5 %all-gather.2.cloned.1.call-start = ((), (), s32[]{:S(2)}) async-start(), calls=%async_computation.3 | async-start | bytes 3244032 | tf_op jit(solution)/shard_map/all_gather | solution.py:351
  108.3 0.7 copy-start.19
  113.9 1.7 copy-start
  115.5 6.9 %copy-start.17 = (f32[128,16]{0,1:T(8,128)S(1)}, f32[128,16]{0,1:T(8,128)}, u32[]{:S(2)}) copy-start(f32[128,16]{0,1:T(8,128)} %param.13) | copy-start | bytes 24580
  115.5 6.9 %copy-start.18 = (s32[128,4]{0,1:T(4,128)S(1)}, s32[128,4]{0,1:T(4,128)}, u32[]{:S(2)}) copy-start(s32[128,4]{0,1:T(4,128)} %param.12) | copy-start | bytes 6148
  115.5 69.9 %copy-start.12 = (bf16[128,512]{1,0:T(8,128)(2,1)S(1)}, bf16[128,512]{1,0:T(8,128)(2,1)}, u32[]{:S(2)}) copy-start(bf16[128,512]{1,0:T(8,128)(2,1)} %cot_ref.3) | copy-start | bytes 393220
  115.5 47.7 %all-to-all-start.1 = ((bf16[16,272,384]{2,1,0:T(8,128)(2,1)}), bf16[16,272,384]{2,1,0:T(8,128)(2,1)S(1)}, u32[]{:S(2)}, u32[]{:S(2)}) async-start(bf16[16,272,384]{2,1,0:T(8,128)(2,1)} %copy-done), calls=%async_computation.1 | async-start | bytes 6684672 | tf_op jit(solution)/shard_map/all_to_all | solution.py:327
  123.0 0.7 copy-start.9
  123.7 0.6 copy-start.13
  185.4 1.9 copy-start.2
  187.3 0.9 copy-start.10
  188.2 0.9 copy-start.14
  189.1 0.9 copy-start.15
Sparse Core Ops, SparseCore 0:
  109.1 76.2 all-gather.1

commit v2 on v1

--- a/solution.py
+++ b/solution.py
@@ -23,10 +23,17 @@
 REST = CAP - HEAD
 PARTS = 8
 COLS = D // PARTS
-CHUNK = PARTS * CAP
+PER = REST * PARTS
+CHUNK = PARTS * HEAD + PER
 ZN, CORES, SUB = 16, 2, 6
 DPROWS = EXP * SUB
 
+LANES = 128
+TILES = KC // LANES
+BLOCK = SUB * TILES
+FAR = 4
+ROOM = 8
+
 VM = pltpu.VMEM
 HB = pl.ANY
 
@@ -44,7 +51,7 @@
 
 
 def cost(flops, moved):
-    return pl.CostEstimate(flops=flops, bytes_accessed=moved, transcendentals=0)
+    return pl.CostEstimate(flops=flops // 100, bytes_accessed=moved // 100, transcendentals=0)
 
 
 def full(*shape):
@@ -64,13 +71,11 @@
 
     for q in range(PARTS):
         fetch(q).start()
-    heads, rests = EXP * HEAD, EXP * REST * PARTS
+    heads, rests = EXP * HEAD, EXP * PER
     to, fr = iota((heads, heads), 0), iota((heads, heads), 1)
     move = jnp.where((to % HEAD) * EXP + to // HEAD == fr, 1.0, 0.0).astype(BF)
     to, fr = iota((rests, rests), 0), iota((rests, rests), 1)
-    per = REST * PARTS
-    place = (to % per) * EXP + to // per
-    move_rest = jnp.where(place == fr, 1.0, 0.0).astype(BF)
+    move_rest = jnp.where((to % PER) * EXP + to // PER == fr, 1.0, 0.0).astype(BF)
     rest = []
     for q in range(PARTS):
         fetch(q).wait()
@@ -80,9 +85,9 @@
         put(q).start()
         rest.append(block[HEAD * EXP :])
     rest = dot(move_rest, jnp.concatenate(rest, axis=0))
-    rest_out[...] = rest.astype(BF).reshape(EXP, per, COLS)
+    rest_out[...] = rest.astype(BF).reshape(EXP, PER, COLS)
     last = pltpu.make_async_copy(
-        rest_out, out_ref.at[:, pl.ds(PARTS * HEAD, per), :], out_sem.at[PARTS]
+        rest_out, out_ref.at[:, pl.ds(PARTS * HEAD, PER), :], out_sem.at[PARTS]
     )
     last.start()
     for q in range(PARTS):
@@ -99,7 +104,7 @@
         scratch_shapes=[
             VM((PARTS, CAP, EXP, COLS), BF),
             VM((PARTS, EXP, HEAD, COLS), BF),
-            VM((EXP, REST * PARTS, COLS), BF),
+            VM((EXP, PER, COLS), BF),
             pltpu.SemaphoreType.DMA((PARTS,)),
             pltpu.SemaphoreType.DMA((PARTS + 1,)),
         ],
@@ -147,9 +152,10 @@
 
     pick_ref[...] = weighted(grow, hit)
     rest_ref[...] = weighted(grow_rest, hit_rest)
+    dots = dots_ref[...].astype(F32)[:, BLOCK, :CAP]
     inner = jnp.zeros((EXP, TOK), F32)
     for r in range(CAP):
-        inner = inner + jnp.where(slot == float(r), dots_ref[:, r : r + 1].astype(F32), 0.0)
+        inner = inner + jnp.where(slot == float(r), dots[:, r : r + 1], 0.0)
     mean = jnp.sum(gate * inner, axis=0, keepdims=True)
     d_probs = mask * ((inner - mean) / chosen_sum)
     d_logits = probs * (d_probs - jnp.sum(probs * d_probs, axis=0, keepdims=True))
@@ -159,8 +165,8 @@
     logit_ref[...] = jnp.concatenate([one, two, three], axis=0)
 
 
-def gates(routing, base, dots):
-    heads, rests = EXP * HEAD, EXP * REST * PARTS
+def gates(routing, base, small):
+    heads, rests = EXP * HEAD, EXP * PER
     return pl.pallas_call(
         gate_kernel,
         out_shape=(
@@ -168,47 +174,75 @@
             jax.ShapeDtypeStruct((2 * TOK, rests), BF),
             jax.ShapeDtypeStruct((3 * EXP, TOK), BF),
         ),
+        grid=(1,),
+        in_specs=[
+            full(4, TOK),
+            full(EXP, TOK),
+            full(EXP, BLOCK + ROOM, LANES),
+        ],
+        out_specs=(full(2 * TOK, heads), full(2 * TOK, rests), full(3 * EXP, TOK)),
         compiler_params=params(16),
         cost_estimate=cost(10**8, 10**6),
         name="gates",
-    )(routing, base, dots)
-
-
-def combine_kernel(pick_ref, rest_ref, logit_ref, cot_ref, head_ref, tail_ref, w_ref, router_ref, out_ref):
+    )(routing, base, small)
+
+
+def routed_kernel(pick_ref, rest_ref, logit_ref, head_ref, tail_ref, router_ref, out_ref):
     q = pl.program_id(0)
-    rests = EXP * REST * PARTS
-    piece = (iota((2 * TOK, rests), 1) % (REST * PARTS)) // REST
+    rests = EXP * PER
+    piece = (iota((2 * TOK, rests), 1) % PER) // REST
     rest = jnp.where(piece == q, rest_ref[...].astype(F32), 0.0).astype(BF)
     mixed = dot(pick_ref[...], head_ref[...].reshape(EXP * HEAD, COLS))
     mixed = mixed + dot(rest, tail_ref[...].reshape(rests, COLS))
     total = mixed[:TOK] + mixed[TOK:]
     router = router_ref[...]
-    total = total + dot(logit_ref[...], jnp.concatenate([router] * 3, axis=0), 0, 0)
-    total = total + dot(cot_ref[...], w_ref[...], 1, 1)
-    out_ref[...] = total.astype(BF)
-
-
-def combine(pick, rest, logit, cot, rows, w, router):
-    heads, rests, per = EXP * HEAD, EXP * REST * PARTS, REST * PARTS
-    return pl.pallas_call(
-        combine_kernel,
+    out_ref[...] = total + dot(logit_ref[...], jnp.concatenate([router] * 3, axis=0), 0, 0)
+
+
+def routed(pick, rest, logit, rows, router):
+    heads, rests = EXP * HEAD, EXP * PER
+    return pl.pallas_call(
+        routed_kernel,
         grid=(PARTS,),
-        out_shape=jax.ShapeDtypeStruct((TOK, D), BF),
+        out_shape=jax.ShapeDtypeStruct((TOK, D), F32),
         in_specs=[
             full(2 * TOK, heads),
             full(2 * TOK, rests),
             full(3 * EXP, TOK),
-            full(TOK, KC),
             pl.BlockSpec((EXP, HEAD, COLS), lambda q: (0, q, 0)),
-            pl.BlockSpec((EXP, per, COLS), lambda q: (0, PARTS * HEAD // per, 0)),
-            pl.BlockSpec((COLS, KC), lambda q: (q, 0)),
+            pl.BlockSpec((EXP, PER, COLS), lambda q: (0, PARTS * HEAD // PER, 0)),
             pl.BlockSpec((EXP, COLS), lambda q: (0, q)),
         ],
         out_specs=pl.BlockSpec((TOK, COLS), lambda q: (0, q)),
         compiler_params=params(32),
-        cost_estimate=cost(2 * 10**9, 8 * 10**6),
-        name="combine",
-    )(pick, rest, logit, cot, rows, rows, w, router)
+        cost_estimate=cost(2 * 10**9, 6 * 10**6),
+        name="routed_terms",
+    )(pick, rest, logit, rows, rows, router)
+
+
+WIDE = 2 * COLS
+
+
+def final_kernel(part_ref, cot_ref, w_ref, out_ref):
+    key_term = dot(cot_ref[...], w_ref[...], 1, 1)
+    out_ref[...] = (part_ref[...] + key_term).astype(BF)
+
+
+def final(part, cot, w):
+    return pl.pallas_call(
+        final_kernel,
+        grid=(D // WIDE,),
+        out_shape=jax.ShapeDtypeStruct((TOK, D), BF),
+        in_specs=[
+            pl.BlockSpec((TOK, WIDE), lambda q: (0, q)),
+            full(TOK, KC),
+            pl.BlockSpec((WIDE, KC), lambda q: (q, 0)),
+        ],
+        out_specs=pl.BlockSpec((TOK, WIDE), lambda q: (0, q)),
+        compiler_params=params(32),
+        cost_estimate=cost(4 * 10**8, 6 * 10**6),
+        name="input_grad",
+    )(part, cot, w)
 
 
 def partial_kernel(core_ref, attn_ref, cot_ref, keep_ref, send_ref):
@@ -242,23 +276,13 @@
     )(core, attn, cot)
 
 
+def near_kernel(place_ref, keep_ref, got_ref, *outs):
+    for rel in range(4):
+        at = lax.rem(place_ref[0] + rel, 4)
+        outs[rel][0] = (keep_ref[at].astype(F32) + got_ref[at].astype(F32)).astype(BF)
+
+
 HALF = DPROWS // 2
-
-
-def near_kernel(place_ref, keep_ref, got_ref, own_ref, up_ref, down_ref, up2_ref, down2_ref):
-    place = place_ref[0]
-    for a in range(4):
-
-        def total(rel):
-            at = 4 * a + lax.rem(place + rel, 4)
-            return keep_ref[at].astype(F32) + got_ref[at].astype(F32)
-
-        own_ref[a] = total(0).astype(BF)
-        up_ref[a] = total(1).astype(BF)
-        down_ref[a] = total(3).astype(BF)
-        far = total(2).astype(BF)
-        up2_ref[a] = far[:HALF]
-        down2_ref[a] = far[HALF:]
 
 
 def smem():
@@ -270,38 +294,126 @@
 
 
 def near(place, keep, got):
-    whole = jax.ShapeDtypeStruct((4, DPROWS, KC), BF)
-    half = jax.ShapeDtypeStruct((4, HALF, KC), BF)
     return pl.pallas_call(
         near_kernel,
-        in_specs=[smem(), vmem(), vmem()],
-        out_specs=[vmem()] * 5,
-        out_shape=(whole, whole, whole, half, half),
+        grid=(FAR,),
+        in_specs=[smem()] + [pl.BlockSpec((4, DPROWS, KC), lambda a: (a, 0, 0))] * 2,
+        out_specs=[pl.BlockSpec((1, DPROWS, KC), lambda a: (a, 0, 0))] * 4,
+        out_shape=(jax.ShapeDtypeStruct((FAR, DPROWS, KC), BF),) * 4,
         compiler_params=params(24),
         cost_estimate=cost(10**6, 5 * 10**6),
         name="near_sums",
     )(place, keep, got)
 
 
-def far_kernel(place_ref, own_ref, up_ref, down_ref, up2_ref, down2_ref, *outs):
-    place = place_ref[0]
-    for rel in range(4):
-        at = lax.rem(place + rel, 4)
-        total = own_ref[at].astype(F32) + up_ref[at].astype(F32) + down_ref[at].astype(F32)
-        outs[rel][:HALF] = (total[:HALF] + up2_ref[at].astype(F32)).astype(BF)
-        outs[rel][HALF:] = (total[HALF:] + down2_ref[at].astype(F32)).astype(BF)
-
-
-def far(place, *given):
+def terms_kernel(own_ref, up_ref, across_ref, down_ref, out_ref):
+    size = DPROWS * TILES
+    to, fr = iota((size, size), 0), iota((size, size), 1)
+    inside = to % BLOCK
+    place = (inside // SUB) * DPROWS + (to // BLOCK) * SUB + inside % SUB
+    move = jnp.where(place == fr, 1.0, 0.0).astype(BF)
+    pieces = []
+    for a in range(FAR):
+        total = own_ref[a].astype(F32) + up_ref[a].astype(F32)
+        total = total + (across_ref[a].astype(F32) + down_ref[a].astype(F32))
+        total = total.astype(BF)
+        tall = [total[:, i * LANES : (i + 1) * LANES] for i in range(TILES)]
+        piece = dot(move, jnp.concatenate(tall, axis=0))
+        pieces.append(piece.reshape(EXP, BLOCK, LANES))
+    out_ref[...] = jnp.concatenate(pieces, axis=1).astype(BF)
+
+
+def near_terms(*given):
+    return pl.pallas_call(
+        terms_kernel,
+        in_specs=[vmem()] * 4,
+        out_specs=vmem(),
+        out_shape=jax.ShapeDtypeStruct((EXP, FAR * BLOCK, LANES), BF),
+        compiler_params=params(16),
+        cost_estimate=cost(10**8, 2 * 10**6),
+        name="near_terms",
+    )(*given)
+
+
+def far_kernel(terms_ref, out_ref):
+    out_ref[...] = jnp.sum(terms_ref[...].astype(F32), axis=0)
+
+
+def far_terms(terms):
     return pl.pallas_call(
         far_kernel,
-        in_specs=[smem()] + [vmem()] * 5,
-        out_specs=[vmem()] * 4,
-        out_shape=(jax.ShapeDtypeStruct((DPROWS, KC), BF),) * 4,
-        compiler_params=params(16),
-        cost_estimate=cost(10**6, 2 * 10**6),
-        name="far_sums",
-    )(place, *given)
+        in_specs=[vmem()],
+        out_specs=vmem(),
+        out_shape=jax.ShapeDtypeStruct((FAR * BLOCK, LANES), F32),
+        compiler_params=params(16),
+        cost_estimate=cost(10**6, 10**6),
+        name="far_terms",
+    )(terms)
+
+
+def adamw_kernel(terms_ref, weight_ref, first_ref, second_ref, *outs):
+    total = jnp.sum(terms_ref[...], axis=0)
+    grad = jnp.concatenate([total[i * SUB : (i + 1) * SUB] for i in range(TILES)], axis=1)
+    for out, value in zip(outs, adamw(weight_ref[...], first_ref[...], second_ref[...], grad)):
+        out[...] = value
+
+
+def update(*given):
+    return pl.pallas_call(
+        adamw_kernel,
+        in_specs=[vmem()] * 4,
+        out_specs=[vmem()] * 3,
+        out_shape=(jax.ShapeDtypeStruct((SUB, KC), F32),) * 3,
+        compiler_params=params(16),
+        cost_estimate=cost(10**6, 10**6),
+        name="adamw",
+    )(*given)
+
+
+def small_kernel(weight_ref, dots_ref, out_ref):
+    weight = weight_ref[...]
+    tall = jnp.concatenate([weight[:, i * LANES : (i + 1) * LANES] for i in range(TILES)], axis=0)
+    to, fr = iota((EXP * ROOM, EXP), 0), iota((EXP * ROOM, EXP), 1)
+    spread = dot(jnp.where(to == fr * ROOM, 1.0, 0.0).astype(BF), dots_ref[...])
+    spread = spread.reshape(EXP, ROOM, LANES)
+    tall = jnp.broadcast_to(tall[None], (EXP, BLOCK, LANES))
+    out_ref[...] = jnp.concatenate([tall, spread], axis=1).astype(BF)
+
+
+def small_block(weight, dots):
+    return pl.pallas_call(
+        small_kernel,
+        in_specs=[vmem()] * 2,
+        out_specs=vmem(),
+        out_shape=jax.ShapeDtypeStruct((EXP, BLOCK + ROOM, LANES), BF),
+        compiler_params=params(16),
+        cost_estimate=cost(10**6, 10**6),
+        name="small_block",
+    )(weight, dots)
+
+
+def order_kernel(small_ref, out_ref):
+    size = EXP * (BLOCK + ROOM)
+    blocks = small_ref[...].reshape(size, LANES)
+    fr = iota((1, size), 1)
+    expert, inside = fr // (BLOCK + ROOM), fr % (BLOCK + ROOM)
+    row = expert * SUB + inside % SUB
+    to = iota((DPROWS, size), 0)
+    for i in range(TILES):
+        move = jnp.where(jnp.where(inside // SUB == i, row, -1) == to, 1.0, 0.0).astype(BF)
+        out_ref[:, i * LANES : (i + 1) * LANES] = dot(move, blocks).astype(BF)
+
+
+def order_rows(small):
+    return pl.pallas_call(
+        order_kernel,
+        in_specs=[vmem()],
+        out_specs=vmem(),
+        out_shape=jax.ShapeDtypeStruct((DPROWS, KC), BF),
+        compiler_params=params(16),
+        cost_estimate=cost(10**8, 10**6),
+        name="order_key_rows",
+    )(small)
 
 
 def along_z(step):
@@ -325,6 +437,17 @@
 
 def exchange(x):
     return lax.all_to_all(x, "expert", split_axis=0, concat_axis=0, tiled=True)
+
+
+def exchange_far(x):
+    groups = [
+        [(4 * a + b) * CORES + c for a in range(FAR)] for b in range(4) for c in range(CORES)
+    ]
+    return lax.all_to_all(x, "dp", 0, 0, axis_index_groups=groups, tiled=True)
+
+
+def swap_core(x):
+    return lax.ppermute(x, "dp", [(i, i ^ 1) for i in range(ZN * CORES)])
 
 
 def local(
@@ -340,31 +463,27 @@
     second_moment,
 ):
     dp = lax.axis_index("dp")
-    core, z = lax.rem(dp, CORES), dp // CORES
-    near_place, far_place = lax.rem(z, 4)[None], (z // 4)[None]
-    w = jnp.broadcast_to(key_weight.astype(BF)[None], (EXP, SUB, KC))
-    inner = jnp.pad(expert_dots, ((0, 0), (0, KC - CAP)))[:, None, :]
-    small = jnp.concatenate([w, inner, jnp.zeros_like(inner)], axis=1)
+    core, z = lax.rem(dp, CORES)[None], dp // CORES
+    near_place = lax.rem(z, 4)[None]
+    dots = jnp.pad(expert_dots, ((0, 0), (0, LANES - CAP)))
+    small, cot = lax.optimization_barrier((small_block(key_weight, dots), key_cot))
     small = exchange(small)
-    w = small[:, :SUB].reshape(DPROWS, KC)
-    dots = small[:, SUB, :CAP]
-    w = lax.all_gather(w, "dp", axis=0, tiled=True)
-    rows = exchange(pack(jnp.swapaxes(expert_rows, 0, 1)))
-    pick, rest, logit = gates(routing.T, router_base.T, dots)
-    keep, send = partials(core[None], attn_input, key_cot)
-    got = lax.ppermute(send, "dp", [(i, i ^ 1) for i in range(ZN * CORES)])
-    own, up, down, up2, down2 = near(near_place, keep, got)
-    own, up, across, down = far(
-        far_place, own, shift(up, 1), shift(down, -1), shift(up2, 2), shift(down2, -2)
-    )
-    up, across, down = shift(up, 4), shift(across, 8), shift(down, -4)
-    summed = (
-        own.astype(F32) + up.astype(F32) + across.astype(F32) + down.astype(F32)
-    ).astype(BF)
-    summed = exchange(summed.reshape(EXP, SUB, KC))
-    key_grad = jnp.sum(summed.astype(F32), axis=0)
-    updated = adamw(key_weight, first_moment, second_moment, key_grad)
-    input_grad = combine(pick, rest, logit, key_cot, rows, w, router_weight.T)
+    keep, send = partials(core, attn_input, cot)
+    got = swap_core(send)
+    packed = pack(jnp.swapaxes(expert_rows, 0, 1))
+    small, packed, keep, got = lax.optimization_barrier((small, packed, keep, got))
+    key_rows, packed, keep = lax.optimization_barrier((order_rows(small), packed, keep))
+    w = lax.all_gather(key_rows, "dp", axis=0, tiled=True)
+    rows = exchange(packed)
+    own, up, across, down = near(near_place, keep, got)
+    terms = near_terms(own, shift(up, 1), shift(across, -2), shift(down, -1))
+    terms, rows = lax.optimization_barrier((terms, rows))
+    grads = far_terms(exchange(terms))
+    pick, rest, logit = gates(routing.T, router_base.T, small)
+    part = routed(pick, rest, logit, rows, router_weight.T)
+    grads = exchange_far(grads.reshape(FAR, BLOCK, LANES))
+    updated = update(grads, key_weight, first_moment, second_moment)
+    input_grad = final(part, key_cot, w)
     return (input_grad, *updated)
 
 

time: 205 us -> 150 us (0.73)
  waiting for transfers between devices: 83.7 us -> 35.9 us
  starting transfers between devices: 56.2 us -> 45.1 us
  blocking collectives: 11.1 us -> 14.5 us
  Pallas kernels: 15.9 us -> 18.8 us
    all_to_all x2, waiting for transfers between devices: 43.8 us -> 0.01 us  [exchange(): return lax.all_to_all(x, 'expert', split_axis=0, concat_axis=0, tiled=True)]
    ppermute x7 -> x3, starting transfers between devices: 40.9 us -> 15.9 us  [shift(): return lax.ppermute(x, 'dp', along_z(step))]
    all_gather x1, waiting for transfers between devices: 22.1 us -> 0.01 us  [local(): w = lax.all_gather(key_rows, 'dp', axis=0, tiled=True)]
    ppermute x7 -> x3, waiting for transfers between devices: 14.4 us -> 29.8 us  [shift(): return lax.ppermute(x, 'dp', along_z(step))]
    all_to_all x0 -> x1, starting transfers between devices: none -> 11 us  [exchange_far(): return lax.all_to_all(x, 'dp', 0, 0, axis_index_groups=groups, tiled=True)]
    all_to_all x0 -> x1, waiting for transfers between devices: none -> 6.01 us  [exchange_far(): return lax.all_to_all(x, 'dp', 0, 0, axis_index_groups=groups, tiled=True)]
    all_to_all x1, blocking collectives: 11.1 us -> 14.5 us  [exchange(): return lax.all_to_all(x, 'expert', split_axis=0, concat_axis=0, tiled=True)]
    ppermute x1, waiting for transfers between devices: 3.35 us -> 0.01 us  [swap_core(): return lax.ppermute(x, 'dp', [(i, i ^ 1) for i in range(ZN * CORES)])]
  transfers between devices with their start and end apart: 11 -> 8, of which waited for: 8 -> 4; matrix products, arithmetic and copies ran while one was open for 1% -> 0% of each run, Pallas kernels for 3% -> 8%
where the time goes in v2:
time: 150 us; the launch traced here: 148 us
  starting transfers between devices  45.1 us (30%)
  waiting for transfers between devices  35.9 us (24%)
  local copies, waits for them, and re-layouts  19.1 us (13%)
  Pallas kernels  18.8 us (13%)
  blocking collectives  14.5 us (10%)
  between operations  14.2 us (9%)
    ppermute x3, waiting for transfers between devices, shift(): return lax.ppermute(x, 'dp', along_z(step))  29.8 us
    unnamed x40, local copies, waits for them, and re-layouts  18.4 us
    all_to_all x2, starting transfers between devices, exchange(): return lax.all_to_all(x, 'expert', split_axis=0, concat_axis=0, tiled=True)  16.2 us
    ppermute x3, starting transfers between devices, shift(): return lax.ppermute(x, 'dp', along_z(step))  15.9 us
    all_to_all x1, blocking collectives, exchange(): return lax.all_to_all(x, 'expert', split_axis=0, concat_axis=0, tiled=True)  14.5 us
    all_to_all x1, starting transfers between devices, exchange_far(): return lax.all_to_all(x, 'dp', 0, 0, axis_index_groups=groups, tiled=True)  11 us
    all_to_all x1, waiting for transfers between devices, exchange_far(): return lax.all_to_all(x, 'dp', 0, 0, axis_index_groups=groups, tiled=True)  6.01 us
    pallas_call x1, Pallas kernels, pack(): pl.pallas_call(pack_kernel, out_shape=jax.ShapeDtypeStruct((EXP, CHUNK, C...  4.82 us
  transfers between devices with their start and end apart: 8, of which 4 were waited for; matrix products, arithmetic and copies ran while one was open for 0% of the time, Pallas kernels for 8%

profile of v2, /device:TPU:24, one launch (start us, length us, event | category | flops | bytes accessed | tf_op | source)
XLA Modules:
  0.0 147.5 jit_solution(5810616277566716836)
XLA Ops:
  7.2 0.7 pad.4.dots_ref
  7.9 0.7 copy-done.14
  8.6 0.8 small_block.1
  9.4 1.1 copy-done.10
  10.5 0.9 copy-done.11
  11.4 2.5 %key_partials.1 = (bf16[16,96,512]{2,1,0:T(8,128)(2,1)S(1)}, bf16[16,96,512]{2,1,0:T(8,128)(2,1)S(1)}) custom-call(s32[1]{0:T(128)} %bitcast.3.core_ref, bf16[128,3072]{1,0:T(8,128)(2,1)S(1)} %copy-done.10, bf16[128,512]{1,0:T(8,128)(2,1)S(1)} %copy-done.11), custom_call_target="tpu_custom_call" | custom-call | flops 4026531 | bytes 50000 | tf_op jit(solution)/shard_map/key_partials/pallas_call | solution.py:261
  13.9 0.0 copy-start.5
  13.9 1.2 copy-done.5
  15.1 1.9 %collective-permute-start = (bf16[16,96,512]{2,1,0:T(8,128)(2,1)S(1)}, bf16[16,96,512]{2,1,0:T(8,128)(2,1)S(1)}, u32[]{:S(2)}, u32[]{:S(2)}) collective-permute-start(bf16[16,96,512]{2,1,0:T(8,128)(2,1)S(1)} %get-tuple-element.30), channel_id=1, source_target_pairs={{0,16},{16,0},{32,48},{48,32},{64,80},{80,64},{96,112},{112,96},{1... | collective-permute-start | bytes 4718600 | tf_op jit(solution)/shard_map/ppermute | solution.py:450
  17.0 9.0 %all-to-all-start = ((bf16[16,32,128]{2,1,0:T(8,128)(2,1)}), bf16[16,32,128]{2,1,0:T(8,128)(2,1)S(1)}, u32[]{:S(2)}, u32[]{:S(2)}) async-start(bf16[16,32,128]{2,1,0:T(8,128)(2,1)} %small_block.1), calls=%async_computation | async-start | bytes 262144 | tf_op jit(solution)/shard_map/all_to_all | solution.py:439
  26.0 0.0 all-gather.2.cloned.1.call-start
  26.0 0.0 copy-start.3
  26.0 1.9 %copy-done.3 = bf16[16,34,3072]{2,0,1:T(8,128)(2,1)S(1)} copy-done((bf16[16,34,3072]{2,0,1:T(8,128)(2,1)S(1)}, bf16[16,34,3072]{2,0,1:T(8,128)(2,1)}, u32[]{:S(2)}) %copy-start.3) | copy-done | bytes 3342360
  28.0 4.8 %pack_rows.1 = bf16[16,272,384]{2,1,0:T(8,128)(2,1)S(1)} custom-call(bf16[34,16,3072]{2,1,0:T(8,128)(2,1)S(1)} %bitcast.7), custom_call_target="tpu_custom_call" | custom-call | flops 16106127 | bytes 66846 | tf_op jit(solution)/shard_map/pack_rows/pallas_call | solution.py:99
  32.8 0.0 copy-start
  32.8 1.7 %copy-done = bf16[16,272,384]{2,1,0:T(8,128)(2,1)} copy-done((bf16[16,272,384]{2,1,0:T(8,128)(2,1)}, bf16[16,272,384]{2,1,0:T(8,128)(2,1)S(1)}, u32[]{:S(2)}) %copy-start) | copy-done | bytes 3342360
  34.5 0.0 all-to-all-done.dots_ref.small_ref
  34.5 0.0 collective-permute-done.got_ref
  34.5 1.2 copy-done.7
  35.7 1.0 order_key_rows.1
  36.6 0.0 all-gather.2.cloned.1.call-update
  36.7 7.2 %all-to-all-start.1 = ((bf16[16,272,384]{2,1,0:T(8,128)(2,1)}), bf16[16,272,384]{2,1,0:T(8,128)(2,1)S(1)}, u32[]{:S(2)}, u32[]{:S(2)}) async-start(bf16[16,272,384]{2,1,0:T(8,128)(2,1)} %copy-done), calls=%async_computation.1 | async-start | bytes 6684672 | tf_op jit(solution)/shard_map/all_to_all | solution.py:439
  43.9 1.4 copy-done.6
  45.3 1.4 copy-done.8
  46.7 0.4 near_sums.1
  47.2 2.0 %collective-permute-start.1 = (bf16[4,96,512]{2,1,0:T(8,128)(2,1)S(1)}, bf16[4,96,512]{2,1,0:T(8,128)(2,1)S(1)}, u32[]{:S(2)}, u32[]{:S(2)}) collective-permute-start(bf16[4,96,512]{2,1,0:T(8,128)(2,1)S(1)} %get-tuple-element.40), channel_id=1, source_target_pairs={{0,32},{16,48},{32,64},{48,80},{64,96},{80,112},{96,128},{112,144}... | collective-permute-start | bytes 1179656 | tf_op jit(solution)/shard_map/ppermute | solution.py:424
  49.2 10.9 %collective-permute-start.2 = (bf16[4,96,512]{2,1,0:T(8,128)(2,1)S(1)}, bf16[4,96,512]{2,1,0:T(8,128)(2,1)S(1)}, u32[]{:S(2)}, u32[]{:S(2)}) collective-permute-start(bf16[4,96,512]{2,1,0:T(8,128)(2,1)S(1)} %get-tuple-element.41), channel_id=1, source_target_pairs={{0,448},{16,464},{32,480},{48,496},{64,0},{80,16},{96,32},{112,48}... | collective-permute-start | bytes 1179656 | tf_op jit(solution)/shard_map/ppermute | solution.py:424
  60.2 2.9 %collective-permute-start.3 = (bf16[4,96,512]{2,1,0:T(8,128)(2,1)S(1)}, bf16[4,96,512]{2,1,0:T(8,128)(2,1)S(1)}, u32[]{:S(2)}, u32[]{:S(2)}) collective-permute-start(bf16[4,96,512]{2,1,0:T(8,128)(2,1)S(1)} %get-tuple-element.42), channel_id=1, source_target_pairs={{0,480},{16,496},{32,0},{48,16},{64,32},{80,48},{96,64},{112,80},{... | collective-permute-start | bytes 1179656 | tf_op jit(solution)/shard_map/ppermute | solution.py:424
  63.1 4.8 %collective-permute-done.1.up_ref = bf16[4,96,512]{2,1,0:T(8,128)(2,1)S(1)} collective-permute-done((bf16[4,96,512]{2,1,0:T(8,128)(2,1)S(1)}, bf16[4,96,512]{2,1,0:T(8,128)(2,1)S(1)}, u32[]{:S(2)}, u32[]{:S(2)}) %collective-permute-start.1) | collective-permute-done | bytes 393248 | tf_op jit(solution)/shard_map/ppermute | solution.py:424
  67.8 14.8 %collective-permute-done.2.across_ref = bf16[4,96,512]{2,1,0:T(8,128)(2,1)S(1)} collective-permute-done((bf16[4,96,512]{2,1,0:T(8,128)(2,1)S(1)}, bf16[4,96,512]{2,1,0:T(8,128)(2,1)S(1)}, u32[]{:S(2)}, u32[]{:S(2)}) %collective-permute-start.2) | collective-permute-done | bytes 393248 | tf_op jit(solution)/shard_map/ppermute | solution.py:424
  82.7 10.2 %collective-permute-done.3.down_ref = bf16[4,96,512]{2,1,0:T(8,128)(2,1)S(1)} collective-permute-done((bf16[4,96,512]{2,1,0:T(8,128)(2,1)S(1)}, bf16[4,96,512]{2,1,0:T(8,128)(2,1)S(1)}, u32[]{:S(2)}, u32[]{:S(2)}) %collective-permute-start.3) | collective-permute-done | bytes 393248 | tf_op jit(solution)/shard_map/ppermute | solution.py:424
  92.9 0.8 near_terms.1
  93.7 0.0 copy-start.9
  93.7 0.7 copy-done.9
  94.5 0.0 all-to-all-done.1.head_ref.tail_ref
  94.5 14.5 %all_to_all.20.terms_ref = bf16[16,96,128]{2,1,0:T(8,128)(2,1)S(1)} all-to-all(bf16[16,96,128]{2,1,0:T(8,128)(2,1)} %copy-done.9), channel_id=1, replica_groups=mesh['dp'=32,'expert'=16] {'expert'}, dimensions={0} | all-to-all | bytes 786432 | tf_op jit(solution)/shard_map/all_to_all | solution.py:439
  108.9 0.7 far_terms.1
  109.6 11.0 %all-to-all-start.3 = ((f32[4,24,128]{2,1,0:T(8,128)}), f32[4,24,128]{2,1,0:T(8,128)S(1)}, u32[]{:S(2)}, u32[]{:S(2)}) async-start(f32[4,24,128]{2,1,0:T(8,128)} %bitcast.6), calls=%async_computation.3 | async-start | bytes 98304 | tf_op jit(solution)/shard_map/all_to_all | solution.py:446
  120.6 0.7 gates.1
  121.4 0.9 copy-done.13
  122.3 3.9 %routed_terms.1.part_ref = f32[128,3072]{1,0:T(8,128)S(1)} custom-call(bf16[256,512]{1,0:T(8,128)(2,1)S(1)} %get-tuple-element.32.pick_ref, bf16[256,256]{1,0:T(8,128)(2,1)S(1)} %get-tuple-element.33.rest_ref, bf16[48,128]{1,0:T(8,128)(2,1)S(1)} %get-tuple-element.34.logit_ref, bf16[16,272,384]{2,1,0:T(8,128)(2,1)S(1)} %all-to-all-done.1.head_ref.tail_ref, ...), custom_call_target="tpu_custom_call" | custom-call | flops 20000000 | bytes 60000 | tf_op jit(solution)/shard_map/routed_terms/pallas_call | solution.py:204
  126.2 1.2 copy-done.1
  127.4 6.0 %all-to-all-done.3.terms_ref = f32[4,24,128]{2,1,0:T(8,128)S(1)} async-done(((f32[4,24,128]{2,1,0:T(8,128)}), f32[4,24,128]{2,1,0:T(8,128)S(1)}, u32[]{:S(2)}, u32[]{:S(2)}) %all-to-all-start.3) | async-done | bytes 49184 | tf_op jit(solution)/shard_map/all_to_all | solution.py:446
  133.4 0.7 copy-done.17
  134.1 0.6 adamw.1
  134.8 1.4 copy-done.2
  136.2 1.9 %copy-done.4 = bf16[3072,512]{1,0:T(8,128)(2,1)S(1)} copy-done((bf16[3072,512]{1,0:T(8,128)(2,1)S(1)}, bf16[3072,512]{1,0:T(8,128)(2,1)}, u32[]{:S(2)}) %copy-start.4) | copy-done | bytes 3145752
  138.1 2.6 %input_grad.1 = bf16[128,3072]{1,0:T(8,128)(2,1)} custom-call(f32[128,3072]{1,0:T(8,128)S(1)} %copy-done.2, bf16[128,512]{1,0:T(8,128)(2,1)S(1)} %copy-done.12, bf16[3072,512]{1,0:T(8,128)(2,1)S(1)} %copy-done.4), custom_call_target="tpu_custom_call" | custom-call | flops 4000000 | bytes 60000 | tf_op jit(solution)/shard_map/input_grad/pallas_call | solution.py:232
  (22 shorter events, 0.0 us)
Async XLA Ops:
  7.9 0.7 copy-start.14
  9.4 1.1 copy-start.10
  10.5 0.9 copy-start.11
  13.9 1.2 copy-start.5
  15.1 19.4 %collective-permute-start = (bf16[16,96,512]{2,1,0:T(8,128)(2,1)S(1)}, bf16[16,96,512]{2,1,0:T(8,128)(2,1)S(1)}, u32[]{:S(2)}, u32[]{:S(2)}) collective-permute-start(bf16[16,96,512]{2,1,0:T(8,128)(2,1)S(1)} %get-tuple-element.30), channel_id=1, source_target_pairs={{0,16},{16,0},{32,48},{48,32},{64,80},{80,64},{96,112},{112,96},{1... | collective-permute-start | bytes 4718600 | tf_op jit(solution)/shard_map/ppermute | solution.py:450
  17.0 17.5 %all-to-all-start = ((bf16[16,32,128]{2,1,0:T(8,128)(2,1)}), bf16[16,32,128]{2,1,0:T(8,128)(2,1)S(1)}, u32[]{:S(2)}, u32[]{:S(2)}) async-start(bf16[16,32,128]{2,1,0:T(8,128)(2,1)} %small_block.1), calls=%async_computation | async-start | bytes 262144 | tf_op jit(solution)/shard_map/all_to_all | solution.py:439
  26.0 108.8 %all-gather.2.cloned.1.call-start = ((), (), s32[]{:S(2)}) async-start(), calls=%async_computation.4 | async-start | bytes 3244032 | tf_op jit(solution)/shard_map/all_gather | solution.py:476
  26.0 1.9 %copy-start.3 = (bf16[16,34,3072]{2,0,1:T(8,128)(2,1)S(1)}, bf16[16,34,3072]{2,0,1:T(8,128)(2,1)}, u32[]{:S(2)}) copy-start(bf16[16,34,3072]{2,0,1:T(8,128)(2,1)} %param.15) | copy-start | bytes 10027012
  32.8 1.7 %copy-start = (bf16[16,272,384]{2,1,0:T(8,128)(2,1)}, bf16[16,272,384]{2,1,0:T(8,128)(2,1)S(1)}, u32[]{:S(2)}) copy-start(bf16[16,272,384]{2,1,0:T(8,128)(2,1)S(1)} %pack_rows.1) | copy-start | bytes 10027012
  34.5 1.2 copy-start.7
  36.7 57.8 %all-to-all-start.1 = ((bf16[16,272,384]{2,1,0:T(8,128)(2,1)}), bf16[16,272,384]{2,1,0:T(8,128)(2,1)S(1)}, u32[]{:S(2)}, u32[]{:S(2)}) async-start(bf16[16,272,384]{2,1,0:T(8,128)(2,1)} %copy-done), calls=%async_computation.1 | async-start | bytes 6684672 | tf_op jit(solution)/shard_map/all_to_all | solution.py:439
  43.9 1.4 copy-start.6
  45.3 1.4 copy-start.8
  46.7 73.9 %copy-start.18 = (f32[128,16]{0,1:T(8,128)S(1)}, f32[128,16]{0,1:T(8,128)}, u32[]{:S(2)}) copy-start(f32[128,16]{0,1:T(8,128)} %param.13) | copy-start | bytes 24580
  46.7 73.9 %copy-start.19 = (s32[128,4]{0,1:T(4,128)S(1)}, s32[128,4]{0,1:T(4,128)}, u32[]{:S(2)}) copy-start(s32[128,4]{0,1:T(4,128)} %param.12) | copy-start | bytes 6148
  47.2 20.7 %collective-permute-start.1 = (bf16[4,96,512]{2,1,0:T(8,128)(2,1)S(1)}, bf16[4,96,512]{2,1,0:T(8,128)(2,1)S(1)}, u32[]{:S(2)}, u32[]{:S(2)}) collective-permute-start(bf16[4,96,512]{2,1,0:T(8,128)(2,1)S(1)} %get-tuple-element.40), channel_id=1, source_target_pairs={{0,32},{16,48},{32,64},{48,80},{64,96},{80,112},{96,128},{112,144}... | collective-permute-start | bytes 1179656 | tf_op jit(solution)/shard_map/ppermute | solution.py:424
  49.2 33.5 %collective-permute-start.2 = (bf16[4,96,512]{2,1,0:T(8,128)(2,1)S(1)}, bf16[4,96,512]{2,1,0:T(8,128)(2,1)S(1)}, u32[]{:S(2)}, u32[]{:S(2)}) collective-permute-start(bf16[4,96,512]{2,1,0:T(8,128)(2,1)S(1)} %get-tuple-element.41), channel_id=1, source_target_pairs={{0,448},{16,464},{32,480},{48,496},{64,0},{80,16},{96,32},{112,48}... | collective-permute-start | bytes 1179656 | tf_op jit(solution)/shard_map/ppermute | solution.py:424
  60.2 32.8 %collective-permute-start.3 = (bf16[4,96,512]{2,1,0:T(8,128)(2,1)S(1)}, bf16[4,96,512]{2,1,0:T(8,128)(2,1)S(1)}, u32[]{:S(2)}, u32[]{:S(2)}) collective-permute-start(bf16[4,96,512]{2,1,0:T(8,128)(2,1)S(1)} %get-tuple-element.42), channel_id=1, source_target_pairs={{0,480},{16,496},{32,0},{48,16},{64,32},{80,48},{96,64},{112,80},{... | collective-permute-start | bytes 1179656 | tf_op jit(solution)/shard_map/ppermute | solution.py:424
  93.7 0.7 copy-start.9
  109.6 23.8 %all-to-all-start.3 = ((f32[4,24,128]{2,1,0:T(8,128)}), f32[4,24,128]{2,1,0:T(8,128)S(1)}, u32[]{:S(2)}, u32[]{:S(2)}) async-start(f32[4,24,128]{2,1,0:T(8,128)} %bitcast.6), calls=%async_computation.3 | async-start | bytes 98304 | tf_op jit(solution)/shard_map/all_to_all | solution.py:446
  121.3 0.9 copy-start.13
  122.2 11.1 %copy-start.15 = (f32[6,512]{1,0:T(8,128)S(1)}, f32[6,512]{1,0:T(8,128)}, u32[]{:S(2)}) copy-start(f32[6,512]{1,0:T(8,128)} %weight_ref.3) | copy-start | bytes 36868
  122.2 11.1 %copy-start.16 = (f32[6,512]{1,0:T(8,128)S(1)}, f32[6,512]{1,0:T(8,128)}, u32[]{:S(2)}) copy-start(f32[6,512]{1,0:T(8,128)} %first_ref.1) | copy-start | bytes 36868
  122.3 12.5 %copy-start.12 = (bf16[128,512]{1,0:T(8,128)(2,1)S(1)}, bf16[128,512]{1,0:T(8,128)(2,1)}, u32[]{:S(2)}) copy-start(bf16[128,512]{1,0:T(8,128)(2,1)} %cot_ref.2) | copy-start | bytes 393220
  126.2 1.2 copy-start.1
  133.4 0.7 copy-start.17
  134.8 1.4 copy-start.2
  136.2 1.9 %copy-start.4 = (bf16[3072,512]{1,0:T(8,128)(2,1)S(1)}, bf16[3072,512]{1,0:T(8,128)(2,1)}, u32[]{:S(2)}) copy-start(bf16[3072,512]{1,0:T(8,128)(2,1)} %all-gather.2.cloned.1.call-done.w_ref) | copy-start | bytes 9437188
Sparse Core Ops, SparseCore 0:
  36.8 80.7 all-gather.1

commit v3 on v2

--- a/solution.py
+++ b/solution.py
@@ -24,7 +24,7 @@
 PARTS = 8
 COLS = D // PARTS
 PER = REST * PARTS
-CHUNK = PARTS * HEAD + PER
+ROWS = PARTS * HEAD + PER
 ZN, CORES, SUB = 16, 2, 6
 DPROWS = EXP * SUB
 
@@ -32,6 +32,9 @@
 TILES = KC // LANES
 BLOCK = SUB * TILES
 FAR = 4
+SPAN = COLS // LANES
+LINE = BLOCK // SPAN
+KEYS = ZN * LINE
 ROOM = 8
 
 VM = pltpu.VMEM
@@ -52,6 +55,13 @@
 
 def cost(flops, moved):
     return pl.CostEstimate(flops=flops // 100, bytes_accessed=moved // 100, transcendentals=0)
+
+
+BIG = 56
+
+
+def smem():
+    return pl.BlockSpec(memory_space=pltpu.SMEM)
 
 
 def full(*shape):
@@ -98,7 +108,7 @@
 def pack(rows):
     return pl.pallas_call(
         pack_kernel,
-        out_shape=jax.ShapeDtypeStruct((EXP, CHUNK, COLS), BF),
+        out_shape=jax.ShapeDtypeStruct((EXP, ROWS, COLS), BF),
         in_specs=[pl.BlockSpec(memory_space=HB)],
         out_specs=pl.BlockSpec(memory_space=HB),
         scratch_shapes=[
@@ -108,7 +118,7 @@
             pltpu.SemaphoreType.DMA((PARTS,)),
             pltpu.SemaphoreType.DMA((PARTS + 1,)),
         ],
-        compiler_params=params(32),
+        compiler_params=params(BIG),
         cost_estimate=cost(2 * 512 * 512 * D, 2 * EXP * CAP * D * 2),
         name="pack_rows",
     )(rows)
@@ -187,7 +197,9 @@
     )(routing, base, small)
 
 
-def routed_kernel(pick_ref, rest_ref, logit_ref, head_ref, tail_ref, router_ref, out_ref):
+def combine_kernel(
+    pick_ref, rest_ref, logit_ref, cot_ref, head_ref, tail_ref, w_ref, router_ref, out_ref
+):
     q = pl.program_id(0)
     rests = EXP * PER
     piece = (iota((2 * TOK, rests), 1) % PER) // REST
@@ -196,53 +208,32 @@
     mixed = mixed + dot(rest, tail_ref[...].reshape(rests, COLS))
     total = mixed[:TOK] + mixed[TOK:]
     router = router_ref[...]
-    out_ref[...] = total + dot(logit_ref[...], jnp.concatenate([router] * 3, axis=0), 0, 0)
-
-
-def routed(pick, rest, logit, rows, router):
+    total = total + dot(logit_ref[...], jnp.concatenate([router] * 3, axis=0), 0, 0)
+    total = total + dot(cot_ref[...], w_ref[...], 1, 1)
+    out_ref[...] = total.astype(BF)
+
+
+def combine(pick, rest, logit, cot, rows, w, router):
     heads, rests = EXP * HEAD, EXP * PER
     return pl.pallas_call(
-        routed_kernel,
+        combine_kernel,
         grid=(PARTS,),
-        out_shape=jax.ShapeDtypeStruct((TOK, D), F32),
+        out_shape=jax.ShapeDtypeStruct((TOK, D), BF),
         in_specs=[
             full(2 * TOK, heads),
             full(2 * TOK, rests),
             full(3 * EXP, TOK),
+            full(TOK, KC),
             pl.BlockSpec((EXP, HEAD, COLS), lambda q: (0, q, 0)),
             pl.BlockSpec((EXP, PER, COLS), lambda q: (0, PARTS * HEAD // PER, 0)),
+            pl.BlockSpec((COLS, KC), lambda q: (q, 0)),
             pl.BlockSpec((EXP, COLS), lambda q: (0, q)),
         ],
         out_specs=pl.BlockSpec((TOK, COLS), lambda q: (0, q)),
-        compiler_params=params(32),
-        cost_estimate=cost(2 * 10**9, 6 * 10**6),
-        name="routed_terms",
-    )(pick, rest, logit, rows, rows, router)
-
-
-WIDE = 2 * COLS
-
-
-def final_kernel(part_ref, cot_ref, w_ref, out_ref):
-    key_term = dot(cot_ref[...], w_ref[...], 1, 1)
-    out_ref[...] = (part_ref[...] + key_term).astype(BF)
-
-
-def final(part, cot, w):
-    return pl.pallas_call(
-        final_kernel,
-        grid=(D // WIDE,),
-        out_shape=jax.ShapeDtypeStruct((TOK, D), BF),
-        in_specs=[
-            pl.BlockSpec((TOK, WIDE), lambda q: (0, q)),
-            full(TOK, KC),
-            pl.BlockSpec((WIDE, KC), lambda q: (q, 0)),
-        ],
-        out_specs=pl.BlockSpec((TOK, WIDE), lambda q: (0, q)),
-        compiler_params=params(32),
-        cost_estimate=cost(4 * 10**8, 6 * 10**6),
-        name="input_grad",
-    )(part, cot, w)
+        compiler_params=params(BIG),
+        cost_estimate=cost(2 * 10**9, 8 * 10**6),
+        name="combine",
+    )(pick, rest, logit, cot, rows, rows, w, router)
 
 
 def partial_kernel(core_ref, attn_ref, cot_ref, keep_ref, send_ref):
@@ -276,83 +267,100 @@
     )(core, attn, cot)
 
 
-def near_kernel(place_ref, keep_ref, got_ref, *outs):
+PIECES = [
+    (tile, span)
+    for tile in range(TILES)
+    for span in range(SPAN)
+    if tile * SUB < (span + 1) * LINE and (tile + 1) * SUB > span * LINE
+]
+
+
+def fill_kernel(keep_ref, got_ref, out_ref, moves):
+    tall, wide = 2 * EXP * LINE, 2 * DPROWS
+
+    @pl.when(pl.program_id(0) == 0)
+    def _():
+        to, fr = iota((tall, wide), 0), iota((tall, wide), 1)
+        expert, pair, line = to // (2 * LINE), (to // LINE) % 2, to % LINE
+        same = (fr // DPROWS == pair) & ((fr % DPROWS) // SUB == expert)
+        for n, (tile, span) in enumerate(PIECES):
+            hit = same & (tile * SUB + fr % SUB == span * LINE + line)
+            moves[n] = jnp.where(hit, 1.0, 0.0).astype(BF)
+
+    for i in range(2):
+        at = slice(2 * i, 2 * i + 2)
+        total = keep_ref[at].astype(F32) + got_ref[at].astype(F32)
+        total = total.reshape(wide, KC).astype(BF)
+        spans = [jnp.zeros((tall, LANES), F32)] * SPAN
+        for n, (tile, span) in enumerate(PIECES):
+            spans[span] = spans[span] + dot(moves[n], total[:, tile * LANES : (tile + 1) * LANES])
+        out = jnp.concatenate(spans, axis=1).astype(BF)
+        out_ref[:, i * 2 * LINE : (i + 1) * 2 * LINE, :] = out.reshape(EXP, 2 * LINE, COLS)
+
+
+def fill(keep, got):
+    block = pl.BlockSpec((4, DPROWS, KC), lambda i: (i, 0, 0))
+    return pl.pallas_call(
+        fill_kernel,
+        grid=(ZN // 4,),
+        out_shape=jax.ShapeDtypeStruct((EXP, KEYS, COLS), BF),
+        in_specs=[block, block],
+        out_specs=pl.BlockSpec((EXP, 4 * LINE, COLS), lambda i: (0, i, 0)),
+        scratch_shapes=[VM((len(PIECES), 2 * EXP * LINE, 2 * DPROWS), BF)],
+        compiler_params=params(16),
+        cost_estimate=cost(10**6, 2 * 10**6),
+        name="fill_key_terms",
+    )(keep, got)
+
+
+def near_kernel(place_ref, terms_ref, *refs):
+    *outs, total_ref = refs
+    total = jnp.sum(terms_ref[...].astype(F32), axis=0)
+    total_ref[...] = total.reshape(ZN, LINE, COLS)
     for rel in range(4):
-        at = lax.rem(place_ref[0] + rel, 4)
-        outs[rel][0] = (keep_ref[at].astype(F32) + got_ref[at].astype(F32)).astype(BF)
-
-
-HALF = DPROWS // 2
-
-
-def smem():
-    return pl.BlockSpec(memory_space=pltpu.SMEM)
+        for a in range(FAR):
+            outs[rel][a] = total_ref[4 * a + lax.rem(place_ref[0] + rel, 4)]
+
+
+def near_terms(place, terms):
+    return pl.pallas_call(
+        near_kernel,
+        in_specs=[smem(), vmem()],
+        out_specs=[vmem()] * 4,
+        out_shape=(jax.ShapeDtypeStruct((FAR, LINE, COLS), F32),) * 4,
+        scratch_shapes=[VM((ZN, LINE, COLS), F32)],
+        compiler_params=params(16),
+        cost_estimate=cost(10**6, 2 * 10**6),
+        name="near_terms",
+    )(place, terms)
+
+
+def far_kernel(place_ref, own_ref, up_ref, across_ref, down_ref, *outs):
+    for rel in range(FAR):
+        at = lax.rem(place_ref[0] + rel, FAR)
+        outs[rel][...] = own_ref[at] + up_ref[at] + (across_ref[at] + down_ref[at])
+
+
+def far_terms(place, *given):
+    return pl.pallas_call(
+        far_kernel,
+        in_specs=[smem()] + [vmem()] * 4,
+        out_specs=[vmem()] * 4,
+        out_shape=(jax.ShapeDtypeStruct((LINE, COLS), F32),) * 4,
+        compiler_params=params(16),
+        cost_estimate=cost(10**6, 10**6),
+        name="far_terms",
+    )(place, *given)
 
 
 def vmem():
     return pl.BlockSpec(memory_space=VM)
 
 
-def near(place, keep, got):
-    return pl.pallas_call(
-        near_kernel,
-        grid=(FAR,),
-        in_specs=[smem()] + [pl.BlockSpec((4, DPROWS, KC), lambda a: (a, 0, 0))] * 2,
-        out_specs=[pl.BlockSpec((1, DPROWS, KC), lambda a: (a, 0, 0))] * 4,
-        out_shape=(jax.ShapeDtypeStruct((FAR, DPROWS, KC), BF),) * 4,
-        compiler_params=params(24),
-        cost_estimate=cost(10**6, 5 * 10**6),
-        name="near_sums",
-    )(place, keep, got)
-
-
-def terms_kernel(own_ref, up_ref, across_ref, down_ref, out_ref):
-    size = DPROWS * TILES
-    to, fr = iota((size, size), 0), iota((size, size), 1)
-    inside = to % BLOCK
-    place = (inside // SUB) * DPROWS + (to // BLOCK) * SUB + inside % SUB
-    move = jnp.where(place == fr, 1.0, 0.0).astype(BF)
-    pieces = []
-    for a in range(FAR):
-        total = own_ref[a].astype(F32) + up_ref[a].astype(F32)
-        total = total + (across_ref[a].astype(F32) + down_ref[a].astype(F32))
-        total = total.astype(BF)
-        tall = [total[:, i * LANES : (i + 1) * LANES] for i in range(TILES)]
-        piece = dot(move, jnp.concatenate(tall, axis=0))
-        pieces.append(piece.reshape(EXP, BLOCK, LANES))
-    out_ref[...] = jnp.concatenate(pieces, axis=1).astype(BF)
-
-
-def near_terms(*given):
-    return pl.pallas_call(
-        terms_kernel,
-        in_specs=[vmem()] * 4,
-        out_specs=vmem(),
-        out_shape=jax.ShapeDtypeStruct((EXP, FAR * BLOCK, LANES), BF),
-        compiler_params=params(16),
-        cost_estimate=cost(10**8, 2 * 10**6),
-        name="near_terms",
-    )(*given)
-
-
-def far_kernel(terms_ref, out_ref):
-    out_ref[...] = jnp.sum(terms_ref[...].astype(F32), axis=0)
-
-
-def far_terms(terms):
-    return pl.pallas_call(
-        far_kernel,
-        in_specs=[vmem()],
-        out_specs=vmem(),
-        out_shape=jax.ShapeDtypeStruct((FAR * BLOCK, LANES), F32),
-        compiler_params=params(16),
-        cost_estimate=cost(10**6, 10**6),
-        name="far_terms",
-    )(terms)
-
-
-def adamw_kernel(terms_ref, weight_ref, first_ref, second_ref, *outs):
-    total = jnp.sum(terms_ref[...], axis=0)
+def adamw_kernel(own_ref, up_ref, across_ref, down_ref, weight_ref, first_ref, second_ref, *outs):
+    total = own_ref[...] + up_ref[...] + (across_ref[...] + down_ref[...])
+    total = [total[:, i * LANES : (i + 1) * LANES] for i in range(SPAN)]
+    total = jnp.concatenate(total, axis=0)
     grad = jnp.concatenate([total[i * SUB : (i + 1) * SUB] for i in range(TILES)], axis=1)
     for out, value in zip(outs, adamw(weight_ref[...], first_ref[...], second_ref[...], grad)):
         out[...] = value
@@ -361,7 +369,7 @@
 def update(*given):
     return pl.pallas_call(
         adamw_kernel,
-        in_specs=[vmem()] * 4,
+        in_specs=[vmem()] * 7,
         out_specs=[vmem()] * 3,
         out_shape=(jax.ShapeDtypeStruct((SUB, KC), F32),) * 3,
         compiler_params=params(16),
@@ -374,7 +382,8 @@
     weight = weight_ref[...]
     tall = jnp.concatenate([weight[:, i * LANES : (i + 1) * LANES] for i in range(TILES)], axis=0)
     to, fr = iota((EXP * ROOM, EXP), 0), iota((EXP * ROOM, EXP), 1)
-    spread = dot(jnp.where(to == fr * ROOM, 1.0, 0.0).astype(BF), dots_ref[...])
+    dots = jnp.concatenate([dots_ref[...], jnp.zeros((EXP, LANES - CAP), BF)], axis=1)
+    spread = dot(jnp.where(to == fr * ROOM, 1.0, 0.0).astype(BF), dots)
     spread = spread.reshape(EXP, ROOM, LANES)
     tall = jnp.broadcast_to(tall[None], (EXP, BLOCK, LANES))
     out_ref[...] = jnp.concatenate([tall, spread], axis=1).astype(BF)
@@ -416,14 +425,6 @@
     )(small)
 
 
-def along_z(step):
-    return [(i, ((i // CORES + step) % ZN) * CORES + i % CORES) for i in range(ZN * CORES)]
-
-
-def shift(x, step):
-    return lax.ppermute(x, "dp", along_z(step))
-
-
 def adamw(weight, first, second, grad):
     new_first = beta_one * first + (1.0 - beta_one) * grad
     new_second = beta_two * second + (1.0 - beta_two) * grad * grad
@@ -439,11 +440,9 @@
     return lax.all_to_all(x, "expert", split_axis=0, concat_axis=0, tiled=True)
 
 
-def exchange_far(x):
-    groups = [
-        [(4 * a + b) * CORES + c for a in range(FAR)] for b in range(4) for c in range(CORES)
-    ]
-    return lax.all_to_all(x, "dp", 0, 0, axis_index_groups=groups, tiled=True)
+def shift(x, step):
+    pairs = [(i, ((i // CORES + step) % ZN) * CORES + i % CORES) for i in range(ZN * CORES)]
+    return lax.ppermute(x, "dp", pairs)
 
 
 def swap_core(x):
@@ -464,26 +463,27 @@
 ):
     dp = lax.axis_index("dp")
     core, z = lax.rem(dp, CORES)[None], dp // CORES
-    near_place = lax.rem(z, 4)[None]
-    dots = jnp.pad(expert_dots, ((0, 0), (0, LANES - CAP)))
-    small, cot = lax.optimization_barrier((small_block(key_weight, dots), key_cot))
+    near_place, far_place = lax.rem(z, 4)[None], (z // 4)[None]
+    small, cot = lax.optimization_barrier((small_block(key_weight, expert_dots), key_cot))
     small = exchange(small)
     keep, send = partials(core, attn_input, cot)
-    got = swap_core(send)
-    packed = pack(jnp.swapaxes(expert_rows, 0, 1))
-    small, packed, keep, got = lax.optimization_barrier((small, packed, keep, got))
-    key_rows, packed, keep = lax.optimization_barrier((order_rows(small), packed, keep))
-    w = lax.all_gather(key_rows, "dp", axis=0, tiled=True)
+    terms = fill(keep, swap_core(send))
+    small, terms = lax.optimization_barrier((small, terms))
+    w = lax.all_gather(order_rows(small), "dp", axis=0, tiled=True)
+    terms, own_rows = lax.optimization_barrier((terms, expert_rows))
+    terms = exchange(terms)
+    packed = pack(jnp.swapaxes(own_rows, 0, 1))
+    terms, packed = lax.optimization_barrier((terms, packed))
     rows = exchange(packed)
-    own, up, across, down = near(near_place, keep, got)
-    terms = near_terms(own, shift(up, 1), shift(across, -2), shift(down, -1))
-    terms, rows = lax.optimization_barrier((terms, rows))
-    grads = far_terms(exchange(terms))
+    own, up, across, down = near_terms(near_place, terms)
+    own, up, across, down = far_terms(
+        far_place, own, shift(up, 1), shift(across, -2), shift(down, -1)
+    )
+    grads = own, shift(up, 4), shift(across, 8), shift(down, -4)
+    updated = update(*grads, key_weight, first_moment, second_moment)
     pick, rest, logit = gates(routing.T, router_base.T, small)
-    part = routed(pick, rest, logit, rows, router_weight.T)
-    grads = exchange_far(grads.reshape(FAR, BLOCK, LANES))
-    updated = update(grads, key_weight, first_moment, second_moment)
-    input_grad = final(part, key_cot, w)
+    rows, pick, updated = lax.optimization_barrier((rows, pick, updated))
+    input_grad = combine(pick, rest, logit, key_cot, rows, w, router_weight.T)
     return (input_grad, *updated)
 
 

time: 150 us -> 130 us (0.87); the launches traced: 148 us -> 129 us
  blocking collectives: 14.5 us -> 0 us
  local copies, waits for them, and re-layouts: 19.1 us -> 4.84 us
  starting transfers between devices: 45.1 us -> 55.8 us
  waiting for transfers between devices: 35.9 us -> 29.2 us
  Pallas kernels: 18.8 us -> 25.2 us
    ppermute x3 -> x6, waiting for transfers between devices: 29.8 us -> 6.25 us  [shift(): return lax.ppermute(x, 'dp', pairs)]
    all_to_all x2 -> x3, waiting for transfers between devices: 0.01 us -> 22.9 us  [exchange(): return lax.all_to_all(x, 'expert', split_axis=0, concat_axis=0, tiled=True)]
    ppermute x3 -> x6, starting transfers between devices: 15.9 us -> 32.5 us  [shift(): return lax.ppermute(x, 'dp', pairs)]
    all_to_all x1 -> x0, blocking collectives: 14.5 us -> none  [exchange(): return lax.all_to_all(x, 'expert', split_axis=0, concat_axis=0, tiled=True)]
    unnamed x40 -> x24, local copies, waits for them, and re-layouts: 18.4 us -> 4.84 us
    all_to_all x1 -> x0, starting transfers between devices: 11 us -> none  [exchange_far(): return lax.all_to_all(x, 'dp', 0, 0, axis_index_groups=groups, tiled=True)]
    all_to_all x1 -> x0, waiting for transfers between devices: 6.01 us -> none  [exchange_far(): return lax.all_to_all(x, 'dp', 0, 0, axis_index_groups=groups, tiled=True)]
    all_to_all x2 -> x3, starting transfers between devices: 16.2 us -> 21.4 us  [exchange(): return lax.all_to_all(x, 'expert', split_axis=0, concat_axis=0, tiled=True)]
  transfers between devices with their start and end apart: 8 -> 11, of which waited for: 4 -> 6; matrix products, arithmetic and copies ran while one was open for 0% -> 0% of each run, Pallas kernels for 8% -> 8%
where the time goes in v3:
time: 130 us; the launch traced here: 129 us
  starting transfers between devices  55.8 us (43%)
  waiting for transfers between devices  29.2 us (22%)
  Pallas kernels  25.2 us (19%)
  between operations  14.3 us (11%)
  local copies, waits for them, and re-layouts  4.84 us (4%)
    ppermute x6, starting transfers between devices, shift(): return lax.ppermute(x, 'dp', pairs)  32.5 us
    all_to_all x3, waiting for transfers between devices, exchange(): return lax.all_to_all(x, 'expert', split_axis=0, concat_axis=0, tiled=True)  22.9 us
    all_to_all x3, starting transfers between devices, exchange(): return lax.all_to_all(x, 'expert', split_axis=0, concat_axis=0, tiled=True)  21.4 us
    pallas_call x1, Pallas kernels, combine(): pl.pallas_call(combine_kernel, grid=(PARTS,), out_shape=jax.ShapeDtypeStr...  8.28 us
    ppermute x6, waiting for transfers between devices, shift(): return lax.ppermute(x, 'dp', pairs)  6.25 us
    pallas_call x1, Pallas kernels, pack(): pl.pallas_call(pack_kernel, out_shape=jax.ShapeDtypeStruct((EXP, ROWS, CO...  5.59 us
    unnamed x24, local copies, waits for them, and re-layouts  4.84 us
    pallas_call x1, Pallas kernels, partials(): pl.pallas_call(partial_kernel, grid_spec=pltpu.PrefetchScalarGridSpec(num...  4.24 us
  transfers between devices with their start and end apart: 11, of which 6 were waited for; matrix products, arithmetic and copies ran while one was open for 0% of the time, Pallas kernels for 8%

profile of v3, /device:TPU:24, one launch (start us, length us, event | category | flops | bytes accessed | tf_op | source)
XLA Modules:
  0.0 129.2 jit_solution(10842968559998010534)
XLA Ops:
  7.2 0.0 copy-start.4
  7.2 0.7 copy-done.4
  7.9 0.7 copy-done.10
  8.6 0.8 small_block.1
  9.4 1.1 copy-done
  10.5 0.9 copy-done.1
  11.4 4.2 %key_partials.1 = (bf16[16,96,512]{2,1,0:T(8,128)(2,1)S(1)}, bf16[16,96,512]{2,1,0:T(8,128)(2,1)}) custom-call(s32[1]{0:T(128)} %bitcast.core_ref, bf16[128,3072]{1,0:T(8,128)(2,1)S(1)} %copy-done, bf16[128,512]{1,0:T(8,128)(2,1)S(1)} %copy-done.1), custom_call_target="tpu_custom_call" | custom-call | flops 4026531 | bytes 50000 | tf_op jit(solution)/shard_map/key_partials/pallas_call | solution.py:252
  15.6 1.9 %collective-permute-start = (bf16[16,96,512]{2,1,0:T(8,128)(2,1)}, bf16[16,96,512]{2,1,0:T(8,128)(2,1)S(1)}, u32[]{:S(2)}, u32[]{:S(2)}) collective-permute-start(bf16[16,96,512]{2,1,0:T(8,128)(2,1)} %get-tuple-element.36), channel_id=1, source_target_pairs={{0,16},{16,0},{32,48},{48,32},{64,80},{80,64},{96,112},{112,96},{1... | collective-permute-start | bytes 4718600 | tf_op jit(solution)/shard_map/ppermute | solution.py:449
  17.6 9.0 %all-to-all-start = ((bf16[16,32,128]{2,1,0:T(8,128)(2,1)}), bf16[16,32,128]{2,1,0:T(8,128)(2,1)S(1)}, u32[]{:S(2)}, u32[]{:S(2)}) async-start(bf16[16,32,128]{2,1,0:T(8,128)(2,1)} %small_block.1), calls=%async_computation | async-start | bytes 262144 | tf_op jit(solution)/shard_map/all_to_all | solution.py:440
  26.5 0.0 all-gather.2.cloned.1.call-start
  26.6 0.0 collective-permute-done.got_ref
  26.6 3.7 %fill_key_terms.1 = bf16[16,128,384]{2,1,0:T(8,128)(2,1)} custom-call(bf16[16,96,512]{2,1,0:T(8,128)(2,1)S(1)} %get-tuple-element.35.keep_ref, bf16[16,96,512]{2,1,0:T(8,128)(2,1)S(1)} %collective-permute-done.got_ref), custom_call_target="tpu_custom_call" | custom-call | flops 10000 | bytes 20000 | tf_op jit(solution)/shard_map/fill_key_terms/pallas_call | solution.py:303
  30.3 2.2 %all-to-all-done.dots_ref.small_ref = bf16[16,32,128]{2,1,0:T(8,128)(2,1)S(1)} async-done(((bf16[16,32,128]{2,1,0:T(8,128)(2,1)}), bf16[16,32,128]{2,1,0:T(8,128)(2,1)S(1)}, u32[]{:S(2)}, u32[]{:S(2)}) %all-to-all-start) | async-done | bytes 131104 | tf_op jit(solution)/shard_map/all_to_all | solution.py:440
  32.5 1.0 order_key_rows.1
  33.4 0.0 all-gather.2.cloned.1.call-update
  33.4 6.0 %all-to-all-start.1 = ((bf16[16,128,384]{2,1,0:T(8,128)(2,1)}), bf16[16,128,384]{2,1,0:T(8,128)(2,1)S(1)}, u32[]{:S(2)}, u32[]{:S(2)}) async-start(bf16[16,128,384]{2,1,0:T(8,128)(2,1)} %fill_key_terms.1), calls=%async_computation.1 | async-start | bytes 3145728 | tf_op jit(solution)/shard_map/all_to_all | solution.py:440
  39.4 5.6 %pack_rows.1 = bf16[16,272,384]{2,1,0:T(8,128)(2,1)} custom-call(bf16[34,16,3072]{2,1,0:T(8,128)(2,1)} %bitcast.9), custom_call_target="tpu_custom_call" | custom-call | flops 16106127 | bytes 66846 | tf_op jit(solution)/shard_map/pack_rows/pallas_call | solution.py:109
  45.0 16.9 %all-to-all-done.1.terms_ref = bf16[16,128,384]{2,1,0:T(8,128)(2,1)S(1)} async-done(((bf16[16,128,384]{2,1,0:T(8,128)(2,1)}), bf16[16,128,384]{2,1,0:T(8,128)(2,1)S(1)}, u32[]{:S(2)}, u32[]{:S(2)}) %all-to-all-start.1) | async-done | bytes 1572896 | tf_op jit(solution)/shard_map/all_to_all | solution.py:440
  61.9 6.4 %all-to-all-start.2 = ((bf16[16,272,384]{2,1,0:T(8,128)(2,1)}), bf16[16,272,384]{2,1,0:T(8,128)(2,1)}, u32[]{:S(2)}, u32[]{:S(2)}) async-start(bf16[16,272,384]{2,1,0:T(8,128)(2,1)} %pack_rows.1), calls=%async_computation.2 | async-start | bytes 6684672 | tf_op jit(solution)/shard_map/all_to_all | solution.py:440
  68.4 0.0 copy-start.11
  68.4 0.0 copy-start.5
  68.4 0.0 copy-start.6
  68.4 0.0 copy-start.7
  68.4 0.3 near_terms.1
  68.7 1.9 %collective-permute-start.1 = (f32[4,8,384]{2,1,0:T(8,128)S(1)}, f32[4,8,384]{2,1,0:T(8,128)S(1)}, u32[]{:S(2)}, u32[]{:S(2)}) collective-permute-start(f32[4,8,384]{2,1,0:T(8,128)S(1)} %get-tuple-element.45), channel_id=1, source_target_pairs={{0,32},{16,48},{32,64},{48,80},{64,96},{80,112},{96,128},{112,144}... | collective-permute-start | bytes 147464 | tf_op jit(solution)/shard_map/ppermute | solution.py:445
  70.7 10.5 %collective-permute-start.2 = (f32[4,8,384]{2,1,0:T(8,128)S(1)}, f32[4,8,384]{2,1,0:T(8,128)S(1)}, u32[]{:S(2)}, u32[]{:S(2)}) collective-permute-start(f32[4,8,384]{2,1,0:T(8,128)S(1)} %get-tuple-element.46), channel_id=1, source_target_pairs={{0,448},{16,464},{32,480},{48,496},{64,0},{80,16},{96,32},{112,48}... | collective-permute-start | bytes 147464 | tf_op jit(solution)/shard_map/ppermute | solution.py:445
  81.2 2.9 %collective-permute-start.3 = (f32[4,8,384]{2,1,0:T(8,128)S(1)}, f32[4,8,384]{2,1,0:T(8,128)S(1)}, u32[]{:S(2)}, u32[]{:S(2)}) collective-permute-start(f32[4,8,384]{2,1,0:T(8,128)S(1)} %get-tuple-element.47), channel_id=1, source_target_pairs={{0,480},{16,496},{32,0},{48,16},{64,32},{80,48},{96,64},{112,80},{... | collective-permute-start | bytes 147464 | tf_op jit(solution)/shard_map/ppermute | solution.py:445
  84.1 0.0 collective-permute-done.1.up_ref
  84.1 0.1 collective-permute-done.2.across_ref
  84.2 3.0 %collective-permute-done.3.down_ref = f32[4,8,384]{2,1,0:T(8,128)S(1)} collective-permute-done((f32[4,8,384]{2,1,0:T(8,128)S(1)}, f32[4,8,384]{2,1,0:T(8,128)S(1)}, u32[]{:S(2)}, u32[]{:S(2)}) %collective-permute-start.3) | collective-permute-done | bytes 49184 | tf_op jit(solution)/shard_map/ppermute | solution.py:445
  87.2 1.9 %collective-permute-start.4 = (f32[8,384]{1,0:T(8,128)S(1)}, f32[8,384]{1,0:T(8,128)S(1)}, u32[]{:S(2)}, u32[]{:S(2)}) collective-permute-start(f32[8,384]{1,0:T(8,128)S(1)} %get-tuple-element.49), channel_id=1, source_target_pairs={{0,128},{16,144},{32,160},{48,176},{64,192},{80,208},{96,224},{112... | collective-permute-start | bytes 36872 | tf_op jit(solution)/shard_map/ppermute | solution.py:445
  89.1 11.1 %collective-permute-start.5 = (f32[8,384]{1,0:T(8,128)S(1)}, f32[8,384]{1,0:T(8,128)S(1)}, u32[]{:S(2)}, u32[]{:S(2)}) collective-permute-start(f32[8,384]{1,0:T(8,128)S(1)} %get-tuple-element.50), channel_id=1, source_target_pairs={{0,256},{16,272},{32,288},{48,304},{64,320},{80,336},{96,352},{112... | collective-permute-start | bytes 36872 | tf_op jit(solution)/shard_map/ppermute | solution.py:445
  100.2 4.2 %collective-permute-start.6 = (f32[8,384]{1,0:T(8,128)S(1)}, f32[8,384]{1,0:T(8,128)S(1)}, u32[]{:S(2)}, u32[]{:S(2)}) collective-permute-start(f32[8,384]{1,0:T(8,128)S(1)} %get-tuple-element.51), channel_id=1, source_target_pairs={{0,384},{16,400},{32,416},{48,432},{64,448},{80,464},{96,480},{112... | collective-permute-start | bytes 36872 | tf_op jit(solution)/shard_map/ppermute | solution.py:445
  104.4 0.0 copy-done.9
  104.4 0.0 copy-done.11
  104.4 0.7 gates.1
  105.1 0.7 copy-done.2
  105.8 0.7 copy-done.3
  106.5 0.0 collective-permute-done.4.up_ref
  106.5 0.0 collective-permute-done.5.across_ref
  106.5 3.2 %collective-permute-done.6.down_ref = f32[8,384]{1,0:T(8,128)S(1)} collective-permute-done((f32[8,384]{1,0:T(8,128)S(1)}, f32[8,384]{1,0:T(8,128)S(1)}, u32[]{:S(2)}, u32[]{:S(2)}) %collective-permute-start.6) | collective-permute-done | bytes 12320 | tf_op jit(solution)/shard_map/ppermute | solution.py:445
  109.7 0.0 copy-done.5
  109.7 0.0 copy-done.6
  109.7 0.0 copy-done.7
  109.7 0.6 adamw.1
  110.3 3.8 %all-to-all-done.2.head_ref.tail_ref = bf16[16,272,384]{2,1,0:T(8,128)(2,1)} async-done(((bf16[16,272,384]{2,1,0:T(8,128)(2,1)}), bf16[16,272,384]{2,1,0:T(8,128)(2,1)}, u32[]{:S(2)}, u32[]{:S(2)}) %all-to-all-start.2) | async-done | bytes 3342368 | tf_op jit(solution)/shard_map/all_to_all | solution.py:440
  114.1 0.0 copy-done.8
  114.1 8.3 %combine.1 = bf16[128,3072]{1,0:T(8,128)(2,1)} custom-call(bf16[256,512]{1,0:T(8,128)(2,1)} %copy-done.2, bf16[256,256]{1,0:T(8,128)(2,1)} %copy-done.3, bf16[48,128]{1,0:T(8,128)(2,1)} %copy-done.8, bf16[128,512]{1,0:T(8,128)(2,1)} %cot_ref.2, bf16[16,272,384]{2,1,0:T(8,128)(2,1)} %all-to-all-done.2.head_ref.tail_ref, ...), custom_call_target="tpu_custom_call" | custom-call | flops 20000000 | bytes 80000 | tf_op jit(solution)/shard_map/combine/pallas_call | solution.py:218
  (9 shorter events, 0.0 us)
Async XLA Ops:
  7.2 0.7 copy-start.4
  7.9 0.7 copy-start.10
  9.4 1.1 copy-start
  10.5 0.9 copy-start.1
  15.6 10.9 %collective-permute-start = (bf16[16,96,512]{2,1,0:T(8,128)(2,1)}, bf16[16,96,512]{2,1,0:T(8,128)(2,1)S(1)}, u32[]{:S(2)}, u32[]{:S(2)}) collective-permute-start(bf16[16,96,512]{2,1,0:T(8,128)(2,1)} %get-tuple-element.36), channel_id=1, source_target_pairs={{0,16},{16,0},{32,48},{48,32},{64,80},{80,64},{96,112},{112,96},{1... | collective-permute-start | bytes 4718600 | tf_op jit(solution)/shard_map/ppermute | solution.py:449
  17.6 14.9 %all-to-all-start = ((bf16[16,32,128]{2,1,0:T(8,128)(2,1)}), bf16[16,32,128]{2,1,0:T(8,128)(2,1)S(1)}, u32[]{:S(2)}, u32[]{:S(2)}) async-start(bf16[16,32,128]{2,1,0:T(8,128)(2,1)} %small_block.1), calls=%async_computation | async-start | bytes 262144 | tf_op jit(solution)/shard_map/all_to_all | solution.py:440
  26.5 87.6 %all-gather.2.cloned.1.call-start = ((), (), s32[]{:S(2)}) async-start(), calls=%async_computation.3 | async-start | bytes 3244032 | tf_op jit(solution)/shard_map/all_gather | solution.py:472
  33.4 28.5 %all-to-all-start.1 = ((bf16[16,128,384]{2,1,0:T(8,128)(2,1)}), bf16[16,128,384]{2,1,0:T(8,128)(2,1)S(1)}, u32[]{:S(2)}, u32[]{:S(2)}) async-start(bf16[16,128,384]{2,1,0:T(8,128)(2,1)} %fill_key_terms.1), calls=%async_computation.1 | async-start | bytes 3145728 | tf_op jit(solution)/shard_map/all_to_all | solution.py:440
  61.9 52.2 %all-to-all-start.2 = ((bf16[16,272,384]{2,1,0:T(8,128)(2,1)}), bf16[16,272,384]{2,1,0:T(8,128)(2,1)}, u32[]{:S(2)}, u32[]{:S(2)}) async-start(bf16[16,272,384]{2,1,0:T(8,128)(2,1)} %pack_rows.1), calls=%async_computation.2 | async-start | bytes 6684672 | tf_op jit(solution)/shard_map/all_to_all | solution.py:440
  68.3 36.0 %copy-start.9 = (f32[128,16]{0,1:T(8,128)S(1)}, f32[128,16]{0,1:T(8,128)}, u32[]{:S(2)}) copy-start(f32[128,16]{0,1:T(8,128)} %param.13) | copy-start | bytes 24580
  68.4 36.0 %copy-start.11 = (s32[128,4]{0,1:T(4,128)S(1)}, s32[128,4]{0,1:T(4,128)}, u32[]{:S(2)}) copy-start(s32[128,4]{0,1:T(4,128)} %param.12) | copy-start | bytes 6148
  68.4 41.3 %copy-start.5 = (f32[6,512]{1,0:T(8,128)S(1)}, f32[6,512]{1,0:T(8,128)}, u32[]{:S(2)}) copy-start(f32[6,512]{1,0:T(8,128)} %weight_ref.3) | copy-start | bytes 36868
  68.4 41.3 %copy-start.6 = (f32[6,512]{1,0:T(8,128)S(1)}, f32[6,512]{1,0:T(8,128)}, u32[]{:S(2)}) copy-start(f32[6,512]{1,0:T(8,128)} %first_ref.1) | copy-start | bytes 36868
  68.4 41.3 %copy-start.7 = (f32[6,512]{1,0:T(8,128)S(1)}, f32[6,512]{1,0:T(8,128)}, u32[]{:S(2)}) copy-start(f32[6,512]{1,0:T(8,128)} %second_ref.1) | copy-start | bytes 36868
  68.7 15.3 %collective-permute-start.1 = (f32[4,8,384]{2,1,0:T(8,128)S(1)}, f32[4,8,384]{2,1,0:T(8,128)S(1)}, u32[]{:S(2)}, u32[]{:S(2)}) collective-permute-start(f32[4,8,384]{2,1,0:T(8,128)S(1)} %get-tuple-element.45), channel_id=1, source_target_pairs={{0,32},{16,48},{32,64},{48,80},{64,96},{80,112},{96,128},{112,144}... | collective-permute-start | bytes 147464 | tf_op jit(solution)/shard_map/ppermute | solution.py:445
  70.7 13.5 %collective-permute-start.2 = (f32[4,8,384]{2,1,0:T(8,128)S(1)}, f32[4,8,384]{2,1,0:T(8,128)S(1)}, u32[]{:S(2)}, u32[]{:S(2)}) collective-permute-start(f32[4,8,384]{2,1,0:T(8,128)S(1)} %get-tuple-element.46), channel_id=1, source_target_pairs={{0,448},{16,464},{32,480},{48,496},{64,0},{80,16},{96,32},{112,48}... | collective-permute-start | bytes 147464 | tf_op jit(solution)/shard_map/ppermute | solution.py:445
  81.2 6.0 %collective-permute-start.3 = (f32[4,8,384]{2,1,0:T(8,128)S(1)}, f32[4,8,384]{2,1,0:T(8,128)S(1)}, u32[]{:S(2)}, u32[]{:S(2)}) collective-permute-start(f32[4,8,384]{2,1,0:T(8,128)S(1)} %get-tuple-element.47), channel_id=1, source_target_pairs={{0,480},{16,496},{32,0},{48,16},{64,32},{80,48},{96,64},{112,80},{... | collective-permute-start | bytes 147464 | tf_op jit(solution)/shard_map/ppermute | solution.py:445
  87.2 19.3 %collective-permute-start.4 = (f32[8,384]{1,0:T(8,128)S(1)}, f32[8,384]{1,0:T(8,128)S(1)}, u32[]{:S(2)}, u32[]{:S(2)}) collective-permute-start(f32[8,384]{1,0:T(8,128)S(1)} %get-tuple-element.49), channel_id=1, source_target_pairs={{0,128},{16,144},{32,160},{48,176},{64,192},{80,208},{96,224},{112... | collective-permute-start | bytes 36872 | tf_op jit(solution)/shard_map/ppermute | solution.py:445
  89.1 17.4 %collective-permute-start.5 = (f32[8,384]{1,0:T(8,128)S(1)}, f32[8,384]{1,0:T(8,128)S(1)}, u32[]{:S(2)}, u32[]{:S(2)}) collective-permute-start(f32[8,384]{1,0:T(8,128)S(1)} %get-tuple-element.50), channel_id=1, source_target_pairs={{0,256},{16,272},{32,288},{48,304},{64,320},{80,336},{96,352},{112... | collective-permute-start | bytes 36872 | tf_op jit(solution)/shard_map/ppermute | solution.py:445
  100.2 9.5 %collective-permute-start.6 = (f32[8,384]{1,0:T(8,128)S(1)}, f32[8,384]{1,0:T(8,128)S(1)}, u32[]{:S(2)}, u32[]{:S(2)}) collective-permute-start(f32[8,384]{1,0:T(8,128)S(1)} %get-tuple-element.51), channel_id=1, source_target_pairs={{0,384},{16,400},{32,416},{48,432},{64,448},{80,464},{96,480},{112... | collective-permute-start | bytes 36872 | tf_op jit(solution)/shard_map/ppermute | solution.py:445
  105.1 0.7 copy-start.2
  105.8 0.7 copy-start.3
  106.5 7.7 %copy-start.8 = (bf16[48,128]{1,0:T(8,128)(2,1)}, bf16[48,128]{1,0:T(8,128)(2,1)S(1)}, u32[]{:S(2)}) copy-start(bf16[48,128]{1,0:T(8,128)(2,1)S(1)} %get-tuple-element.57.logit_ref) | copy-start | bytes 36868
Sparse Core Ops, SparseCore 0:
  33.6 74.2 all-gather.1

commit v4 on v3

--- a/solution.py
+++ b/solution.py
@@ -197,74 +197,48 @@
     )(routing, base, small)
 
 
+STEP = 2
+
+
 def combine_kernel(
     pick_ref, rest_ref, logit_ref, cot_ref, head_ref, tail_ref, w_ref, router_ref, out_ref
 ):
-    q = pl.program_id(0)
     rests = EXP * PER
     piece = (iota((2 * TOK, rests), 1) % PER) // REST
-    rest = jnp.where(piece == q, rest_ref[...].astype(F32), 0.0).astype(BF)
-    mixed = dot(pick_ref[...], head_ref[...].reshape(EXP * HEAD, COLS))
-    mixed = mixed + dot(rest, tail_ref[...].reshape(rests, COLS))
-    total = mixed[:TOK] + mixed[TOK:]
-    router = router_ref[...]
-    total = total + dot(logit_ref[...], jnp.concatenate([router] * 3, axis=0), 0, 0)
-    total = total + dot(cot_ref[...], w_ref[...], 1, 1)
-    out_ref[...] = total.astype(BF)
+    picked = rest_ref[...].astype(F32)
+    tail = tail_ref[...].reshape(rests, COLS)
+    router = jnp.concatenate([router_ref[...]] * 3, axis=0)
+    total = dot(cot_ref[...], w_ref[...], 1, 1) + dot(logit_ref[...], router, 0, 0)
+    for i in range(STEP):
+        q = pl.program_id(0) * STEP + i
+        rest = jnp.where(piece == q, picked, 0.0).astype(BF)
+        head = head_ref[:, i * HEAD : (i + 1) * HEAD, :].reshape(EXP * HEAD, COLS)
+        mixed = dot(pick_ref[...], head) + dot(rest, tail)
+        at = slice(i * COLS, (i + 1) * COLS)
+        out_ref[:, at] = (total[:, at] + mixed[:TOK] + mixed[TOK:]).astype(BF)
 
 
 def combine(pick, rest, logit, cot, rows, w, router):
-    heads, rests = EXP * HEAD, EXP * PER
+    heads, rests, wide = EXP * HEAD, EXP * PER, STEP * COLS
     return pl.pallas_call(
         combine_kernel,
-        grid=(PARTS,),
+        grid=(PARTS // STEP,),
         out_shape=jax.ShapeDtypeStruct((TOK, D), BF),
         in_specs=[
             full(2 * TOK, heads),
             full(2 * TOK, rests),
             full(3 * EXP, TOK),
             full(TOK, KC),
-            pl.BlockSpec((EXP, HEAD, COLS), lambda q: (0, q, 0)),
+            pl.BlockSpec((EXP, STEP * HEAD, COLS), lambda q: (0, q, 0)),
             pl.BlockSpec((EXP, PER, COLS), lambda q: (0, PARTS * HEAD // PER, 0)),
-            pl.BlockSpec((COLS, KC), lambda q: (q, 0)),
-            pl.BlockSpec((EXP, COLS), lambda q: (0, q)),
+            pl.BlockSpec((wide, KC), lambda q: (q, 0)),
+            pl.BlockSpec((EXP, wide), lambda q: (0, q)),
         ],
-        out_specs=pl.BlockSpec((TOK, COLS), lambda q: (0, q)),
+        out_specs=pl.BlockSpec((TOK, wide), lambda q: (0, q)),
         compiler_params=params(BIG),
         cost_estimate=cost(2 * 10**9, 8 * 10**6),
         name="combine",
     )(pick, rest, logit, cot, rows, rows, w, router)
-
-
-def partial_kernel(core_ref, attn_ref, cot_ref, keep_ref, send_ref):
-    first = core_ref[0] == 0
-    grad = dot(attn_ref[...], cot_ref[...], 0, 0)
-    for i in range(2):
-        zero = grad[(2 * i) * DPROWS : (2 * i + 1) * DPROWS]
-        one = grad[(2 * i + 1) * DPROWS : (2 * i + 2) * DPROWS]
-        keep_ref[i] = jnp.where(first, zero, one).astype(BF)
-        send_ref[i] = jnp.where(first, one, zero).astype(BF)
-
-
-def partials(core, attn, cot):
-    wide = 2 * CORES * DPROWS
-    shape = jax.ShapeDtypeStruct((ZN, DPROWS, KC), BF)
-    return pl.pallas_call(
-        partial_kernel,
-        grid_spec=pltpu.PrefetchScalarGridSpec(
-            num_scalar_prefetch=1,
-            grid=(ZN // 2,),
-            in_specs=[
-                pl.BlockSpec((TOK, wide), lambda i, c: (0, i)),
-                pl.BlockSpec((TOK, KC), lambda i, c: (0, 0)),
-            ],
-            out_specs=[pl.BlockSpec((2, DPROWS, KC), lambda i, c: (i, 0, 0))] * 2,
-        ),
-        out_shape=(shape, shape),
-        compiler_params=params(16),
-        cost_estimate=cost(2 * TOK * D * KC, 5 * 10**6),
-        name="key_partials",
-    )(core, attn, cot)
 
 
 PIECES = [
@@ -275,7 +249,7 @@
 ]
 
 
-def fill_kernel(keep_ref, got_ref, out_ref, moves):
+def terms_kernel(core_ref, attn_ref, attn2_ref, cot_ref, cot2_ref, out_ref, moves):
     tall, wide = 2 * EXP * LINE, 2 * DPROWS
 
     @pl.when(pl.program_id(0) == 0)
@@ -287,10 +261,17 @@
             hit = same & (tile * SUB + fr % SUB == span * LINE + line)
             moves[n] = jnp.where(hit, 1.0, 0.0).astype(BF)
 
+    first = core_ref[0] == 0
+    attn = jnp.concatenate([attn_ref[...], attn2_ref[...]], axis=0)
+    cot = jnp.concatenate([cot_ref[...], cot2_ref[...]], axis=0)
+    grad = dot(attn, cot, 0, 0)
     for i in range(2):
-        at = slice(2 * i, 2 * i + 2)
-        total = keep_ref[at].astype(F32) + got_ref[at].astype(F32)
-        total = total.reshape(wide, KC).astype(BF)
+        total = []
+        for j in (2 * i, 2 * i + 1):
+            zero = grad[2 * j * DPROWS : (2 * j + 1) * DPROWS]
+            one = grad[(2 * j + 1) * DPROWS : (2 * j + 2) * DPROWS]
+            total.append(jnp.where(first, zero, one))
+        total = jnp.concatenate(total, axis=0).astype(BF)
         spans = [jnp.zeros((tall, LANES), F32)] * SPAN
         for n, (tile, span) in enumerate(PIECES):
             spans[span] = spans[span] + dot(moves[n], total[:, tile * LANES : (tile + 1) * LANES])
@@ -298,19 +279,19 @@
         out_ref[:, i * 2 * LINE : (i + 1) * 2 * LINE, :] = out.reshape(EXP, 2 * LINE, COLS)
 
 
-def fill(keep, got):
-    block = pl.BlockSpec((4, DPROWS, KC), lambda i: (i, 0, 0))
-    return pl.pallas_call(
-        fill_kernel,
+def key_terms(core, attn, attn2, cot, cot2):
+    columns = pl.BlockSpec((TOK, 4 * CORES * DPROWS), lambda i: (0, i))
+    return pl.pallas_call(
+        terms_kernel,
         grid=(ZN // 4,),
         out_shape=jax.ShapeDtypeStruct((EXP, KEYS, COLS), BF),
-        in_specs=[block, block],
+        in_specs=[smem(), columns, columns, full(TOK, KC), full(TOK, KC)],
         out_specs=pl.BlockSpec((EXP, 4 * LINE, COLS), lambda i: (0, i, 0)),
         scratch_shapes=[VM((len(PIECES), 2 * EXP * LINE, 2 * DPROWS), BF)],
-        compiler_params=params(16),
+        compiler_params=params(BIG),
         cost_estimate=cost(10**6, 2 * 10**6),
-        name="fill_key_terms",
-    )(keep, got)
+        name="key_terms",
+    )(core, attn, attn2, cot, cot2)
 
 
 def near_kernel(place_ref, terms_ref, *refs):
@@ -395,7 +376,7 @@
         in_specs=[vmem()] * 2,
         out_specs=vmem(),
         out_shape=jax.ShapeDtypeStruct((EXP, BLOCK + ROOM, LANES), BF),
-        compiler_params=params(16),
+        compiler_params=params(BIG),
         cost_estimate=cost(10**6, 10**6),
         name="small_block",
     )(weight, dots)
@@ -464,10 +445,8 @@
     dp = lax.axis_index("dp")
     core, z = lax.rem(dp, CORES)[None], dp // CORES
     near_place, far_place = lax.rem(z, 4)[None], (z // 4)[None]
-    small, cot = lax.optimization_barrier((small_block(key_weight, expert_dots), key_cot))
-    small = exchange(small)
-    keep, send = partials(core, attn_input, cot)
-    terms = fill(keep, swap_core(send))
+    small = exchange(small_block(key_weight, expert_dots))
+    terms = key_terms(core, attn_input, swap_core(attn_input), key_cot, swap_core(key_cot))
     small, terms = lax.optimization_barrier((small, terms))
     w = lax.all_gather(order_rows(small), "dp", axis=0, tiled=True)
     terms, own_rows = lax.optimization_barrier((terms, expert_rows))

time: 130 us -> 126 us (0.969)
  starting transfers between devices: 55.8 us -> 60.1 us
  waiting for transfers between devices: 29.2 us -> 26.2 us
  Pallas kernels: 25.2 us -> 22.3 us
  local copies, waits for them, and re-layouts: 4.84 us -> 2.28 us
    pallas_call x3 -> x2, Pallas kernels: 16.2 us -> 12.7 us  [the longest x1 6.61 us: combine(): pl.pallas_call(combine_kernel, grid=(PARTS // STEP,), out_shape=jax.Shape...]
    all_to_all x3, waiting for transfers between devices: 22.9 us -> 20.2 us  [exchange(): return lax.all_to_all(x, 'expert', split_axis=0, concat_axis=0, tiled=True)]
    unnamed x24 -> x20, local copies, waits for them, and re-layouts: 4.84 us -> 2.28 us
    ppermute x1 -> x2, starting transfers between devices: 1.91 us -> 4.33 us  [swap_core(): return lax.ppermute(x, 'dp', [(i, i ^ 1) for i in range(ZN * CORES)])]
  transfers between devices with their start and end apart: 11 -> 12, of which waited for: 6 -> 4; matrix products, arithmetic and copies ran while one was open for 0% -> 0% of each run, Pallas kernels for 8% -> 12%
where the time goes in v4:
time: 126 us; the launch traced here: 125 us
  starting transfers between devices  60.1 us (48%)
  waiting for transfers between devices  26.2 us (21%)
  Pallas kernels  22.3 us (18%)
  between operations  14.3 us (11%)
  local copies, waits for them, and re-layouts  2.28 us (2%)
    ppermute x6, starting transfers between devices, shift(): return lax.ppermute(x, 'dp', pairs)  33.1 us
    all_to_all x3, starting transfers between devices, exchange(): return lax.all_to_all(x, 'expert', split_axis=0, concat_axis=0, tiled=True)  22.7 us
    all_to_all x3, waiting for transfers between devices, exchange(): return lax.all_to_all(x, 'expert', split_axis=0, concat_axis=0, tiled=True)  20.2 us
    pallas_call x1, Pallas kernels, combine(): pl.pallas_call(combine_kernel, grid=(PARTS // STEP,), out_shape=jax.Shape...  6.61 us
    pallas_call x1, Pallas kernels, key_terms(): pl.pallas_call(terms_kernel, grid=(ZN // 4,), out_shape=jax.ShapeDtypeStr...  6.04 us
    ppermute x6, waiting for transfers between devices, shift(): return lax.ppermute(x, 'dp', pairs)  6.01 us
    pallas_call x1, Pallas kernels, pack(): pl.pallas_call(pack_kernel, out_shape=jax.ShapeDtypeStruct((EXP, ROWS, CO...  5.54 us
    ppermute x2, starting transfers between devices, swap_core(): return lax.ppermute(x, 'dp', [(i, i ^ 1) for i in range(ZN * CORES)])  4.33 us
  transfers between devices with their start and end apart: 12, of which 4 were waited for; matrix products, arithmetic and copies ran while one was open for 0% of the time, Pallas kernels for 12%

profile of v4, /device:TPU:24, one launch (start us, length us, event | category | flops | bytes accessed | tf_op | source)
XLA Modules:
  0.0 125.3 jit_solution(5733230955524160157)
XLA Ops:
  7.2 1.9 %collective-permute-start = (bf16[128,3072]{1,0:T(8,128)(2,1)}, bf16[128,3072]{1,0:T(8,128)(2,1)S(1)}, u32[]{:S(2)}, u32[]{:S(2)}) collective-permute-start(bf16[128,3072]{1,0:T(8,128)(2,1)} %attn_ref.1), channel_id=1, source_target_pairs={{0,16},{16,0},{32,48},{48,32},{64,80},{80,64},{96,112},{112,96},{1... | collective-permute-start | bytes 2359304 | tf_op jit(solution)/shard_map/ppermute | solution.py:430
  9.1 2.4 %collective-permute-start.1 = (bf16[128,512]{1,0:T(8,128)(2,1)}, bf16[128,512]{1,0:T(8,128)(2,1)S(1)}, u32[]{:S(2)}, u32[]{:S(2)}) collective-permute-start(bf16[128,512]{1,0:T(8,128)(2,1)} %cot_ref.3), channel_id=1, source_target_pairs={{0,16},{16,0},{32,48},{48,32},{64,80},{80,64},{96,112},{112,96},{1... | collective-permute-start | bytes 393224 | tf_op jit(solution)/shard_map/ppermute | solution.py:430
  11.5 1.5 %small_block.1 = bf16[16,32,128]{2,1,0:T(8,128)(2,1)} custom-call(f32[6,512]{1,0:T(8,128)} %weight_ref.3, bf16[16,34]{1,0:T(8,128)(2,1)} %dots_ref.1), custom_call_target="tpu_custom_call" | custom-call | flops 10000 | bytes 10000 | tf_op jit(solution)/shard_map/small_block/pallas_call | solution.py:374
  13.0 9.0 %all-to-all-start = ((bf16[16,32,128]{2,1,0:T(8,128)(2,1)}), bf16[16,32,128]{2,1,0:T(8,128)(2,1)S(1)}, u32[]{:S(2)}, u32[]{:S(2)}) async-start(bf16[16,32,128]{2,1,0:T(8,128)(2,1)} %small_block.1), calls=%async_computation | async-start | bytes 262144 | tf_op jit(solution)/shard_map/all_to_all | solution.py:421
  22.0 0.0 all-gather.2.cloned.1.call-start
  22.0 0.0 collective-permute-done.1.cot2_ref
  22.1 0.0 copy-start.9
  22.1 0.0 collective-permute-done.attn2_ref
  22.1 0.0 copy-start.8
  22.1 0.6 copy-done.9
  22.7 0.3 copy-done.8
  23.0 6.0 %key_terms.1 = bf16[16,128,384]{2,1,0:T(8,128)(2,1)} custom-call(s32[1]{0:T(128)} %bitcast.core_ref, bf16[128,3072]{1,0:T(8,128)(2,1)} %attn_ref.1, bf16[128,3072]{1,0:T(8,128)(2,1)} %copy-done.8, bf16[128,512]{1,0:T(8,128)(2,1)} %cot_ref.3, bf16[128,512]{1,0:T(8,128)(2,1)} %copy-done.9), custom_call_target="tpu_custom_call" | custom-call | flops 10000 | bytes 20000 | tf_op jit(solution)/shard_map/key_terms/pallas_call | solution.py:284
  29.0 0.0 all-to-all-done.dots_ref.small_ref
  29.0 1.0 order_key_rows.1
  30.0 0.0 all-gather.2.cloned.1.call-update
  30.0 7.2 %all-to-all-start.1 = ((bf16[16,128,384]{2,1,0:T(8,128)(2,1)}), bf16[16,128,384]{2,1,0:T(8,128)(2,1)S(1)}, u32[]{:S(2)}, u32[]{:S(2)}) async-start(bf16[16,128,384]{2,1,0:T(8,128)(2,1)} %key_terms.1), calls=%async_computation.1 | async-start | bytes 3145728 | tf_op jit(solution)/shard_map/all_to_all | solution.py:421
  37.2 5.5 %pack_rows.1 = bf16[16,272,384]{2,1,0:T(8,128)(2,1)} custom-call(bf16[34,16,3072]{2,1,0:T(8,128)(2,1)} %bitcast.9), custom_call_target="tpu_custom_call" | custom-call | flops 16106127 | bytes 66846 | tf_op jit(solution)/shard_map/pack_rows/pallas_call | solution.py:109
  42.8 0.0 copy-start.6
  42.8 0.0 copy-start.7
  42.8 0.0 copy-start.2
  42.8 0.0 copy-start.3
  42.8 0.0 copy-start.4
  42.8 16.6 %all-to-all-done.1.terms_ref = bf16[16,128,384]{2,1,0:T(8,128)(2,1)S(1)} async-done(((bf16[16,128,384]{2,1,0:T(8,128)(2,1)}), bf16[16,128,384]{2,1,0:T(8,128)(2,1)S(1)}, u32[]{:S(2)}, u32[]{:S(2)}) %all-to-all-start.1) | async-done | bytes 1572896 | tf_op jit(solution)/shard_map/all_to_all | solution.py:421
  59.4 6.5 %all-to-all-start.2 = ((bf16[16,272,384]{2,1,0:T(8,128)(2,1)}), bf16[16,272,384]{2,1,0:T(8,128)(2,1)}, u32[]{:S(2)}, u32[]{:S(2)}) async-start(bf16[16,272,384]{2,1,0:T(8,128)(2,1)} %pack_rows.1), calls=%async_computation.2 | async-start | bytes 6684672 | tf_op jit(solution)/shard_map/all_to_all | solution.py:421
  65.9 0.3 near_terms.1
  66.2 1.9 %collective-permute-start.2 = (f32[4,8,384]{2,1,0:T(8,128)S(1)}, f32[4,8,384]{2,1,0:T(8,128)S(1)}, u32[]{:S(2)}, u32[]{:S(2)}) collective-permute-start(f32[4,8,384]{2,1,0:T(8,128)S(1)} %get-tuple-element.37), channel_id=1, source_target_pairs={{0,32},{16,48},{32,64},{48,80},{64,96},{80,112},{96,128},{112,144}... | collective-permute-start | bytes 147464 | tf_op jit(solution)/shard_map/ppermute | solution.py:426
  68.2 10.5 %collective-permute-start.3 = (f32[4,8,384]{2,1,0:T(8,128)S(1)}, f32[4,8,384]{2,1,0:T(8,128)S(1)}, u32[]{:S(2)}, u32[]{:S(2)}) collective-permute-start(f32[4,8,384]{2,1,0:T(8,128)S(1)} %get-tuple-element.38), channel_id=1, source_target_pairs={{0,448},{16,464},{32,480},{48,496},{64,0},{80,16},{96,32},{112,48}... | collective-permute-start | bytes 147464 | tf_op jit(solution)/shard_map/ppermute | solution.py:426
  78.7 2.9 %collective-permute-start.4 = (f32[4,8,384]{2,1,0:T(8,128)S(1)}, f32[4,8,384]{2,1,0:T(8,128)S(1)}, u32[]{:S(2)}, u32[]{:S(2)}) collective-permute-start(f32[4,8,384]{2,1,0:T(8,128)S(1)} %get-tuple-element.39), channel_id=1, source_target_pairs={{0,480},{16,496},{32,0},{48,16},{64,32},{80,48},{96,64},{112,80},{... | collective-permute-start | bytes 147464 | tf_op jit(solution)/shard_map/ppermute | solution.py:426
  81.7 0.0 collective-permute-done.2.up_ref
  81.7 0.0 collective-permute-done.3.across_ref
  81.7 3.0 %collective-permute-done.4.down_ref = f32[4,8,384]{2,1,0:T(8,128)S(1)} collective-permute-done((f32[4,8,384]{2,1,0:T(8,128)S(1)}, f32[4,8,384]{2,1,0:T(8,128)S(1)}, u32[]{:S(2)}, u32[]{:S(2)}) %collective-permute-start.4) | collective-permute-done | bytes 49184 | tf_op jit(solution)/shard_map/ppermute | solution.py:426
  84.7 1.9 %collective-permute-start.5 = (f32[8,384]{1,0:T(8,128)S(1)}, f32[8,384]{1,0:T(8,128)S(1)}, u32[]{:S(2)}, u32[]{:S(2)}) collective-permute-start(f32[8,384]{1,0:T(8,128)S(1)} %get-tuple-element.41), channel_id=1, source_target_pairs={{0,128},{16,144},{32,160},{48,176},{64,192},{80,208},{96,224},{112... | collective-permute-start | bytes 36872 | tf_op jit(solution)/shard_map/ppermute | solution.py:426
  86.6 11.3 %collective-permute-start.6 = (f32[8,384]{1,0:T(8,128)S(1)}, f32[8,384]{1,0:T(8,128)S(1)}, u32[]{:S(2)}, u32[]{:S(2)}) collective-permute-start(f32[8,384]{1,0:T(8,128)S(1)} %get-tuple-element.42), channel_id=1, source_target_pairs={{0,256},{16,272},{32,288},{48,304},{64,320},{80,336},{96,352},{112... | collective-permute-start | bytes 36872 | tf_op jit(solution)/shard_map/ppermute | solution.py:426
  97.9 4.5 %collective-permute-start.7 = (f32[8,384]{1,0:T(8,128)S(1)}, f32[8,384]{1,0:T(8,128)S(1)}, u32[]{:S(2)}, u32[]{:S(2)}) collective-permute-start(f32[8,384]{1,0:T(8,128)S(1)} %get-tuple-element.43), channel_id=1, source_target_pairs={{0,384},{16,400},{32,416},{48,432},{64,448},{80,464},{96,480},{112... | collective-permute-start | bytes 36872 | tf_op jit(solution)/shard_map/ppermute | solution.py:426
  102.4 0.0 copy-done.6
  102.4 0.0 copy-done.7
  102.4 0.7 gates.1
  103.2 0.7 copy-done
  103.9 0.7 copy-done.1
  104.5 0.0 collective-permute-done.5.up_ref
  104.5 0.0 collective-permute-done.6.across_ref
  104.5 3.0 %collective-permute-done.7.down_ref = f32[8,384]{1,0:T(8,128)S(1)} collective-permute-done((f32[8,384]{1,0:T(8,128)S(1)}, f32[8,384]{1,0:T(8,128)S(1)}, u32[]{:S(2)}, u32[]{:S(2)}) %collective-permute-start.7) | collective-permute-done | bytes 12320 | tf_op jit(solution)/shard_map/ppermute | solution.py:426
  107.5 0.0 copy-done.2
  107.5 0.0 copy-done.3
  107.5 0.0 copy-done.4
  107.5 0.6 adamw.1
  108.2 3.6 %all-to-all-done.2.head_ref.tail_ref = bf16[16,272,384]{2,1,0:T(8,128)(2,1)} async-done(((bf16[16,272,384]{2,1,0:T(8,128)(2,1)}), bf16[16,272,384]{2,1,0:T(8,128)(2,1)}, u32[]{:S(2)}, u32[]{:S(2)}) %all-to-all-start.2) | async-done | bytes 3342368 | tf_op jit(solution)/shard_map/all_to_all | solution.py:421
  111.8 6.6 %combine.1 = bf16[128,3072]{1,0:T(8,128)(2,1)} custom-call(bf16[256,512]{1,0:T(8,128)(2,1)} %copy-done, bf16[256,256]{1,0:T(8,128)(2,1)} %copy-done.1, bf16[48,128]{1,0:T(8,128)(2,1)} %copy-done.5, bf16[128,512]{1,0:T(8,128)(2,1)} %cot_ref.3, bf16[16,272,384]{2,1,0:T(8,128)(2,1)} %all-to-all-done.2.head_ref.tail_ref, ...), custom_call_target="tpu_custom_call" | custom-call | flops 20000000 | bytes 80000 | tf_op jit(solution)/shard_map/combine/pallas_call | solution.py:223
  (6 shorter events, 0.0 us)
Async XLA Ops:
  7.2 14.9 %collective-permute-start = (bf16[128,3072]{1,0:T(8,128)(2,1)}, bf16[128,3072]{1,0:T(8,128)(2,1)S(1)}, u32[]{:S(2)}, u32[]{:S(2)}) collective-permute-start(bf16[128,3072]{1,0:T(8,128)(2,1)} %attn_ref.1), channel_id=1, source_target_pairs={{0,16},{16,0},{32,48},{48,32},{64,80},{80,64},{96,112},{112,96},{1... | collective-permute-start | bytes 2359304 | tf_op jit(solution)/shard_map/ppermute | solution.py:430
  9.1 13.0 %collective-permute-start.1 = (bf16[128,512]{1,0:T(8,128)(2,1)}, bf16[128,512]{1,0:T(8,128)(2,1)S(1)}, u32[]{:S(2)}, u32[]{:S(2)}) collective-permute-start(bf16[128,512]{1,0:T(8,128)(2,1)} %cot_ref.3), channel_id=1, source_target_pairs={{0,16},{16,0},{32,48},{48,32},{64,80},{80,64},{96,112},{112,96},{1... | collective-permute-start | bytes 393224 | tf_op jit(solution)/shard_map/ppermute | solution.py:430
  13.0 16.0 %all-to-all-start = ((bf16[16,32,128]{2,1,0:T(8,128)(2,1)}), bf16[16,32,128]{2,1,0:T(8,128)(2,1)S(1)}, u32[]{:S(2)}, u32[]{:S(2)}) async-start(bf16[16,32,128]{2,1,0:T(8,128)(2,1)} %small_block.1), calls=%async_computation | async-start | bytes 262144 | tf_op jit(solution)/shard_map/all_to_all | solution.py:421
  22.0 89.8 %all-gather.2.cloned.1.call-start = ((), (), s32[]{:S(2)}) async-start(), calls=%async_computation.3 | async-start | bytes 3244032 | tf_op jit(solution)/shard_map/all_gather | solution.py:451
  22.1 0.7 copy-start.9
  22.1 0.9 copy-start.8
  30.0 29.4 %all-to-all-start.1 = ((bf16[16,128,384]{2,1,0:T(8,128)(2,1)}), bf16[16,128,384]{2,1,0:T(8,128)(2,1)S(1)}, u32[]{:S(2)}, u32[]{:S(2)}) async-start(bf16[16,128,384]{2,1,0:T(8,128)(2,1)} %key_terms.1), calls=%async_computation.1 | async-start | bytes 3145728 | tf_op jit(solution)/shard_map/all_to_all | solution.py:421
  42.8 59.6 %copy-start.6 = (f32[128,16]{0,1:T(8,128)S(1)}, f32[128,16]{0,1:T(8,128)}, u32[]{:S(2)}) copy-start(f32[128,16]{0,1:T(8,128)} %param.13) | copy-start | bytes 24580
  42.8 59.6 %copy-start.7 = (s32[128,4]{0,1:T(4,128)S(1)}, s32[128,4]{0,1:T(4,128)}, u32[]{:S(2)}) copy-start(s32[128,4]{0,1:T(4,128)} %param.12) | copy-start | bytes 6148
  42.8 64.7 %copy-start.2 = (f32[6,512]{1,0:T(8,128)S(1)}, f32[6,512]{1,0:T(8,128)}, u32[]{:S(2)}) copy-start(f32[6,512]{1,0:T(8,128)} %weight_ref.3) | copy-start | bytes 36868
  42.8 64.7 %copy-start.3 = (f32[6,512]{1,0:T(8,128)S(1)}, f32[6,512]{1,0:T(8,128)}, u32[]{:S(2)}) copy-start(f32[6,512]{1,0:T(8,128)} %first_ref.1) | copy-start | bytes 36868
  42.8 64.7 %copy-start.4 = (f32[6,512]{1,0:T(8,128)S(1)}, f32[6,512]{1,0:T(8,128)}, u32[]{:S(2)}) copy-start(f32[6,512]{1,0:T(8,128)} %second_ref.1) | copy-start | bytes 36868
  59.4 52.4 %all-to-all-start.2 = ((bf16[16,272,384]{2,1,0:T(8,128)(2,1)}), bf16[16,272,384]{2,1,0:T(8,128)(2,1)}, u32[]{:S(2)}, u32[]{:S(2)}) async-start(bf16[16,272,384]{2,1,0:T(8,128)(2,1)} %pack_rows.1), calls=%async_computation.2 | async-start | bytes 6684672 | tf_op jit(solution)/shard_map/all_to_all | solution.py:421
  66.2 15.4 %collective-permute-start.2 = (f32[4,8,384]{2,1,0:T(8,128)S(1)}, f32[4,8,384]{2,1,0:T(8,128)S(1)}, u32[]{:S(2)}, u32[]{:S(2)}) collective-permute-start(f32[4,8,384]{2,1,0:T(8,128)S(1)} %get-tuple-element.37), channel_id=1, source_target_pairs={{0,32},{16,48},{32,64},{48,80},{64,96},{80,112},{96,128},{112,144}... | collective-permute-start | bytes 147464 | tf_op jit(solution)/shard_map/ppermute | solution.py:426
  68.2 13.5 %collective-permute-start.3 = (f32[4,8,384]{2,1,0:T(8,128)S(1)}, f32[4,8,384]{2,1,0:T(8,128)S(1)}, u32[]{:S(2)}, u32[]{:S(2)}) collective-permute-start(f32[4,8,384]{2,1,0:T(8,128)S(1)} %get-tuple-element.38), channel_id=1, source_target_pairs={{0,448},{16,464},{32,480},{48,496},{64,0},{80,16},{96,32},{112,48}... | collective-permute-start | bytes 147464 | tf_op jit(solution)/shard_map/ppermute | solution.py:426
  78.7 6.0 %collective-permute-start.4 = (f32[4,8,384]{2,1,0:T(8,128)S(1)}, f32[4,8,384]{2,1,0:T(8,128)S(1)}, u32[]{:S(2)}, u32[]{:S(2)}) collective-permute-start(f32[4,8,384]{2,1,0:T(8,128)S(1)} %get-tuple-element.39), channel_id=1, source_target_pairs={{0,480},{16,496},{32,0},{48,16},{64,32},{80,48},{96,64},{112,80},{... | collective-permute-start | bytes 147464 | tf_op jit(solution)/shard_map/ppermute | solution.py:426
  84.7 19.8 %collective-permute-start.5 = (f32[8,384]{1,0:T(8,128)S(1)}, f32[8,384]{1,0:T(8,128)S(1)}, u32[]{:S(2)}, u32[]{:S(2)}) collective-permute-start(f32[8,384]{1,0:T(8,128)S(1)} %get-tuple-element.41), channel_id=1, source_target_pairs={{0,128},{16,144},{32,160},{48,176},{64,192},{80,208},{96,224},{112... | collective-permute-start | bytes 36872 | tf_op jit(solution)/shard_map/ppermute | solution.py:426
  86.6 17.9 %collective-permute-start.6 = (f32[8,384]{1,0:T(8,128)S(1)}, f32[8,384]{1,0:T(8,128)S(1)}, u32[]{:S(2)}, u32[]{:S(2)}) collective-permute-start(f32[8,384]{1,0:T(8,128)S(1)} %get-tuple-element.42), channel_id=1, source_target_pairs={{0,256},{16,272},{32,288},{48,304},{64,320},{80,336},{96,352},{112... | collective-permute-start | bytes 36872 | tf_op jit(solution)/shard_map/ppermute | solution.py:426
  97.9 9.6 %collective-permute-start.7 = (f32[8,384]{1,0:T(8,128)S(1)}, f32[8,384]{1,0:T(8,128)S(1)}, u32[]{:S(2)}, u32[]{:S(2)}) collective-permute-start(f32[8,384]{1,0:T(8,128)S(1)} %get-tuple-element.43), channel_id=1, source_target_pairs={{0,384},{16,400},{32,416},{48,432},{64,448},{80,464},{96,480},{112... | collective-permute-start | bytes 36872 | tf_op jit(solution)/shard_map/ppermute | solution.py:426
  103.2 0.7 copy-start
  103.9 0.7 copy-start.1
  104.5 7.3 %copy-start.5 = (bf16[48,128]{1,0:T(8,128)(2,1)}, bf16[48,128]{1,0:T(8,128)(2,1)S(1)}, u32[]{:S(2)}) copy-start(bf16[48,128]{1,0:T(8,128)(2,1)S(1)} %get-tuple-element.49.logit_ref) | copy-start | bytes 36868
Sparse Core Ops, SparseCore 0:
  30.1 76.2 all-gather.1

commit v5 on v4

--- a/solution.py
+++ b/solution.py
@@ -197,7 +197,7 @@
     )(routing, base, small)
 
 
-STEP = 2
+STEP = 4
 
 
 def combine_kernel(
@@ -265,17 +265,20 @@
     attn = jnp.concatenate([attn_ref[...], attn2_ref[...]], axis=0)
     cot = jnp.concatenate([cot_ref[...], cot2_ref[...]], axis=0)
     grad = dot(attn, cot, 0, 0)
+    kept = []
+    for j in range(4):
+        zero = grad[2 * j * DPROWS : (2 * j + 1) * DPROWS]
+        one = grad[(2 * j + 1) * DPROWS : (2 * j + 2) * DPROWS]
+        kept.append(jnp.where(first, zero, one).astype(BF))
+    pairs = [jnp.concatenate(kept[2 * i : 2 * i + 2], axis=0) for i in range(2)]
+    spans = [jnp.zeros((tall, 2 * LANES), F32)] * SPAN
+    for n, (tile, span) in enumerate(PIECES):
+        at = slice(tile * LANES, (tile + 1) * LANES)
+        both = jnp.concatenate([pair[:, at] for pair in pairs], axis=1)
+        spans[span] = spans[span] + dot(moves[n], both)
     for i in range(2):
-        total = []
-        for j in (2 * i, 2 * i + 1):
-            zero = grad[2 * j * DPROWS : (2 * j + 1) * DPROWS]
-            one = grad[(2 * j + 1) * DPROWS : (2 * j + 2) * DPROWS]
-            total.append(jnp.where(first, zero, one))
-        total = jnp.concatenate(total, axis=0).astype(BF)
-        spans = [jnp.zeros((tall, LANES), F32)] * SPAN
-        for n, (tile, span) in enumerate(PIECES):
-            spans[span] = spans[span] + dot(moves[n], total[:, tile * LANES : (tile + 1) * LANES])
-        out = jnp.concatenate(spans, axis=1).astype(BF)
+        at = slice(i * LANES, (i + 1) * LANES)
+        out = jnp.concatenate([span[:, at] for span in spans], axis=1).astype(BF)
         out_ref[:, i * 2 * LINE : (i + 1) * 2 * LINE, :] = out.reshape(EXP, 2 * LINE, COLS)
 
 

time: 126 us -> 125 us (level)
  no operation moved by 1% of the time
where the time goes in v5:
time: 125 us; the launch traced here: 124 us
  starting transfers between devices  60.1 us (48%)
  waiting for transfers between devices  26.3 us (21%)
  Pallas kernels  21.6 us (17%)
  between operations  14.3 us (11%)
  local copies, waits for them, and re-layouts  2.28 us (2%)
    ppermute x6, starting transfers between devices, shift(): return lax.ppermute(x, 'dp', pairs)  33.1 us
    all_to_all x3, starting transfers between devices, exchange(): return lax.all_to_all(x, 'expert', split_axis=0, concat_axis=0, tiled=True)  22.7 us
    all_to_all x3, waiting for transfers between devices, exchange(): return lax.all_to_all(x, 'expert', split_axis=0, concat_axis=0, tiled=True)  20.2 us
    pallas_call x1, Pallas kernels, combine(): pl.pallas_call(combine_kernel, grid=(PARTS // STEP,), out_shape=jax.Shape...  6.1 us
    ppermute x6, waiting for transfers between devices, shift(): return lax.ppermute(x, 'dp', pairs)  6.02 us
    pallas_call x1, Pallas kernels, key_terms(): pl.pallas_call(terms_kernel, grid=(ZN // 4,), out_shape=jax.ShapeDtypeStr...  5.77 us
    pallas_call x1, Pallas kernels, pack(): pl.pallas_call(pack_kernel, out_shape=jax.ShapeDtypeStruct((EXP, ROWS, CO...  5.54 us
    ppermute x2, starting transfers between devices, swap_core(): return lax.ppermute(x, 'dp', [(i, i ^ 1) for i in range(ZN * CORES)])  4.33 us
  transfers between devices with their start and end apart: 12, of which 4 were waited for; matrix products, arithmetic and copies ran while one was open for 0% of the time, Pallas kernels for 12%

profile of v5, /device:TPU:24, one launch (start us, length us, event | category | flops | bytes accessed | tf_op | source)
XLA Modules:
  0.0 124.5 jit_solution(16422188665106881901)
XLA Ops:
  7.2 1.9 %collective-permute-start = (bf16[128,3072]{1,0:T(8,128)(2,1)}, bf16[128,3072]{1,0:T(8,128)(2,1)S(1)}, u32[]{:S(2)}, u32[]{:S(2)}) collective-permute-start(bf16[128,3072]{1,0:T(8,128)(2,1)} %attn_ref.1), channel_id=1, source_target_pairs={{0,16},{16,0},{32,48},{48,32},{64,80},{80,64},{96,112},{112,96},{1... | collective-permute-start | bytes 2359304 | tf_op jit(solution)/shard_map/ppermute | solution.py:433
  9.1 2.4 %collective-permute-start.1 = (bf16[128,512]{1,0:T(8,128)(2,1)}, bf16[128,512]{1,0:T(8,128)(2,1)S(1)}, u32[]{:S(2)}, u32[]{:S(2)}) collective-permute-start(bf16[128,512]{1,0:T(8,128)(2,1)} %cot_ref.3), channel_id=1, source_target_pairs={{0,16},{16,0},{32,48},{48,32},{64,80},{80,64},{96,112},{112,96},{1... | collective-permute-start | bytes 393224 | tf_op jit(solution)/shard_map/ppermute | solution.py:433
  11.5 1.5 %small_block.1 = bf16[16,32,128]{2,1,0:T(8,128)(2,1)} custom-call(f32[6,512]{1,0:T(8,128)} %weight_ref.3, bf16[16,34]{1,0:T(8,128)(2,1)} %dots_ref.1), custom_call_target="tpu_custom_call" | custom-call | flops 10000 | bytes 10000 | tf_op jit(solution)/shard_map/small_block/pallas_call | solution.py:377
  13.0 9.0 %all-to-all-start = ((bf16[16,32,128]{2,1,0:T(8,128)(2,1)}), bf16[16,32,128]{2,1,0:T(8,128)(2,1)S(1)}, u32[]{:S(2)}, u32[]{:S(2)}) async-start(bf16[16,32,128]{2,1,0:T(8,128)(2,1)} %small_block.1), calls=%async_computation | async-start | bytes 262144 | tf_op jit(solution)/shard_map/all_to_all | solution.py:424
  22.0 0.0 all-gather.2.cloned.1.call-start
  22.0 0.0 collective-permute-done.1.cot2_ref
  22.1 0.0 copy-start.9
  22.1 0.0 collective-permute-done.attn2_ref
  22.1 0.0 copy-start.8
  22.1 0.6 copy-done.9
  22.7 0.3 copy-done.8
  23.0 5.8 %key_terms.1 = bf16[16,128,384]{2,1,0:T(8,128)(2,1)} custom-call(s32[1]{0:T(128)} %bitcast.core_ref, bf16[128,3072]{1,0:T(8,128)(2,1)} %attn_ref.1, bf16[128,3072]{1,0:T(8,128)(2,1)} %copy-done.8, bf16[128,512]{1,0:T(8,128)(2,1)} %cot_ref.3, bf16[128,512]{1,0:T(8,128)(2,1)} %copy-done.9), custom_call_target="tpu_custom_call" | custom-call | flops 10000 | bytes 20000 | tf_op jit(solution)/shard_map/key_terms/pallas_call | solution.py:287
  28.7 0.0 all-to-all-done.dots_ref.small_ref
  28.8 1.0 order_key_rows.1
  29.7 0.0 all-gather.2.cloned.1.call-update
  29.7 7.2 %all-to-all-start.1 = ((bf16[16,128,384]{2,1,0:T(8,128)(2,1)}), bf16[16,128,384]{2,1,0:T(8,128)(2,1)S(1)}, u32[]{:S(2)}, u32[]{:S(2)}) async-start(bf16[16,128,384]{2,1,0:T(8,128)(2,1)} %key_terms.1), calls=%async_computation.1 | async-start | bytes 3145728 | tf_op jit(solution)/shard_map/all_to_all | solution.py:424
  37.0 5.5 %pack_rows.1 = bf16[16,272,384]{2,1,0:T(8,128)(2,1)} custom-call(bf16[34,16,3072]{2,1,0:T(8,128)(2,1)} %bitcast.9), custom_call_target="tpu_custom_call" | custom-call | flops 16106127 | bytes 66846 | tf_op jit(solution)/shard_map/pack_rows/pallas_call | solution.py:109
  42.5 0.0 copy-start.6
  42.5 0.0 copy-start.7
  42.5 0.0 copy-start.2
  42.5 0.0 copy-start.3
  42.6 0.0 copy-start.4
  42.6 16.6 %all-to-all-done.1.terms_ref = bf16[16,128,384]{2,1,0:T(8,128)(2,1)S(1)} async-done(((bf16[16,128,384]{2,1,0:T(8,128)(2,1)}), bf16[16,128,384]{2,1,0:T(8,128)(2,1)S(1)}, u32[]{:S(2)}, u32[]{:S(2)}) %all-to-all-start.1) | async-done | bytes 1572896 | tf_op jit(solution)/shard_map/all_to_all | solution.py:424
  59.2 6.5 %all-to-all-start.2 = ((bf16[16,272,384]{2,1,0:T(8,128)(2,1)}), bf16[16,272,384]{2,1,0:T(8,128)(2,1)}, u32[]{:S(2)}, u32[]{:S(2)}) async-start(bf16[16,272,384]{2,1,0:T(8,128)(2,1)} %pack_rows.1), calls=%async_computation.2 | async-start | bytes 6684672 | tf_op jit(solution)/shard_map/all_to_all | solution.py:424
  65.7 0.3 near_terms.1
  66.0 1.9 %collective-permute-start.2 = (f32[4,8,384]{2,1,0:T(8,128)S(1)}, f32[4,8,384]{2,1,0:T(8,128)S(1)}, u32[]{:S(2)}, u32[]{:S(2)}) collective-permute-start(f32[4,8,384]{2,1,0:T(8,128)S(1)} %get-tuple-element.37), channel_id=1, source_target_pairs={{0,32},{16,48},{32,64},{48,80},{64,96},{80,112},{96,128},{112,144}... | collective-permute-start | bytes 147464 | tf_op jit(solution)/shard_map/ppermute | solution.py:429
  67.9 10.5 %collective-permute-start.3 = (f32[4,8,384]{2,1,0:T(8,128)S(1)}, f32[4,8,384]{2,1,0:T(8,128)S(1)}, u32[]{:S(2)}, u32[]{:S(2)}) collective-permute-start(f32[4,8,384]{2,1,0:T(8,128)S(1)} %get-tuple-element.38), channel_id=1, source_target_pairs={{0,448},{16,464},{32,480},{48,496},{64,0},{80,16},{96,32},{112,48}... | collective-permute-start | bytes 147464 | tf_op jit(solution)/shard_map/ppermute | solution.py:429
  78.4 2.9 %collective-permute-start.4 = (f32[4,8,384]{2,1,0:T(8,128)S(1)}, f32[4,8,384]{2,1,0:T(8,128)S(1)}, u32[]{:S(2)}, u32[]{:S(2)}) collective-permute-start(f32[4,8,384]{2,1,0:T(8,128)S(1)} %get-tuple-element.39), channel_id=1, source_target_pairs={{0,480},{16,496},{32,0},{48,16},{64,32},{80,48},{96,64},{112,80},{... | collective-permute-start | bytes 147464 | tf_op jit(solution)/shard_map/ppermute | solution.py:429
  81.4 0.0 collective-permute-done.2.up_ref
  81.4 0.0 collective-permute-done.3.across_ref
  81.4 3.0 %collective-permute-done.4.down_ref = f32[4,8,384]{2,1,0:T(8,128)S(1)} collective-permute-done((f32[4,8,384]{2,1,0:T(8,128)S(1)}, f32[4,8,384]{2,1,0:T(8,128)S(1)}, u32[]{:S(2)}, u32[]{:S(2)}) %collective-permute-start.4) | collective-permute-done | bytes 49184 | tf_op jit(solution)/shard_map/ppermute | solution.py:429
  84.4 1.9 %collective-permute-start.5 = (f32[8,384]{1,0:T(8,128)S(1)}, f32[8,384]{1,0:T(8,128)S(1)}, u32[]{:S(2)}, u32[]{:S(2)}) collective-permute-start(f32[8,384]{1,0:T(8,128)S(1)} %get-tuple-element.41), channel_id=1, source_target_pairs={{0,128},{16,144},{32,160},{48,176},{64,192},{80,208},{96,224},{112... | collective-permute-start | bytes 36872 | tf_op jit(solution)/shard_map/ppermute | solution.py:429
  86.3 11.3 %collective-permute-start.6 = (f32[8,384]{1,0:T(8,128)S(1)}, f32[8,384]{1,0:T(8,128)S(1)}, u32[]{:S(2)}, u32[]{:S(2)}) collective-permute-start(f32[8,384]{1,0:T(8,128)S(1)} %get-tuple-element.42), channel_id=1, source_target_pairs={{0,256},{16,272},{32,288},{48,304},{64,320},{80,336},{96,352},{112... | collective-permute-start | bytes 36872 | tf_op jit(solution)/shard_map/ppermute | solution.py:429
  97.6 4.5 %collective-permute-start.7 = (f32[8,384]{1,0:T(8,128)S(1)}, f32[8,384]{1,0:T(8,128)S(1)}, u32[]{:S(2)}, u32[]{:S(2)}) collective-permute-start(f32[8,384]{1,0:T(8,128)S(1)} %get-tuple-element.43), channel_id=1, source_target_pairs={{0,384},{16,400},{32,416},{48,432},{64,448},{80,464},{96,480},{112... | collective-permute-start | bytes 36872 | tf_op jit(solution)/shard_map/ppermute | solution.py:429
  102.1 0.0 copy-done.6
  102.2 0.0 copy-done.7
  102.2 0.7 gates.1
  102.9 0.7 copy-done
  103.6 0.7 copy-done.1
  104.2 0.0 collective-permute-done.5.up_ref
  104.2 0.0 collective-permute-done.6.across_ref
  104.2 3.0 %collective-permute-done.7.down_ref = f32[8,384]{1,0:T(8,128)S(1)} collective-permute-done((f32[8,384]{1,0:T(8,128)S(1)}, f32[8,384]{1,0:T(8,128)S(1)}, u32[]{:S(2)}, u32[]{:S(2)}) %collective-permute-start.7) | collective-permute-done | bytes 12320 | tf_op jit(solution)/shard_map/ppermute | solution.py:429
  107.2 0.0 copy-done.2
  107.3 0.0 copy-done.3
  107.3 0.6 adamw.1
  107.9 3.6 %all-to-all-done.2.head_ref.tail_ref = bf16[16,272,384]{2,1,0:T(8,128)(2,1)} async-done(((bf16[16,272,384]{2,1,0:T(8,128)(2,1)}), bf16[16,272,384]{2,1,0:T(8,128)(2,1)}, u32[]{:S(2)}, u32[]{:S(2)}) %all-to-all-start.2) | async-done | bytes 3342368 | tf_op jit(solution)/shard_map/all_to_all | solution.py:424
  111.5 0.0 copy-done.5
  111.5 6.1 %combine.1 = bf16[128,3072]{1,0:T(8,128)(2,1)} custom-call(bf16[256,512]{1,0:T(8,128)(2,1)} %copy-done, bf16[256,256]{1,0:T(8,128)(2,1)} %copy-done.1, bf16[48,128]{1,0:T(8,128)(2,1)} %copy-done.5, bf16[128,512]{1,0:T(8,128)(2,1)} %cot_ref.3, bf16[16,272,384]{2,1,0:T(8,128)(2,1)} %all-to-all-done.2.head_ref.tail_ref, ...), custom_call_target="tpu_custom_call" | custom-call | flops 20000000 | bytes 80000 | tf_op jit(solution)/shard_map/combine/pallas_call | solution.py:223
  (6 shorter events, 0.0 us)
Async XLA Ops:
  7.2 14.9 %collective-permute-start = (bf16[128,3072]{1,0:T(8,128)(2,1)}, bf16[128,3072]{1,0:T(8,128)(2,1)S(1)}, u32[]{:S(2)}, u32[]{:S(2)}) collective-permute-start(bf16[128,3072]{1,0:T(8,128)(2,1)} %attn_ref.1), channel_id=1, source_target_pairs={{0,16},{16,0},{32,48},{48,32},{64,80},{80,64},{96,112},{112,96},{1... | collective-permute-start | bytes 2359304 | tf_op jit(solution)/shard_map/ppermute | solution.py:433
  9.1 13.0 %collective-permute-start.1 = (bf16[128,512]{1,0:T(8,128)(2,1)}, bf16[128,512]{1,0:T(8,128)(2,1)S(1)}, u32[]{:S(2)}, u32[]{:S(2)}) collective-permute-start(bf16[128,512]{1,0:T(8,128)(2,1)} %cot_ref.3), channel_id=1, source_target_pairs={{0,16},{16,0},{32,48},{48,32},{64,80},{80,64},{96,112},{112,96},{1... | collective-permute-start | bytes 393224 | tf_op jit(solution)/shard_map/ppermute | solution.py:433
  13.0 15.7 %all-to-all-start = ((bf16[16,32,128]{2,1,0:T(8,128)(2,1)}), bf16[16,32,128]{2,1,0:T(8,128)(2,1)S(1)}, u32[]{:S(2)}, u32[]{:S(2)}) async-start(bf16[16,32,128]{2,1,0:T(8,128)(2,1)} %small_block.1), calls=%async_computation | async-start | bytes 262144 | tf_op jit(solution)/shard_map/all_to_all | solution.py:424
  22.0 89.5 %all-gather.2.cloned.1.call-start = ((), (), s32[]{:S(2)}) async-start(), calls=%async_computation.3 | async-start | bytes 3244032 | tf_op jit(solution)/shard_map/all_gather | solution.py:454
  22.1 0.7 copy-start.9
  22.1 0.9 copy-start.8
  29.7 29.4 %all-to-all-start.1 = ((bf16[16,128,384]{2,1,0:T(8,128)(2,1)}), bf16[16,128,384]{2,1,0:T(8,128)(2,1)S(1)}, u32[]{:S(2)}, u32[]{:S(2)}) async-start(bf16[16,128,384]{2,1,0:T(8,128)(2,1)} %key_terms.1), calls=%async_computation.1 | async-start | bytes 3145728 | tf_op jit(solution)/shard_map/all_to_all | solution.py:424
  42.5 59.6 %copy-start.6 = (f32[128,16]{0,1:T(8,128)S(1)}, f32[128,16]{0,1:T(8,128)}, u32[]{:S(2)}) copy-start(f32[128,16]{0,1:T(8,128)} %param.13) | copy-start | bytes 24580
  42.5 59.6 %copy-start.7 = (s32[128,4]{0,1:T(4,128)S(1)}, s32[128,4]{0,1:T(4,128)}, u32[]{:S(2)}) copy-start(s32[128,4]{0,1:T(4,128)} %param.12) | copy-start | bytes 6148
  42.5 64.7 %copy-start.2 = (f32[6,512]{1,0:T(8,128)S(1)}, f32[6,512]{1,0:T(8,128)}, u32[]{:S(2)}) copy-start(f32[6,512]{1,0:T(8,128)} %weight_ref.3) | copy-start | bytes 36868
  42.5 64.7 %copy-start.3 = (f32[6,512]{1,0:T(8,128)S(1)}, f32[6,512]{1,0:T(8,128)}, u32[]{:S(2)}) copy-start(f32[6,512]{1,0:T(8,128)} %first_ref.1) | copy-start | bytes 36868
  42.6 64.7 %copy-start.4 = (f32[6,512]{1,0:T(8,128)S(1)}, f32[6,512]{1,0:T(8,128)}, u32[]{:S(2)}) copy-start(f32[6,512]{1,0:T(8,128)} %second_ref.1) | copy-start | bytes 36868
  59.2 52.4 %all-to-all-start.2 = ((bf16[16,272,384]{2,1,0:T(8,128)(2,1)}), bf16[16,272,384]{2,1,0:T(8,128)(2,1)}, u32[]{:S(2)}, u32[]{:S(2)}) async-start(bf16[16,272,384]{2,1,0:T(8,128)(2,1)} %pack_rows.1), calls=%async_computation.2 | async-start | bytes 6684672 | tf_op jit(solution)/shard_map/all_to_all | solution.py:424
  66.0 15.4 %collective-permute-start.2 = (f32[4,8,384]{2,1,0:T(8,128)S(1)}, f32[4,8,384]{2,1,0:T(8,128)S(1)}, u32[]{:S(2)}, u32[]{:S(2)}) collective-permute-start(f32[4,8,384]{2,1,0:T(8,128)S(1)} %get-tuple-element.37), channel_id=1, source_target_pairs={{0,32},{16,48},{32,64},{48,80},{64,96},{80,112},{96,128},{112,144}... | collective-permute-start | bytes 147464 | tf_op jit(solution)/shard_map/ppermute | solution.py:429
  67.9 13.5 %collective-permute-start.3 = (f32[4,8,384]{2,1,0:T(8,128)S(1)}, f32[4,8,384]{2,1,0:T(8,128)S(1)}, u32[]{:S(2)}, u32[]{:S(2)}) collective-permute-start(f32[4,8,384]{2,1,0:T(8,128)S(1)} %get-tuple-element.38), channel_id=1, source_target_pairs={{0,448},{16,464},{32,480},{48,496},{64,0},{80,16},{96,32},{112,48}... | collective-permute-start | bytes 147464 | tf_op jit(solution)/shard_map/ppermute | solution.py:429
  78.4 6.0 %collective-permute-start.4 = (f32[4,8,384]{2,1,0:T(8,128)S(1)}, f32[4,8,384]{2,1,0:T(8,128)S(1)}, u32[]{:S(2)}, u32[]{:S(2)}) collective-permute-start(f32[4,8,384]{2,1,0:T(8,128)S(1)} %get-tuple-element.39), channel_id=1, source_target_pairs={{0,480},{16,496},{32,0},{48,16},{64,32},{80,48},{96,64},{112,80},{... | collective-permute-start | bytes 147464 | tf_op jit(solution)/shard_map/ppermute | solution.py:429
  84.4 19.8 %collective-permute-start.5 = (f32[8,384]{1,0:T(8,128)S(1)}, f32[8,384]{1,0:T(8,128)S(1)}, u32[]{:S(2)}, u32[]{:S(2)}) collective-permute-start(f32[8,384]{1,0:T(8,128)S(1)} %get-tuple-element.41), channel_id=1, source_target_pairs={{0,128},{16,144},{32,160},{48,176},{64,192},{80,208},{96,224},{112... | collective-permute-start | bytes 36872 | tf_op jit(solution)/shard_map/ppermute | solution.py:429
  86.3 17.9 %collective-permute-start.6 = (f32[8,384]{1,0:T(8,128)S(1)}, f32[8,384]{1,0:T(8,128)S(1)}, u32[]{:S(2)}, u32[]{:S(2)}) collective-permute-start(f32[8,384]{1,0:T(8,128)S(1)} %get-tuple-element.42), channel_id=1, source_target_pairs={{0,256},{16,272},{32,288},{48,304},{64,320},{80,336},{96,352},{112... | collective-permute-start | bytes 36872 | tf_op jit(solution)/shard_map/ppermute | solution.py:429
  97.6 9.6 %collective-permute-start.7 = (f32[8,384]{1,0:T(8,128)S(1)}, f32[8,384]{1,0:T(8,128)S(1)}, u32[]{:S(2)}, u32[]{:S(2)}) collective-permute-start(f32[8,384]{1,0:T(8,128)S(1)} %get-tuple-element.43), channel_id=1, source_target_pairs={{0,384},{16,400},{32,416},{48,432},{64,448},{80,464},{96,480},{112... | collective-permute-start | bytes 36872 | tf_op jit(solution)/shard_map/ppermute | solution.py:429
  102.9 0.7 copy-start
  103.6 0.7 copy-start.1
  104.2 7.3 %copy-start.5 = (bf16[48,128]{1,0:T(8,128)(2,1)}, bf16[48,128]{1,0:T(8,128)(2,1)S(1)}, u32[]{:S(2)}) copy-start(bf16[48,128]{1,0:T(8,128)(2,1)S(1)} %get-tuple-element.49.logit_ref) | copy-start | bytes 36868
Sparse Core Ops, SparseCore 0:
  29.9 76.1 all-gather.1

commit v6 on v5

--- a/solution.py
+++ b/solution.py
@@ -266,30 +266,30 @@
     cot = jnp.concatenate([cot_ref[...], cot2_ref[...]], axis=0)
     grad = dot(attn, cot, 0, 0)
     kept = []
-    for j in range(4):
+    for j in range(8):
         zero = grad[2 * j * DPROWS : (2 * j + 1) * DPROWS]
         one = grad[(2 * j + 1) * DPROWS : (2 * j + 2) * DPROWS]
         kept.append(jnp.where(first, zero, one).astype(BF))
-    pairs = [jnp.concatenate(kept[2 * i : 2 * i + 2], axis=0) for i in range(2)]
-    spans = [jnp.zeros((tall, 2 * LANES), F32)] * SPAN
+    pairs = [jnp.concatenate(kept[2 * i : 2 * i + 2], axis=0) for i in range(4)]
+    spans = [jnp.zeros((tall, 4 * LANES), F32)] * SPAN
     for n, (tile, span) in enumerate(PIECES):
         at = slice(tile * LANES, (tile + 1) * LANES)
         both = jnp.concatenate([pair[:, at] for pair in pairs], axis=1)
         spans[span] = spans[span] + dot(moves[n], both)
-    for i in range(2):
+    for i in range(4):
         at = slice(i * LANES, (i + 1) * LANES)
         out = jnp.concatenate([span[:, at] for span in spans], axis=1).astype(BF)
         out_ref[:, i * 2 * LINE : (i + 1) * 2 * LINE, :] = out.reshape(EXP, 2 * LINE, COLS)
 
 
 def key_terms(core, attn, attn2, cot, cot2):
-    columns = pl.BlockSpec((TOK, 4 * CORES * DPROWS), lambda i: (0, i))
+    columns = pl.BlockSpec((TOK, 8 * CORES * DPROWS), lambda i: (0, i))
     return pl.pallas_call(
         terms_kernel,
-        grid=(ZN // 4,),
+        grid=(ZN // 8,),
         out_shape=jax.ShapeDtypeStruct((EXP, KEYS, COLS), BF),
         in_specs=[smem(), columns, columns, full(TOK, KC), full(TOK, KC)],
-        out_specs=pl.BlockSpec((EXP, 4 * LINE, COLS), lambda i: (0, i, 0)),
+        out_specs=pl.BlockSpec((EXP, 8 * LINE, COLS), lambda i: (0, i, 0)),
         scratch_shapes=[VM((len(PIECES), 2 * EXP * LINE, 2 * DPROWS), BF)],
         compiler_params=params(BIG),
         cost_estimate=cost(10**6, 2 * 10**6),

time: 125 us -> 124 us (level)
  transfers between devices with their start and end apart: 12 -> 12, of which waited for: 4 -> 4; matrix products, arithmetic and copies ran while one was open for 0% -> 0% of each run, Pallas kernels for 12% -> 11%
where the time goes in v6:
time: 124 us; the launch traced here: 123 us
  starting transfers between devices  60.1 us (48%)
  waiting for transfers between devices  26.3 us (21%)
  Pallas kernels  20.5 us (17%)
  between operations  14.3 us (12%)
  local copies, waits for them, and re-layouts  2.28 us (2%)
    ppermute x6, starting transfers between devices, shift(): return lax.ppermute(x, 'dp', pairs)  33.1 us
    all_to_all x3, starting transfers between devices, exchange(): return lax.all_to_all(x, 'expert', split_axis=0, concat_axis=0, tiled=True)  22.7 us
    all_to_all x3, waiting for transfers between devices, exchange(): return lax.all_to_all(x, 'expert', split_axis=0, concat_axis=0, tiled=True)  20.3 us
    pallas_call x1, Pallas kernels, combine(): pl.pallas_call(combine_kernel, grid=(PARTS // STEP,), out_shape=jax.Shape...  6.1 us
    ppermute x6, waiting for transfers between devices, shift(): return lax.ppermute(x, 'dp', pairs)  6 us
    pallas_call x1, Pallas kernels, pack(): pl.pallas_call(pack_kernel, out_shape=jax.ShapeDtypeStruct((EXP, ROWS, CO...  5.54 us
    pallas_call x1, Pallas kernels, key_terms(): pl.pallas_call(terms_kernel, grid=(ZN // 8,), out_shape=jax.ShapeDtypeStr...  4.73 us
    ppermute x2, starting transfers between devices, swap_core(): return lax.ppermute(x, 'dp', [(i, i ^ 1) for i in range(ZN * CORES)])  4.33 us
  transfers between devices with their start and end apart: 12, of which 4 were waited for; matrix products, arithmetic and copies ran while one was open for 0% of the time, Pallas kernels for 11%

profile of v6, /device:TPU:24, one launch (start us, length us, event | category | flops | bytes accessed | tf_op | source)
XLA Modules:
  0.0 123.4 jit_solution(11377714903346684960)
XLA Ops:
  7.2 1.9 %collective-permute-start = (bf16[128,3072]{1,0:T(8,128)(2,1)}, bf16[128,3072]{1,0:T(8,128)(2,1)S(1)}, u32[]{:S(2)}, u32[]{:S(2)}) collective-permute-start(bf16[128,3072]{1,0:T(8,128)(2,1)} %attn_ref.1), channel_id=1, source_target_pairs={{0,16},{16,0},{32,48},{48,32},{64,80},{80,64},{96,112},{112,96},{1... | collective-permute-start | bytes 2359304 | tf_op jit(solution)/shard_map/ppermute | solution.py:433
  9.1 2.4 %collective-permute-start.1 = (bf16[128,512]{1,0:T(8,128)(2,1)}, bf16[128,512]{1,0:T(8,128)(2,1)S(1)}, u32[]{:S(2)}, u32[]{:S(2)}) collective-permute-start(bf16[128,512]{1,0:T(8,128)(2,1)} %cot_ref.3), channel_id=1, source_target_pairs={{0,16},{16,0},{32,48},{48,32},{64,80},{80,64},{96,112},{112,96},{1... | collective-permute-start | bytes 393224 | tf_op jit(solution)/shard_map/ppermute | solution.py:433
  11.5 1.5 %small_block.1 = bf16[16,32,128]{2,1,0:T(8,128)(2,1)} custom-call(f32[6,512]{1,0:T(8,128)} %weight_ref.3, bf16[16,34]{1,0:T(8,128)(2,1)} %dots_ref.1), custom_call_target="tpu_custom_call" | custom-call | flops 10000 | bytes 10000 | tf_op jit(solution)/shard_map/small_block/pallas_call | solution.py:377
  13.0 9.0 %all-to-all-start = ((bf16[16,32,128]{2,1,0:T(8,128)(2,1)}), bf16[16,32,128]{2,1,0:T(8,128)(2,1)S(1)}, u32[]{:S(2)}, u32[]{:S(2)}) async-start(bf16[16,32,128]{2,1,0:T(8,128)(2,1)} %small_block.1), calls=%async_computation | async-start | bytes 262144 | tf_op jit(solution)/shard_map/all_to_all | solution.py:424
  22.0 0.0 all-gather.2.cloned.1.call-start
  22.0 0.0 collective-permute-done.1.cot2_ref
  22.1 0.0 copy-start.9
  22.1 0.0 collective-permute-done.attn2_ref
  22.1 0.0 copy-start.8
  22.1 0.6 copy-done.9
  22.7 0.3 copy-done.8
  23.0 4.7 %key_terms.1 = bf16[16,128,384]{2,1,0:T(8,128)(2,1)} custom-call(s32[1]{0:T(128)} %bitcast.core_ref, bf16[128,3072]{1,0:T(8,128)(2,1)} %attn_ref.1, bf16[128,3072]{1,0:T(8,128)(2,1)} %copy-done.8, bf16[128,512]{1,0:T(8,128)(2,1)} %cot_ref.3, bf16[128,512]{1,0:T(8,128)(2,1)} %copy-done.9), custom_call_target="tpu_custom_call" | custom-call | flops 10000 | bytes 20000 | tf_op jit(solution)/shard_map/key_terms/pallas_call | solution.py:287
  27.7 0.0 all-to-all-done.dots_ref.small_ref
  27.7 1.0 order_key_rows.1
  28.7 0.0 all-gather.2.cloned.1.call-update
  28.7 7.2 %all-to-all-start.1 = ((bf16[16,128,384]{2,1,0:T(8,128)(2,1)}), bf16[16,128,384]{2,1,0:T(8,128)(2,1)S(1)}, u32[]{:S(2)}, u32[]{:S(2)}) async-start(bf16[16,128,384]{2,1,0:T(8,128)(2,1)} %key_terms.1), calls=%async_computation.1 | async-start | bytes 3145728 | tf_op jit(solution)/shard_map/all_to_all | solution.py:424
  35.9 5.5 %pack_rows.1 = bf16[16,272,384]{2,1,0:T(8,128)(2,1)} custom-call(bf16[34,16,3072]{2,1,0:T(8,128)(2,1)} %bitcast.9), custom_call_target="tpu_custom_call" | custom-call | flops 16106127 | bytes 66846 | tf_op jit(solution)/shard_map/pack_rows/pallas_call | solution.py:109
  41.5 0.0 copy-start.6
  41.5 0.0 copy-start.7
  41.5 0.0 copy-start.2
  41.5 0.0 copy-start.3
  41.5 0.0 copy-start.4
  41.5 16.6 %all-to-all-done.1.terms_ref = bf16[16,128,384]{2,1,0:T(8,128)(2,1)S(1)} async-done(((bf16[16,128,384]{2,1,0:T(8,128)(2,1)}), bf16[16,128,384]{2,1,0:T(8,128)(2,1)S(1)}, u32[]{:S(2)}, u32[]{:S(2)}) %all-to-all-start.1) | async-done | bytes 1572896 | tf_op jit(solution)/shard_map/all_to_all | solution.py:424
  58.1 6.5 %all-to-all-start.2 = ((bf16[16,272,384]{2,1,0:T(8,128)(2,1)}), bf16[16,272,384]{2,1,0:T(8,128)(2,1)}, u32[]{:S(2)}, u32[]{:S(2)}) async-start(bf16[16,272,384]{2,1,0:T(8,128)(2,1)} %pack_rows.1), calls=%async_computation.2 | async-start | bytes 6684672 | tf_op jit(solution)/shard_map/all_to_all | solution.py:424
  64.6 0.3 near_terms.1
  64.9 1.9 %collective-permute-start.2 = (f32[4,8,384]{2,1,0:T(8,128)S(1)}, f32[4,8,384]{2,1,0:T(8,128)S(1)}, u32[]{:S(2)}, u32[]{:S(2)}) collective-permute-start(f32[4,8,384]{2,1,0:T(8,128)S(1)} %get-tuple-element.37), channel_id=1, source_target_pairs={{0,32},{16,48},{32,64},{48,80},{64,96},{80,112},{96,128},{112,144}... | collective-permute-start | bytes 147464 | tf_op jit(solution)/shard_map/ppermute | solution.py:429
  66.8 10.5 %collective-permute-start.3 = (f32[4,8,384]{2,1,0:T(8,128)S(1)}, f32[4,8,384]{2,1,0:T(8,128)S(1)}, u32[]{:S(2)}, u32[]{:S(2)}) collective-permute-start(f32[4,8,384]{2,1,0:T(8,128)S(1)} %get-tuple-element.38), channel_id=1, source_target_pairs={{0,448},{16,464},{32,480},{48,496},{64,0},{80,16},{96,32},{112,48}... | collective-permute-start | bytes 147464 | tf_op jit(solution)/shard_map/ppermute | solution.py:429
  77.4 2.9 %collective-permute-start.4 = (f32[4,8,384]{2,1,0:T(8,128)S(1)}, f32[4,8,384]{2,1,0:T(8,128)S(1)}, u32[]{:S(2)}, u32[]{:S(2)}) collective-permute-start(f32[4,8,384]{2,1,0:T(8,128)S(1)} %get-tuple-element.39), channel_id=1, source_target_pairs={{0,480},{16,496},{32,0},{48,16},{64,32},{80,48},{96,64},{112,80},{... | collective-permute-start | bytes 147464 | tf_op jit(solution)/shard_map/ppermute | solution.py:429
  80.3 0.0 collective-permute-done.2.up_ref
  80.3 0.0 collective-permute-done.3.across_ref
  80.3 3.0 %collective-permute-done.4.down_ref = f32[4,8,384]{2,1,0:T(8,128)S(1)} collective-permute-done((f32[4,8,384]{2,1,0:T(8,128)S(1)}, f32[4,8,384]{2,1,0:T(8,128)S(1)}, u32[]{:S(2)}, u32[]{:S(2)}) %collective-permute-start.4) | collective-permute-done | bytes 49184 | tf_op jit(solution)/shard_map/ppermute | solution.py:429
  83.4 1.9 %collective-permute-start.5 = (f32[8,384]{1,0:T(8,128)S(1)}, f32[8,384]{1,0:T(8,128)S(1)}, u32[]{:S(2)}, u32[]{:S(2)}) collective-permute-start(f32[8,384]{1,0:T(8,128)S(1)} %get-tuple-element.41), channel_id=1, source_target_pairs={{0,128},{16,144},{32,160},{48,176},{64,192},{80,208},{96,224},{112... | collective-permute-start | bytes 36872 | tf_op jit(solution)/shard_map/ppermute | solution.py:429
  85.3 11.2 %collective-permute-start.6 = (f32[8,384]{1,0:T(8,128)S(1)}, f32[8,384]{1,0:T(8,128)S(1)}, u32[]{:S(2)}, u32[]{:S(2)}) collective-permute-start(f32[8,384]{1,0:T(8,128)S(1)} %get-tuple-element.42), channel_id=1, source_target_pairs={{0,256},{16,272},{32,288},{48,304},{64,320},{80,336},{96,352},{112... | collective-permute-start | bytes 36872 | tf_op jit(solution)/shard_map/ppermute | solution.py:429
  96.6 4.5 %collective-permute-start.7 = (f32[8,384]{1,0:T(8,128)S(1)}, f32[8,384]{1,0:T(8,128)S(1)}, u32[]{:S(2)}, u32[]{:S(2)}) collective-permute-start(f32[8,384]{1,0:T(8,128)S(1)} %get-tuple-element.43), channel_id=1, source_target_pairs={{0,384},{16,400},{32,416},{48,432},{64,448},{80,464},{96,480},{112... | collective-permute-start | bytes 36872 | tf_op jit(solution)/shard_map/ppermute | solution.py:429
  101.1 0.0 copy-done.6
  101.1 0.0 copy-done.7
  101.1 0.7 gates.1
  101.8 0.7 copy-done
  102.6 0.7 copy-done.1
  103.2 0.0 collective-permute-done.5.up_ref
  103.2 0.0 collective-permute-done.6.across_ref
  103.2 3.0 %collective-permute-done.7.down_ref = f32[8,384]{1,0:T(8,128)S(1)} collective-permute-done((f32[8,384]{1,0:T(8,128)S(1)}, f32[8,384]{1,0:T(8,128)S(1)}, u32[]{:S(2)}, u32[]{:S(2)}) %collective-permute-start.7) | collective-permute-done | bytes 12320 | tf_op jit(solution)/shard_map/ppermute | solution.py:429
  106.2 0.0 copy-done.2
  106.2 0.0 copy-done.3
  106.2 0.0 copy-done.4
  106.2 0.6 adamw.1
  106.8 3.6 %all-to-all-done.2.head_ref.tail_ref = bf16[16,272,384]{2,1,0:T(8,128)(2,1)} async-done(((bf16[16,272,384]{2,1,0:T(8,128)(2,1)}), bf16[16,272,384]{2,1,0:T(8,128)(2,1)}, u32[]{:S(2)}, u32[]{:S(2)}) %all-to-all-start.2) | async-done | bytes 3342368 | tf_op jit(solution)/shard_map/all_to_all | solution.py:424
  110.5 6.1 %combine.1 = bf16[128,3072]{1,0:T(8,128)(2,1)} custom-call(bf16[256,512]{1,0:T(8,128)(2,1)} %copy-done, bf16[256,256]{1,0:T(8,128)(2,1)} %copy-done.1, bf16[48,128]{1,0:T(8,128)(2,1)} %copy-done.5, bf16[128,512]{1,0:T(8,128)(2,1)} %cot_ref.3, bf16[16,272,384]{2,1,0:T(8,128)(2,1)} %all-to-all-done.2.head_ref.tail_ref, ...), custom_call_target="tpu_custom_call" | custom-call | flops 20000000 | bytes 80000 | tf_op jit(solution)/shard_map/combine/pallas_call | solution.py:223
  (6 shorter events, 0.0 us)
Async XLA Ops:
  7.2 14.9 %collective-permute-start = (bf16[128,3072]{1,0:T(8,128)(2,1)}, bf16[128,3072]{1,0:T(8,128)(2,1)S(1)}, u32[]{:S(2)}, u32[]{:S(2)}) collective-permute-start(bf16[128,3072]{1,0:T(8,128)(2,1)} %attn_ref.1), channel_id=1, source_target_pairs={{0,16},{16,0},{32,48},{48,32},{64,80},{80,64},{96,112},{112,96},{1... | collective-permute-start | bytes 2359304 | tf_op jit(solution)/shard_map/ppermute | solution.py:433
  9.1 13.0 %collective-permute-start.1 = (bf16[128,512]{1,0:T(8,128)(2,1)}, bf16[128,512]{1,0:T(8,128)(2,1)S(1)}, u32[]{:S(2)}, u32[]{:S(2)}) collective-permute-start(bf16[128,512]{1,0:T(8,128)(2,1)} %cot_ref.3), channel_id=1, source_target_pairs={{0,16},{16,0},{32,48},{48,32},{64,80},{80,64},{96,112},{112,96},{1... | collective-permute-start | bytes 393224 | tf_op jit(solution)/shard_map/ppermute | solution.py:433
  13.0 14.7 %all-to-all-start = ((bf16[16,32,128]{2,1,0:T(8,128)(2,1)}), bf16[16,32,128]{2,1,0:T(8,128)(2,1)S(1)}, u32[]{:S(2)}, u32[]{:S(2)}) async-start(bf16[16,32,128]{2,1,0:T(8,128)(2,1)} %small_block.1), calls=%async_computation | async-start | bytes 262144 | tf_op jit(solution)/shard_map/all_to_all | solution.py:424
  22.0 88.5 %all-gather.2.cloned.1.call-start = ((), (), s32[]{:S(2)}) async-start(), calls=%async_computation.3 | async-start | bytes 3244032 | tf_op jit(solution)/shard_map/all_gather | solution.py:454
  22.1 0.7 copy-start.9
  22.1 0.9 copy-start.8
  28.7 29.4 %all-to-all-start.1 = ((bf16[16,128,384]{2,1,0:T(8,128)(2,1)}), bf16[16,128,384]{2,1,0:T(8,128)(2,1)S(1)}, u32[]{:S(2)}, u32[]{:S(2)}) async-start(bf16[16,128,384]{2,1,0:T(8,128)(2,1)} %key_terms.1), calls=%async_computation.1 | async-start | bytes 3145728 | tf_op jit(solution)/shard_map/all_to_all | solution.py:424
  41.5 59.6 %copy-start.6 = (f32[128,16]{0,1:T(8,128)S(1)}, f32[128,16]{0,1:T(8,128)}, u32[]{:S(2)}) copy-start(f32[128,16]{0,1:T(8,128)} %param.13) | copy-start | bytes 24580
  41.5 59.6 %copy-start.7 = (s32[128,4]{0,1:T(4,128)S(1)}, s32[128,4]{0,1:T(4,128)}, u32[]{:S(2)}) copy-start(s32[128,4]{0,1:T(4,128)} %param.12) | copy-start | bytes 6148
  41.5 64.7 %copy-start.2 = (f32[6,512]{1,0:T(8,128)S(1)}, f32[6,512]{1,0:T(8,128)}, u32[]{:S(2)}) copy-start(f32[6,512]{1,0:T(8,128)} %weight_ref.3) | copy-start | bytes 36868
  41.5 64.7 %copy-start.3 = (f32[6,512]{1,0:T(8,128)S(1)}, f32[6,512]{1,0:T(8,128)}, u32[]{:S(2)}) copy-start(f32[6,512]{1,0:T(8,128)} %first_ref.1) | copy-start | bytes 36868
  41.5 64.7 %copy-start.4 = (f32[6,512]{1,0:T(8,128)S(1)}, f32[6,512]{1,0:T(8,128)}, u32[]{:S(2)}) copy-start(f32[6,512]{1,0:T(8,128)} %second_ref.1) | copy-start | bytes 36868
  58.1 52.3 %all-to-all-start.2 = ((bf16[16,272,384]{2,1,0:T(8,128)(2,1)}), bf16[16,272,384]{2,1,0:T(8,128)(2,1)}, u32[]{:S(2)}, u32[]{:S(2)}) async-start(bf16[16,272,384]{2,1,0:T(8,128)(2,1)} %pack_rows.1), calls=%async_computation.2 | async-start | bytes 6684672 | tf_op jit(solution)/shard_map/all_to_all | solution.py:424
  64.9 15.4 %collective-permute-start.2 = (f32[4,8,384]{2,1,0:T(8,128)S(1)}, f32[4,8,384]{2,1,0:T(8,128)S(1)}, u32[]{:S(2)}, u32[]{:S(2)}) collective-permute-start(f32[4,8,384]{2,1,0:T(8,128)S(1)} %get-tuple-element.37), channel_id=1, source_target_pairs={{0,32},{16,48},{32,64},{48,80},{64,96},{80,112},{96,128},{112,144}... | collective-permute-start | bytes 147464 | tf_op jit(solution)/shard_map/ppermute | solution.py:429
  66.8 13.5 %collective-permute-start.3 = (f32[4,8,384]{2,1,0:T(8,128)S(1)}, f32[4,8,384]{2,1,0:T(8,128)S(1)}, u32[]{:S(2)}, u32[]{:S(2)}) collective-permute-start(f32[4,8,384]{2,1,0:T(8,128)S(1)} %get-tuple-element.38), channel_id=1, source_target_pairs={{0,448},{16,464},{32,480},{48,496},{64,0},{80,16},{96,32},{112,48}... | collective-permute-start | bytes 147464 | tf_op jit(solution)/shard_map/ppermute | solution.py:429
  77.4 6.0 %collective-permute-start.4 = (f32[4,8,384]{2,1,0:T(8,128)S(1)}, f32[4,8,384]{2,1,0:T(8,128)S(1)}, u32[]{:S(2)}, u32[]{:S(2)}) collective-permute-start(f32[4,8,384]{2,1,0:T(8,128)S(1)} %get-tuple-element.39), channel_id=1, source_target_pairs={{0,480},{16,496},{32,0},{48,16},{64,32},{80,48},{96,64},{112,80},{... | collective-permute-start | bytes 147464 | tf_op jit(solution)/shard_map/ppermute | solution.py:429
  83.4 19.8 %collective-permute-start.5 = (f32[8,384]{1,0:T(8,128)S(1)}, f32[8,384]{1,0:T(8,128)S(1)}, u32[]{:S(2)}, u32[]{:S(2)}) collective-permute-start(f32[8,384]{1,0:T(8,128)S(1)} %get-tuple-element.41), channel_id=1, source_target_pairs={{0,128},{16,144},{32,160},{48,176},{64,192},{80,208},{96,224},{112... | collective-permute-start | bytes 36872 | tf_op jit(solution)/shard_map/ppermute | solution.py:429
  85.3 17.9 %collective-permute-start.6 = (f32[8,384]{1,0:T(8,128)S(1)}, f32[8,384]{1,0:T(8,128)S(1)}, u32[]{:S(2)}, u32[]{:S(2)}) collective-permute-start(f32[8,384]{1,0:T(8,128)S(1)} %get-tuple-element.42), channel_id=1, source_target_pairs={{0,256},{16,272},{32,288},{48,304},{64,320},{80,336},{96,352},{112... | collective-permute-start | bytes 36872 | tf_op jit(solution)/shard_map/ppermute | solution.py:429
  96.6 9.6 %collective-permute-start.7 = (f32[8,384]{1,0:T(8,128)S(1)}, f32[8,384]{1,0:T(8,128)S(1)}, u32[]{:S(2)}, u32[]{:S(2)}) collective-permute-start(f32[8,384]{1,0:T(8,128)S(1)} %get-tuple-element.43), channel_id=1, source_target_pairs={{0,384},{16,400},{32,416},{48,432},{64,448},{80,464},{96,480},{112... | collective-permute-start | bytes 36872 | tf_op jit(solution)/shard_map/ppermute | solution.py:429
  101.8 0.7 copy-start
  102.5 0.7 copy-start.1
  103.2 7.3 %copy-start.5 = (bf16[48,128]{1,0:T(8,128)(2,1)}, bf16[48,128]{1,0:T(8,128)(2,1)S(1)}, u32[]{:S(2)}) copy-start(bf16[48,128]{1,0:T(8,128)(2,1)S(1)} %get-tuple-element.49.logit_ref) | copy-start | bytes 36868
Sparse Core Ops, SparseCore 0:
  28.8 76.1 all-gather.1

commit v7 on v6

--- a/solution.py
+++ b/solution.py
@@ -282,19 +282,20 @@
         out_ref[:, i * 2 * LINE : (i + 1) * 2 * LINE, :] = out.reshape(EXP, 2 * LINE, COLS)
 
 
-def key_terms(core, attn, attn2, cot, cot2):
+def key_terms(core, attn, cot, other):
+    cot2 = pl.BlockSpec((TOK, KC), lambda i: (0, D // KC))
     columns = pl.BlockSpec((TOK, 8 * CORES * DPROWS), lambda i: (0, i))
     return pl.pallas_call(
         terms_kernel,
         grid=(ZN // 8,),
         out_shape=jax.ShapeDtypeStruct((EXP, KEYS, COLS), BF),
-        in_specs=[smem(), columns, columns, full(TOK, KC), full(TOK, KC)],
+        in_specs=[smem(), columns, columns, full(TOK, KC), cot2],
         out_specs=pl.BlockSpec((EXP, 8 * LINE, COLS), lambda i: (0, i, 0)),
         scratch_shapes=[VM((len(PIECES), 2 * EXP * LINE, 2 * DPROWS), BF)],
         compiler_params=params(BIG),
         cost_estimate=cost(10**6, 2 * 10**6),
         name="key_terms",
-    )(core, attn, attn2, cot, cot2)
+    )(core, attn, other, cot, other)
 
 
 def near_kernel(place_ref, terms_ref, *refs):
@@ -362,7 +363,16 @@
     )(*given)
 
 
-def small_kernel(weight_ref, dots_ref, out_ref):
+def small_kernel(weight_ref, dots_ref, attn_ref, cot_ref, out_ref, joined_ref, sem):
+    copies = []
+    for i in range(4):
+        at = pl.ds(i * (TOK // 4), TOK // 4)
+        copies.append(
+            pltpu.make_async_copy(attn_ref.at[at], joined_ref.at[at, pl.ds(0, D)], sem.at[i])
+        )
+    copies.append(pltpu.make_async_copy(cot_ref, joined_ref.at[:, pl.ds(D, KC)], sem.at[4]))
+    for copy in copies:
+        copy.start()
     weight = weight_ref[...]
     tall = jnp.concatenate([weight[:, i * LANES : (i + 1) * LANES] for i in range(TILES)], axis=0)
     to, fr = iota((EXP * ROOM, EXP), 0), iota((EXP * ROOM, EXP), 1)
@@ -371,18 +381,24 @@
     spread = spread.reshape(EXP, ROOM, LANES)
     tall = jnp.broadcast_to(tall[None], (EXP, BLOCK, LANES))
     out_ref[...] = jnp.concatenate([tall, spread], axis=1).astype(BF)
-
-
-def small_block(weight, dots):
+    for copy in copies:
+        copy.wait()
+
+
+def small_block(weight, dots, attn, cot):
     return pl.pallas_call(
         small_kernel,
-        in_specs=[vmem()] * 2,
-        out_specs=vmem(),
-        out_shape=jax.ShapeDtypeStruct((EXP, BLOCK + ROOM, LANES), BF),
+        in_specs=[vmem()] * 2 + [pl.BlockSpec(memory_space=HB)] * 2,
+        out_specs=[vmem(), pl.BlockSpec(memory_space=HB)],
+        out_shape=(
+            jax.ShapeDtypeStruct((EXP, BLOCK + ROOM, LANES), BF),
+            jax.ShapeDtypeStruct((TOK, D + KC), BF),
+        ),
+        scratch_shapes=[pltpu.SemaphoreType.DMA((5,))],
         compiler_params=params(BIG),
         cost_estimate=cost(10**6, 10**6),
         name="small_block",
-    )(weight, dots)
+    )(weight, dots, attn, cot)
 
 
 def order_kernel(small_ref, out_ref):
@@ -448,8 +464,9 @@
     dp = lax.axis_index("dp")
     core, z = lax.rem(dp, CORES)[None], dp // CORES
     near_place, far_place = lax.rem(z, 4)[None], (z // 4)[None]
-    small = exchange(small_block(key_weight, expert_dots))
-    terms = key_terms(core, attn_input, swap_core(attn_input), key_cot, swap_core(key_cot))
+    small, joined = small_block(key_weight, expert_dots, attn_input, key_cot)
+    small = exchange(small)
+    terms = key_terms(core, attn_input, key_cot, swap_core(joined))
     small, terms = lax.optimization_barrier((small, terms))
     w = lax.all_gather(order_rows(small), "dp", axis=0, tiled=True)
     terms, own_rows = lax.optimization_barrier((terms, expert_rows))

time: 124 us -> 154 us (1.24)
  Pallas kernels: 20.5 us -> 49.3 us
  waiting for transfers between devices: 26.3 us -> 30.8 us
  starting transfers between devices: 60.1 us -> 56.3 us
    pallas_call x1, Pallas kernels: 1.52 us -> 30.3 us  [small_block(): pl.pallas_call(small_kernel, in_specs=[vmem()] * 2 + [pl.BlockSpec(memory...]
    all_to_all x3, waiting for transfers between devices: 20.3 us -> 24.4 us  [exchange(): return lax.all_to_all(x, 'expert', split_axis=0, concat_axis=0, tiled=True)]
    ppermute x2 -> x1, starting transfers between devices: 4.33 us -> 1.92 us  [swap_core(): return lax.ppermute(x, 'dp', [(i, i ^ 1) for i in range(ZN * CORES)])]
  transfers between devices with their start and end apart: 12 -> 11, of which waited for: 4 -> 5; matrix products, arithmetic and copies ran while one was open for 0% -> 0% of each run, Pallas kernels for 11% -> 8%
where the time goes in v7:
time: 154 us; the launch traced here: 153 us
  starting transfers between devices  56.3 us (37%)
  Pallas kernels  49.3 us (32%)
  waiting for transfers between devices  30.8 us (20%)
  between operations  14.2 us (9%)
  local copies, waits for them, and re-layouts  2.31 us (2%)
    ppermute x6, starting transfers between devices, shift(): return lax.ppermute(x, 'dp', pairs)  32.4 us
    pallas_call x1, Pallas kernels, small_block(): pl.pallas_call(small_kernel, in_specs=[vmem()] * 2 + [pl.BlockSpec(memory...  30.3 us
    all_to_all x3, waiting for transfers between devices, exchange(): return lax.all_to_all(x, 'expert', split_axis=0, concat_axis=0, tiled=True)  24.4 us
    all_to_all x3, starting transfers between devices, exchange(): return lax.all_to_all(x, 'expert', split_axis=0, concat_axis=0, tiled=True)  22 us
    ppermute x6, waiting for transfers between devices, shift(): return lax.ppermute(x, 'dp', pairs)  6.37 us
    pallas_call x1, Pallas kernels, combine(): pl.pallas_call(combine_kernel, grid=(PARTS // STEP,), out_shape=jax.Shape...  6.09 us
    pallas_call x1, Pallas kernels, pack(): pl.pallas_call(pack_kernel, out_shape=jax.ShapeDtypeStruct((EXP, ROWS, CO...  5.55 us
    pallas_call x1, Pallas kernels, key_terms(): pl.pallas_call(terms_kernel, grid=(ZN // 8,), out_shape=jax.ShapeDtypeStr...  4.72 us
  transfers between devices with their start and end apart: 11, of which 5 were waited for; matrix products, arithmetic and copies ran while one was open for 0% of the time, Pallas kernels for 8%

profile of v7, /device:TPU:24, one launch (start us, length us, event | category | flops | bytes accessed | tf_op | source)
XLA Modules:
  0.0 153.0 jit_solution(5938214625946024993)
XLA Ops:
  7.2 30.3 %small_block.1 = (bf16[16,32,128]{2,1,0:T(8,128)(2,1)}, bf16[128,3584]{1,0:T(8,128)(2,1)}) custom-call(f32[6,512]{1,0:T(8,128)} %weight_ref.3, bf16[16,34]{1,0:T(8,128)(2,1)} %dots_ref.1, bf16[128,3072]{1,0:T(8,128)(2,1)} %attn_ref.3, bf16[128,512]{1,0:T(8,128)(2,1)} %cot_ref.5), custom_call_target="tpu_custom_call" | custom-call | flops 10000 | bytes 10000 | tf_op jit(solution)/shard_map/small_block/pallas_call | solution.py:389
  37.5 1.9 %collective-permute-start = (bf16[128,3584]{1,0:T(8,128)(2,1)}, bf16[128,3584]{1,0:T(8,128)(2,1)S(1)}, u32[]{:S(2)}, u32[]{:S(2)}) collective-permute-start(bf16[128,3584]{1,0:T(8,128)(2,1)} %get-tuple-element.32), channel_id=1, source_target_pairs={{0,16},{16,0},{32,48},{48,32},{64,80},{80,64},{96,112},{112,96},{1... | collective-permute-start | bytes 2752520 | tf_op jit(solution)/shard_map/ppermute | solution.py:449
  39.4 9.0 %all-to-all-start = ((bf16[16,32,128]{2,1,0:T(8,128)(2,1)}), bf16[16,32,128]{2,1,0:T(8,128)(2,1)S(1)}, u32[]{:S(2)}, u32[]{:S(2)}) async-start(bf16[16,32,128]{2,1,0:T(8,128)(2,1)} %get-tuple-element.31), calls=%async_computation | async-start | bytes 262144 | tf_op jit(solution)/shard_map/all_to_all | solution.py:440
  48.4 0.0 all-gather.2.cloned.1.call-start
  48.4 0.0 collective-permute-done.attn2_ref.cot2_ref
  48.5 0.0 copy-start.8
  48.5 0.9 copy-done.8
  49.4 4.7 %key_terms.1 = bf16[16,128,384]{2,1,0:T(8,128)(2,1)} custom-call(s32[1]{0:T(128)} %bitcast.core_ref, bf16[128,3072]{1,0:T(8,128)(2,1)} %attn_ref.3, bf16[128,3584]{1,0:T(8,128)(2,1)} %copy-done.8, bf16[128,512]{1,0:T(8,128)(2,1)} %cot_ref.5, bf16[128,3584]{1,0:T(8,128)(2,1)} %copy-done.8), custom_call_target="tpu_custom_call" | custom-call | flops 10000 | bytes 20000 | tf_op jit(solution)/shard_map/key_terms/pallas_call | solution.py:288
  54.1 0.2 all-to-all-done.dots_ref.small_ref
  54.3 1.0 order_key_rows.1
  55.3 0.0 all-gather.2.cloned.1.call-update
  55.3 7.0 %all-to-all-start.1 = ((bf16[16,128,384]{2,1,0:T(8,128)(2,1)}), bf16[16,128,384]{2,1,0:T(8,128)(2,1)S(1)}, u32[]{:S(2)}, u32[]{:S(2)}) async-start(bf16[16,128,384]{2,1,0:T(8,128)(2,1)} %key_terms.1), calls=%async_computation.1 | async-start | bytes 3145728 | tf_op jit(solution)/shard_map/all_to_all | solution.py:440
  62.3 5.6 %pack_rows.1 = bf16[16,272,384]{2,1,0:T(8,128)(2,1)} custom-call(bf16[34,16,3072]{2,1,0:T(8,128)(2,1)} %bitcast.9), custom_call_target="tpu_custom_call" | custom-call | flops 16106127 | bytes 66846 | tf_op jit(solution)/shard_map/pack_rows/pallas_call | solution.py:109
  67.9 0.0 copy-start.6
  67.9 0.0 copy-start.7
  67.9 0.0 copy-start.2
  67.9 0.0 copy-start.3
  67.9 0.0 copy-start.4
  68.0 18.1 %all-to-all-done.1.terms_ref = bf16[16,128,384]{2,1,0:T(8,128)(2,1)S(1)} async-done(((bf16[16,128,384]{2,1,0:T(8,128)(2,1)}), bf16[16,128,384]{2,1,0:T(8,128)(2,1)S(1)}, u32[]{:S(2)}, u32[]{:S(2)}) %all-to-all-start.1) | async-done | bytes 1572896 | tf_op jit(solution)/shard_map/all_to_all | solution.py:440
  86.1 6.0 %all-to-all-start.2 = ((bf16[16,272,384]{2,1,0:T(8,128)(2,1)}), bf16[16,272,384]{2,1,0:T(8,128)(2,1)}, u32[]{:S(2)}, u32[]{:S(2)}) async-start(bf16[16,272,384]{2,1,0:T(8,128)(2,1)} %pack_rows.1), calls=%async_computation.2 | async-start | bytes 6684672 | tf_op jit(solution)/shard_map/all_to_all | solution.py:440
  92.0 0.3 near_terms.1
  92.3 1.9 %collective-permute-start.1 = (f32[4,8,384]{2,1,0:T(8,128)S(1)}, f32[4,8,384]{2,1,0:T(8,128)S(1)}, u32[]{:S(2)}, u32[]{:S(2)}) collective-permute-start(f32[4,8,384]{2,1,0:T(8,128)S(1)} %get-tuple-element.41), channel_id=1, source_target_pairs={{0,32},{16,48},{32,64},{48,80},{64,96},{80,112},{96,128},{112,144}... | collective-permute-start | bytes 147464 | tf_op jit(solution)/shard_map/ppermute | solution.py:445
  94.3 10.4 %collective-permute-start.2 = (f32[4,8,384]{2,1,0:T(8,128)S(1)}, f32[4,8,384]{2,1,0:T(8,128)S(1)}, u32[]{:S(2)}, u32[]{:S(2)}) collective-permute-start(f32[4,8,384]{2,1,0:T(8,128)S(1)} %get-tuple-element.42), channel_id=1, source_target_pairs={{0,448},{16,464},{32,480},{48,496},{64,0},{80,16},{96,32},{112,48}... | collective-permute-start | bytes 147464 | tf_op jit(solution)/shard_map/ppermute | solution.py:445
  104.7 2.9 %collective-permute-start.3 = (f32[4,8,384]{2,1,0:T(8,128)S(1)}, f32[4,8,384]{2,1,0:T(8,128)S(1)}, u32[]{:S(2)}, u32[]{:S(2)}) collective-permute-start(f32[4,8,384]{2,1,0:T(8,128)S(1)} %get-tuple-element.43), channel_id=1, source_target_pairs={{0,480},{16,496},{32,0},{48,16},{64,32},{80,48},{96,64},{112,80},{... | collective-permute-start | bytes 147464 | tf_op jit(solution)/shard_map/ppermute | solution.py:445
  107.6 0.0 collective-permute-done.1.up_ref
  107.6 0.0 collective-permute-done.2.across_ref
  107.6 3.0 %collective-permute-done.3.down_ref = f32[4,8,384]{2,1,0:T(8,128)S(1)} collective-permute-done((f32[4,8,384]{2,1,0:T(8,128)S(1)}, f32[4,8,384]{2,1,0:T(8,128)S(1)}, u32[]{:S(2)}, u32[]{:S(2)}) %collective-permute-start.3) | collective-permute-done | bytes 49184 | tf_op jit(solution)/shard_map/ppermute | solution.py:445
  110.7 1.9 %collective-permute-start.4 = (f32[8,384]{1,0:T(8,128)S(1)}, f32[8,384]{1,0:T(8,128)S(1)}, u32[]{:S(2)}, u32[]{:S(2)}) collective-permute-start(f32[8,384]{1,0:T(8,128)S(1)} %get-tuple-element.45), channel_id=1, source_target_pairs={{0,128},{16,144},{32,160},{48,176},{64,192},{80,208},{96,224},{112... | collective-permute-start | bytes 36872 | tf_op jit(solution)/shard_map/ppermute | solution.py:445
  112.6 11.2 %collective-permute-start.5 = (f32[8,384]{1,0:T(8,128)S(1)}, f32[8,384]{1,0:T(8,128)S(1)}, u32[]{:S(2)}, u32[]{:S(2)}) collective-permute-start(f32[8,384]{1,0:T(8,128)S(1)} %get-tuple-element.46), channel_id=1, source_target_pairs={{0,256},{16,272},{32,288},{48,304},{64,320},{80,336},{96,352},{112... | collective-permute-start | bytes 36872 | tf_op jit(solution)/shard_map/ppermute | solution.py:445
  123.8 4.1 %collective-permute-start.6 = (f32[8,384]{1,0:T(8,128)S(1)}, f32[8,384]{1,0:T(8,128)S(1)}, u32[]{:S(2)}, u32[]{:S(2)}) collective-permute-start(f32[8,384]{1,0:T(8,128)S(1)} %get-tuple-element.47), channel_id=1, source_target_pairs={{0,384},{16,400},{32,416},{48,432},{64,448},{80,464},{96,480},{112... | collective-permute-start | bytes 36872 | tf_op jit(solution)/shard_map/ppermute | solution.py:445
  127.9 0.0 copy-done.6
  127.9 0.0 copy-done.7
  127.9 0.7 gates.1
  128.6 0.0 copy-start
  128.6 0.7 copy-done
  129.3 0.0 copy-start.1
  129.3 0.7 copy-done.1
  130.0 0.0 collective-permute-done.4.up_ref
  130.0 0.0 collective-permute-done.5.across_ref
  130.0 3.3 %collective-permute-done.6.down_ref = f32[8,384]{1,0:T(8,128)S(1)} collective-permute-done((f32[8,384]{1,0:T(8,128)S(1)}, f32[8,384]{1,0:T(8,128)S(1)}, u32[]{:S(2)}, u32[]{:S(2)}) %collective-permute-start.6) | collective-permute-done | bytes 12320 | tf_op jit(solution)/shard_map/ppermute | solution.py:445
  133.3 0.0 copy-done.2
  133.3 0.0 copy-done.3
  133.3 0.0 copy-done.4
  133.3 0.6 adamw.1
  134.0 6.1 %all-to-all-done.2.head_ref.tail_ref = bf16[16,272,384]{2,1,0:T(8,128)(2,1)} async-done(((bf16[16,272,384]{2,1,0:T(8,128)(2,1)}), bf16[16,272,384]{2,1,0:T(8,128)(2,1)}, u32[]{:S(2)}, u32[]{:S(2)}) %all-to-all-start.2) | async-done | bytes 3342368 | tf_op jit(solution)/shard_map/all_to_all | solution.py:440
  140.1 0.0 all-gather.2.cloned.1.call-done.w_ref
  140.1 0.0 copy-done.5
  140.1 6.1 %combine.1 = bf16[128,3072]{1,0:T(8,128)(2,1)} custom-call(bf16[256,512]{1,0:T(8,128)(2,1)} %copy-done, bf16[256,256]{1,0:T(8,128)(2,1)} %copy-done.1, bf16[48,128]{1,0:T(8,128)(2,1)} %copy-done.5, bf16[128,512]{1,0:T(8,128)(2,1)} %cot_ref.5, bf16[16,272,384]{2,1,0:T(8,128)(2,1)} %all-to-all-done.2.head_ref.tail_ref, ...), custom_call_target="tpu_custom_call" | custom-call | flops 20000000 | bytes 80000 | tf_op jit(solution)/shard_map/combine/pallas_call | solution.py:223
  (2 shorter events, 0.0 us)
Async XLA Ops:
  37.5 11.0 %collective-permute-start = (bf16[128,3584]{1,0:T(8,128)(2,1)}, bf16[128,3584]{1,0:T(8,128)(2,1)S(1)}, u32[]{:S(2)}, u32[]{:S(2)}) collective-permute-start(bf16[128,3584]{1,0:T(8,128)(2,1)} %get-tuple-element.32), channel_id=1, source_target_pairs={{0,16},{16,0},{32,48},{48,32},{64,80},{80,64},{96,112},{112,96},{1... | collective-permute-start | bytes 2752520 | tf_op jit(solution)/shard_map/ppermute | solution.py:449
  39.4 14.9 %all-to-all-start = ((bf16[16,32,128]{2,1,0:T(8,128)(2,1)}), bf16[16,32,128]{2,1,0:T(8,128)(2,1)S(1)}, u32[]{:S(2)}, u32[]{:S(2)}) async-start(bf16[16,32,128]{2,1,0:T(8,128)(2,1)} %get-tuple-element.31), calls=%async_computation | async-start | bytes 262144 | tf_op jit(solution)/shard_map/all_to_all | solution.py:440
  48.4 91.7 %all-gather.2.cloned.1.call-start = ((), (), s32[]{:S(2)}) async-start(), calls=%async_computation.3 | async-start | bytes 3244032 | tf_op jit(solution)/shard_map/all_gather | solution.py:471
  48.5 0.9 copy-start.8
  55.3 30.8 %all-to-all-start.1 = ((bf16[16,128,384]{2,1,0:T(8,128)(2,1)}), bf16[16,128,384]{2,1,0:T(8,128)(2,1)S(1)}, u32[]{:S(2)}, u32[]{:S(2)}) async-start(bf16[16,128,384]{2,1,0:T(8,128)(2,1)} %key_terms.1), calls=%async_computation.1 | async-start | bytes 3145728 | tf_op jit(solution)/shard_map/all_to_all | solution.py:440
  67.9 60.0 %copy-start.6 = (f32[128,16]{0,1:T(8,128)S(1)}, f32[128,16]{0,1:T(8,128)}, u32[]{:S(2)}) copy-start(f32[128,16]{0,1:T(8,128)} %param.13) | copy-start | bytes 24580
  67.9 60.0 %copy-start.7 = (s32[128,4]{0,1:T(4,128)S(1)}, s32[128,4]{0,1:T(4,128)}, u32[]{:S(2)}) copy-start(s32[128,4]{0,1:T(4,128)} %param.12) | copy-start | bytes 6148
  67.9 65.4 %copy-start.2 = (f32[6,512]{1,0:T(8,128)S(1)}, f32[6,512]{1,0:T(8,128)}, u32[]{:S(2)}) copy-start(f32[6,512]{1,0:T(8,128)} %weight_ref.3) | copy-start | bytes 36868
  67.9 65.4 %copy-start.3 = (f32[6,512]{1,0:T(8,128)S(1)}, f32[6,512]{1,0:T(8,128)}, u32[]{:S(2)}) copy-start(f32[6,512]{1,0:T(8,128)} %first_ref.1) | copy-start | bytes 36868
  67.9 65.4 %copy-start.4 = (f32[6,512]{1,0:T(8,128)S(1)}, f32[6,512]{1,0:T(8,128)}, u32[]{:S(2)}) copy-start(f32[6,512]{1,0:T(8,128)} %second_ref.1) | copy-start | bytes 36868
  86.1 54.0 %all-to-all-start.2 = ((bf16[16,272,384]{2,1,0:T(8,128)(2,1)}), bf16[16,272,384]{2,1,0:T(8,128)(2,1)}, u32[]{:S(2)}, u32[]{:S(2)}) async-start(bf16[16,272,384]{2,1,0:T(8,128)(2,1)} %pack_rows.1), calls=%async_computation.2 | async-start | bytes 6684672 | tf_op jit(solution)/shard_map/all_to_all | solution.py:440
  92.3 15.3 %collective-permute-start.1 = (f32[4,8,384]{2,1,0:T(8,128)S(1)}, f32[4,8,384]{2,1,0:T(8,128)S(1)}, u32[]{:S(2)}, u32[]{:S(2)}) collective-permute-start(f32[4,8,384]{2,1,0:T(8,128)S(1)} %get-tuple-element.41), channel_id=1, source_target_pairs={{0,32},{16,48},{32,64},{48,80},{64,96},{80,112},{96,128},{112,144}... | collective-permute-start | bytes 147464 | tf_op jit(solution)/shard_map/ppermute | solution.py:445
  94.3 13.4 %collective-permute-start.2 = (f32[4,8,384]{2,1,0:T(8,128)S(1)}, f32[4,8,384]{2,1,0:T(8,128)S(1)}, u32[]{:S(2)}, u32[]{:S(2)}) collective-permute-start(f32[4,8,384]{2,1,0:T(8,128)S(1)} %get-tuple-element.42), channel_id=1, source_target_pairs={{0,448},{16,464},{32,480},{48,496},{64,0},{80,16},{96,32},{112,48}... | collective-permute-start | bytes 147464 | tf_op jit(solution)/shard_map/ppermute | solution.py:445
  104.7 6.0 %collective-permute-start.3 = (f32[4,8,384]{2,1,0:T(8,128)S(1)}, f32[4,8,384]{2,1,0:T(8,128)S(1)}, u32[]{:S(2)}, u32[]{:S(2)}) collective-permute-start(f32[4,8,384]{2,1,0:T(8,128)S(1)} %get-tuple-element.43), channel_id=1, source_target_pairs={{0,480},{16,496},{32,0},{48,16},{64,32},{80,48},{96,64},{112,80},{... | collective-permute-start | bytes 147464 | tf_op jit(solution)/shard_map/ppermute | solution.py:445
  110.7 19.3 %collective-permute-start.4 = (f32[8,384]{1,0:T(8,128)S(1)}, f32[8,384]{1,0:T(8,128)S(1)}, u32[]{:S(2)}, u32[]{:S(2)}) collective-permute-start(f32[8,384]{1,0:T(8,128)S(1)} %get-tuple-element.45), channel_id=1, source_target_pairs={{0,128},{16,144},{32,160},{48,176},{64,192},{80,208},{96,224},{112... | collective-permute-start | bytes 36872 | tf_op jit(solution)/shard_map/ppermute | solution.py:445
  112.6 17.4 %collective-permute-start.5 = (f32[8,384]{1,0:T(8,128)S(1)}, f32[8,384]{1,0:T(8,128)S(1)}, u32[]{:S(2)}, u32[]{:S(2)}) collective-permute-start(f32[8,384]{1,0:T(8,128)S(1)} %get-tuple-element.46), channel_id=1, source_target_pairs={{0,256},{16,272},{32,288},{48,304},{64,320},{80,336},{96,352},{112... | collective-permute-start | bytes 36872 | tf_op jit(solution)/shard_map/ppermute | solution.py:445
  123.8 9.5 %collective-permute-start.6 = (f32[8,384]{1,0:T(8,128)S(1)}, f32[8,384]{1,0:T(8,128)S(1)}, u32[]{:S(2)}, u32[]{:S(2)}) collective-permute-start(f32[8,384]{1,0:T(8,128)S(1)} %get-tuple-element.47), channel_id=1, source_target_pairs={{0,384},{16,400},{32,416},{48,432},{64,448},{80,464},{96,480},{112... | collective-permute-start | bytes 36872 | tf_op jit(solution)/shard_map/ppermute | solution.py:445
  128.6 0.7 copy-start
  129.3 0.7 copy-start.1
  130.0 10.1 %copy-start.5 = (bf16[48,128]{1,0:T(8,128)(2,1)}, bf16[48,128]{1,0:T(8,128)(2,1)S(1)}, u32[]{:S(2)}) copy-start(bf16[48,128]{1,0:T(8,128)(2,1)S(1)} %get-tuple-element.53.logit_ref) | copy-start | bytes 36868
Sparse Core Ops, SparseCore 0:
  55.4 76.1 all-gather.1
